TPU v7x, 512 devices: a whole 4x4x16 slice. The times are simulated.
512 devices in a mesh: wide: 64 (over z, x), narrow: 8 (over y, core).
Axes of the slice: x: 4, y: 4, z: 16, core: 2. Of those that a mesh axis runs over, the one named last changes fastest.
Arguments:
- row_embed: float32 [12288, 512], P(('wide', 'narrow')), may hold values from -10 to 10
- col_embed: float32 [12288, 512], P(('wide', 'narrow')), may hold values from -10 to 10
- logit_scale: float32 [], replicated, may hold values from 1.5 to 3
- targets: int32 [12288], P(('wide', 'narrow')), may hold values from 0 to 12287, each once
Outputs:
- row_grads: float32 [12288, 512], P(('wide', 'narrow'))
- col_grads: float32 [12288, 512], P(('wide', 'narrow'))
All inputs are finite; a program needn't handle non-finite values.
Results may differ from a plain program's by a relative error of at most 0.0005.
Values sent between devices are 32-bit elements; how exact they have to be, the bound alone decides.
No kernel may reach another device: no remote copies, remote signals or barrier semaphores. Data moves between devices by JAX's collectives and lax.ppermute only.
A program may use at most 64 MiB of HBM per device.

v0:
```python
import jax
import jax.numpy as jnp
from jax import lax
from jax.sharding import PartitionSpec as P


def similarity(left_rows, right_rows, factor):
    return factor * lax.dot_general(
        left_rows,
        right_rows,
        (((1,), (1,)), ((), ())),
        precision=lax.Precision.HIGHEST,
        preferred_element_type=jnp.float32,
    )


def local(row_embed, col_embed, logit_scale, targets):
    wide_index = lax.axis_index("wide")
    inner = lax.all_gather(col_embed, "narrow", axis=0, tiled=True)
    col_count = inner.shape[0]
    col_base = wide_index * col_count
    all_rows, all_targets = (
        lax.all_gather(row_embed, "wide", axis=0, tiled=True),
        lax.all_gather(targets, "wide", axis=0, tiled=True),
    )
    scores = similarity(all_rows, inner, logit_scale)
    row_top = jnp.max(scores, axis=1)
    row_total = jnp.sum(jnp.exp(scores - row_top[:, None]), axis=1)
    col_top = jnp.max(scores, axis=0)
    col_total = jnp.sum(jnp.exp(scores - col_top[None, :]), axis=0)
    row_peak = lax.pmax(row_top, "wide")
    row_total = lax.psum(row_total * jnp.exp(row_top - row_peak), "wide")
    row_top = row_peak
    col_peak = lax.pmax(col_top, "narrow")
    col_total = lax.psum(col_total * jnp.exp(col_top - col_peak), "narrow")
    col_top = col_peak
    row_lse = row_top + jnp.log(row_total)
    col_lse = col_top + jnp.log(col_total)
    column_ids = jnp.arange(col_count, dtype=jnp.int32)
    positive = (all_targets[:, None] - col_base == column_ids[None, :]).astype(jnp.float32)
    weights = (
        0.5 * jnp.exp(scores - row_lse[:, None])
        + 0.5 * jnp.exp(scores - col_lse[None, :])
        - positive
    )
    grad_rows = logit_scale * jnp.dot(
        weights, inner, precision=lax.Precision.HIGHEST, preferred_element_type=jnp.float32
    )
    grad_cols = logit_scale * lax.dot_general(
        weights,
        all_rows,
        (((0,), (0,)), ((), ())),
        precision=lax.Precision.HIGHEST,
        preferred_element_type=jnp.float32,
    )
    row_grads = lax.psum_scatter(grad_rows, "wide", scatter_dimension=0, tiled=True)
    col_grads = lax.psum_scatter(grad_cols, "narrow", scatter_dimension=0, tiled=True)
    return (row_grads, col_grads)


def solution(mesh):
    in_specs = (
        P(("wide", "narrow"), None),
        P(("wide", "narrow"), None),
        P(),
        P(("wide", "narrow")),
    )
    out_specs = (P(("wide", "narrow"), None), P(("wide", "narrow"), None))
    return jax.shard_map(local, mesh=mesh, in_specs=in_specs, out_specs=out_specs, check_vma=False)
```

profile of v0, /device:TPU:6, one launch (start us, length us, event | category | flops | bytes accessed | tf_op | source)
XLA Modules:
  0.0 1215.9 jit_solution(3117566147603173163)
XLA Ops:
  7.2 0.0 all-gather.2.cloned.1.call-start
  7.2 0.7 all-gather.2.cloned.1.call-update
  7.9 0.0 reduce-scatter.5.cloned.1.call-start
  8.6 1.3 dynamic-slice
  10.5 0.9 dynamic-update-slice
  11.4 32.8 %all-reduce = s32[1536]{0:T(1024)S(1)} all-reduce(s32[1536]{0:T(1024)S(1)} %dynamic-update-slice), channel_id=1, replica_groups=mesh['wide'=64,'narrow'=8] {'wide'}, use_global_device_ids=true, to_apply=%add | all-reduce | flops 1536 | bytes 12288
  44.2 13.7 %all_gather.10 = f32[192,512]{1,0:T(8,128)S(1)} all-gather(f32[24,512]{1,0:T(8,128)} %param.5), channel_id=1, replica_groups=mesh['wide'=64,'narrow'=8] {'narrow'}, dimensions={0}, use_global_device_ids=true | all-gather | bytes 442368 | tf_op jit(solution)/shard_map/all_gather | solution.py:19
  57.8 99.4 %all-gather.2.cloned.1.call-done = f32[1536,512]{1,0:T(8,128)} async-done(((f32[24,512]{1,0:T(8,128)}), f32[1536,512]{1,0:T(8,128)}) %all-gather.2.cloned.1.call-update) | async-done | bytes 3145744 | tf_op jit(solution)/shard_map/all_gather | solution.py:23
  157.2 5.4 fusion.10
  162.6 12.4 %pmax.15 = f32[192]{0:T(256)S(1)} all-reduce(f32[192]{0:T(256)S(1)} %get-tuple-element.5), channel_id=1, replica_groups=mesh['wide'=64,'narrow'=8] {'narrow'}, use_global_device_ids=true, to_apply=%region_5.0 | all-reduce | flops 192 | bytes 1536 | tf_op jit(solution)/shard_map/pmax | solution.py:34
  175.0 138.7 %pmax.14 = f32[1536]{0:T(1024)S(1)} all-reduce(f32[1536]{0:T(1024)S(1)} %get-tuple-element.4), channel_id=1, replica_groups=mesh['wide'=64,'narrow'=8] {'wide'}, use_global_device_ids=true, to_apply=%region_1.0 | all-reduce | flops 1536 | bytes 12288 | tf_op jit(solution)/shard_map/pmax | solution.py:31
  313.7 0.4 exponential_reduce_fusion.1
  314.2 142.2 %psum.14 = f32[1536]{0:T(1024)S(1)} all-reduce(f32[1536]{0:T(1024)S(1)} %exponential_multiply_fusion), channel_id=1, replica_groups=mesh['wide'=64,'narrow'=8] {'wide'}, use_global_device_ids=true, to_apply=%region_3.0 | all-reduce | flops 1536 | bytes 12288 | tf_op jit(solution)/shard_map/psum | solution.py:32
  456.4 12.4 %psum.15 = f32[192]{0:T(256)S(1)} all-reduce(f32[192]{0:T(256)S(1)} %exponential_multiply_fusion.1), channel_id=1, replica_groups=mesh['wide'=64,'narrow'=8] {'narrow'}, use_global_device_ids=true, to_apply=%region_7.0 | all-reduce | flops 192 | bytes 1536 | tf_op jit(solution)/shard_map/psum | solution.py:35
  468.8 5.3 convolution_multiply_fusion.2
  474.2 0.0 reduce-scatter.5.cloned.1.call-update
  474.2 0.0 reduce-scatter.3.cloned.1.call-start
  474.2 4.7 convolution_multiply_fusion
  479.0 0.0 reduce-scatter.3.cloned.1.call-update
  479.0 29.7 %reduce-scatter.5.cloned.1.call-done = f32[24,512]{1,0:T(8,128)} async-done(((f32[192,512]{1,0:T(8,128)}), f32[24,512]{1,0:T(8,128)}) %reduce-scatter.5.cloned.1.call-update) | async-done | bytes 49168 | tf_op jit(solution)/shard_map/reduce_scatter | solution.py:57
  508.8 700.7 %reduce-scatter.3.cloned.1.call-done = f32[24,512]{1,0:T(8,128)} async-done(((f32[1536,512]{1,0:T(8,128)}), f32[24,512]{1,0:T(8,128)}) %reduce-scatter.3.cloned.1.call-update) | async-done | bytes 49168 | tf_op jit(solution)/shard_map/reduce_scatter | solution.py:56
  (6 shorter events, 0.0 us)
Async XLA Ops:
  7.2 150.1 %all-gather.2.cloned.1.call-start = ((), (), s32[]{:S(2)}) async-start(), calls=%async_computation.2 | async-start | bytes 3194880 | tf_op jit(solution)/shard_map/all_gather | solution.py:23
  7.9 500.9 %reduce-scatter.5.cloned.1.call-start = ((), (), s32[]{:S(2)}) async-start(), calls=%async_computation.4 | async-start | bytes 442368 | tf_op jit(solution)/shard_map/reduce_scatter | solution.py:57
  474.2 735.2 %reduce-scatter.3.cloned.1.call-start = ((), (), s32[]{:S(2)}) async-start(), calls=%async_computation.3 | async-start | bytes 3194880 | tf_op jit(solution)/shard_map/reduce_scatter | solution.py:56
Sparse Core Ops, SparseCore 0:
  10.9 146.2 all-gather.1
  474.3 34.3 reduce-scatter.4
  514.4 695.0 reduce-scatter.2
where the time goes:
time: 1220 us
  waiting for transfers between devices  831 us (68%)
  blocking collectives  352 us (29%)
  matrix products  15.4 us (1%)
  between operations  15.1 us (1%)
    reduce_scatter x1, waiting for transfers between devices, local(): lax.psum_scatter(grad_rows, 'wide', scatter_dimension=0, tiled=True)  701 us
    psum x1, blocking collectives, local(): row_total = lax.psum(row_total * jnp.exp(row_top - row_peak), 'wide')  142 us
    pmax x1, blocking collectives, local(): row_peak = lax.pmax(row_top, 'wide')  139 us
    all_gather x1, waiting for transfers between devices, local(): lax.all_gather(row_embed, 'wide', axis=0, tiled=True)  99.4 us
    unnamed x1, blocking collectives  32.8 us
    reduce_scatter x1, waiting for transfers between devices, local(): lax.psum_scatter(grad_cols, 'narrow', scatter_dimension=0, tiled=True)  29.7 us
  transfers between devices with their start and end apart: 3, of which 3 were waited for; matrix products, arithmetic and copies ran while one was open for 1% of the time, Pallas kernels for 0%

commit v1 on v0

v1 whole, which is shorter than its diff:
```python
import jax
import jax.numpy as jnp
from jax import lax
from jax.sharding import Mesh, PartitionSpec as P

ALL = ("z", "x", "y", "core")
Z, XY, CORE = 16, 16, 2
SWAP = [(0, 1), (1, 0)]


def to_all(block, axes, count):
    sent = jnp.broadcast_to(block[None], (count,) + block.shape)
    return lax.all_to_all(sent, axes, 0, 0, tiled=True)


def combine(tops, totals):
    top = jnp.max(tops, axis=0)
    return top, jnp.sum(totals * jnp.exp(tops - top[None]), axis=0)


def core_pair(block, core):
    other = lax.ppermute(block, "core", SWAP)
    return jnp.where(core == 0, jnp.stack([block, other]), jnp.stack([other, block]))


def local(row_embed, col_embed, logit_scale, targets):
    own, width = row_embed.shape
    core = lax.axis_index("core")
    plane = lax.axis_index("z")
    cols = to_all(col_embed, ("x", "y"), XY).reshape(XY * own, width)
    rows = to_all(row_embed, "z", Z).reshape(Z * own, width)
    cols = core_pair(cols, core).reshape(CORE * XY * own, width)
    row_count, col_count = rows.shape[0], cols.shape[0]

    scores = logit_scale * lax.dot_general(
        rows, cols, (((1,), (1,)), ((), ())),
        precision=lax.Precision.HIGHEST, preferred_element_type=jnp.float32,
    )
    row_top = jnp.max(scores, axis=1)
    row_total = jnp.sum(jnp.exp(scores - row_top[:, None]), axis=1)
    col_top = jnp.max(scores, axis=0)
    col_total = jnp.sum(jnp.exp(scores - col_top[None, :]), axis=0)

    row_message = jnp.concatenate(
        [row_top, row_total, targets.astype(jnp.float32), jnp.zeros((1024 - 2 * row_count - own,), jnp.float32)]
    ).reshape(8, 128)
    row_stats = to_all(row_message, "z", Z).reshape(Z, 1024)
    row_top, row_total = combine(row_stats[:, :row_count], row_stats[:, row_count:2 * row_count])
    row_targets = row_stats[:, 2 * row_count:2 * row_count + own].reshape(row_count).astype(jnp.int32)

    col_message = jnp.concatenate([col_top, col_total]).reshape(12, 128)
    pair = core_pair(col_message, core).reshape(CORE, 2, col_count)
    col_message = jnp.concatenate(combine(pair[:, 0], pair[:, 1])).reshape(12, 128)
    col_stats = to_all(col_message, ("x", "y"), XY).reshape(XY, 2, col_count)
    col_top, col_total = combine(col_stats[:, 0], col_stats[:, 1])

    place = jnp.arange(col_count, dtype=jnp.int32)
    place_core, place_chip, place_own = place // (XY * own), place // own % XY, place % own
    column_ids = ((plane * XY + place_chip) * CORE + place_core) * own + place_own
    weights = (
        jnp.exp(scores - row_top[:, None]) * (0.5 / row_total)[:, None]
        + jnp.exp(scores - col_top[None, :]) * (0.5 / col_total)[None, :]
        - (row_targets[:, None] == column_ids[None, :]).astype(jnp.float32)
    )
    grad_rows = lax.dot_general(
        weights, cols, (((1,), (0,)), ((), ())),
        precision=lax.Precision.HIGH, preferred_element_type=jnp.float32,
    )
    grad_cols = lax.dot_general(
        weights, rows, (((0,), (0,)), ((), ())),
        precision=lax.Precision.HIGH, preferred_element_type=jnp.float32,
    ).reshape(CORE, XY * own, width)
    mine = lax.dynamic_index_in_dim(grad_cols, core, 0, keepdims=False)
    theirs = lax.dynamic_index_in_dim(grad_cols, 1 - core, 0, keepdims=False)
    grad_cols = mine + lax.ppermute(theirs, "core", SWAP)
    row_parts = lax.all_to_all(grad_rows.reshape(Z, own, width), "z", 0, 0, tiled=True)
    col_parts = lax.all_to_all(grad_cols.reshape(XY, own, width), ("x", "y"), 0, 0, tiled=True)
    return logit_scale * jnp.sum(row_parts, axis=0), logit_scale * jnp.sum(col_parts, axis=0)


def solution(mesh):
    grid = Mesh(mesh.devices.reshape(Z, 4, 4, CORE), ALL)
    placed = P(ALL, None)
    return jax.shard_map(
        local, mesh=grid, in_specs=(placed, placed, P(), P(ALL)), out_specs=(placed, placed), check_vma=False
    )
```

time: 1220 us -> 196 us (0.16)
  waiting for transfers between devices: 831 us -> 94.9 us
  blocking collectives: 352 us -> 19.2 us
  starting transfers between devices: 0.12 us -> 44.5 us
  other arithmetic: 0.46 us -> 14.8 us
  between operations: 15.1 us -> 1.5 us
    reduce_scatter x2 -> x0, waiting for transfers between devices: 730 us -> none  [the longest x1 701 us: local(): lax.psum_scatter(grad_rows, 'wide', scatter_dimension=0, tiled=True)]
    psum x2 -> x0, blocking collectives: 155 us -> none  [the longest x1 142 us: local(): row_total = lax.psum(row_total * jnp.exp(row_top - row_peak), 'wide')]
    pmax x2 -> x0, blocking collectives: 151 us -> none  [the longest x1 139 us: local(): row_peak = lax.pmax(row_top, 'wide')]
    all_gather x1 -> x0, waiting for transfers between devices: 99.4 us -> none  [local(): lax.all_gather(row_embed, 'wide', axis=0, tiled=True)]
    all_to_all x0 -> x5, waiting for transfers between devices: none -> 90.5 us  [the longest x3 46.1 us: to_all(): return lax.all_to_all(sent, axes, 0, 0, tiled=True)]
    all_to_all x0 -> x5, starting transfers between devices: none -> 38.8 us  [the longest x3 29.6 us: to_all(): return lax.all_to_all(sent, axes, 0, 0, tiled=True)]
    unnamed x1 -> x0, blocking collectives: 32.8 us -> none
    all_to_all x0 -> x1, blocking collectives: none -> 19.2 us  [to_all(): return lax.all_to_all(sent, axes, 0, 0, tiled=True)]
  transfers between devices with their start and end apart: 3 -> 8, of which waited for: 3 -> 8; matrix products, arithmetic and copies ran while one was open for 1% -> 7% of each run, Pallas kernels for 0% -> 0%
where the time goes in v1:
time: 196 us; the launch traced here: 194 us
  waiting for transfers between devices  94.9 us (48%)
  starting transfers between devices  44.5 us (23%)
  blocking collectives  19.2 us (10%)
  other arithmetic  14.8 us (8%)
  local copies, waits for them, and re-layouts  12.9 us (7%)
  matrix products  6.13 us (3%)
    all_to_all x3, waiting for transfers between devices, to_all(): return lax.all_to_all(sent, axes, 0, 0, tiled=True)  46.1 us
    all_to_all x1, waiting for transfers between devices, local(): lax.all_to_all(grad_rows.reshape(Z, own, width), 'z', 0, 0, tiled=True)  37.4 us
    all_to_all x3, starting transfers between devices, to_all(): return lax.all_to_all(sent, axes, 0, 0, tiled=True)  29.6 us
    all_to_all x1, blocking collectives, to_all(): return lax.all_to_all(sent, axes, 0, 0, tiled=True)  19.2 us
    all_to_all x1, waiting for transfers between devices, local(): lax.all_to_all(grad_cols.reshape(XY, own, width), ('x', 'y'), 0, 0, tiled...  7.03 us
    all_to_all x1, starting transfers between devices, local(): lax.all_to_all(grad_cols.reshape(XY, own, width), ('x', 'y'), 0, 0, tiled...  5.63 us
  transfers between devices with their start and end apart: 8, of which 8 were waited for; matrix products, arithmetic and copies ran while one was open for 7% of the time, Pallas kernels for 0%

profile of v1, /device:TPU:6, one launch (start us, length us, event | category | flops | bytes accessed | tf_op | source)
XLA Modules:
  0.0 194.0 jit_solution(2870769385621853374)
XLA Ops:
  1.5 19.2 %all_to_all.30 = f32[16,24,512]{2,1,0:T(8,128)S(1)} all-to-all(f32[16,24,512]{2,1,0:T(8,128)S(1)} %broadcast_in_dim.12), channel_id=1, replica_groups=mesh['z'=16,'x'=4,'y'=4,'core'=2] {'x','y'}, dimensions={0} | all-to-all | bytes 1572864 | tf_op jit(solution)/shard_map/all_to_all | solution.py:13
  21.7 15.2 %all-to-all-start.1 = ((f32[16,24,512]{2,1,0:T(8,128)}), f32[16,24,512]{2,1,0:T(8,128)S(1)}, u32[]{:S(2)}, u32[]{:S(2)}) async-start(f32[16,24,512]{2,1,0:T(8,128)} %broadcast_in_dim.13), calls=%async_computation.1 | async-start | bytes 1572864 | tf_op jit(solution)/shard_map/all_to_all | solution.py:13
  36.9 1.9 collective-permute-start
  42.0 1.6 maximum_select_fusion
  43.7 30.7 %all-to-all-done.1 = f32[16,24,512]{2,1,0:T(8,128)S(1)} async-done(((f32[16,24,512]{2,1,0:T(8,128)}), f32[16,24,512]{2,1,0:T(8,128)S(1)}, u32[]{:S(2)}, u32[]{:S(2)}) %all-to-all-start.1) | async-done | bytes 786464 | tf_op jit(solution)/shard_map/all_to_all | solution.py:13
  74.4 2.7 %fusion.23 = (f32[768]{0:T(1024)S(1)}, f32[384]{0:T(512)S(1)}, f32[768,384]{1,0:T(8,128)S(1)}) fusion(f32[768,512]{1,0:T(8,128)S(1)} %bitcast.58, f32[384,512]{1,0:T(8,128)S(1)} %bitcast.60, f32[]{:T(128)S(6)} %copy.30), kind=kOutput, calls=%fused_computation.60 | convolution fusion | flops 1812822912 | bytes 3543556 | tf_op jit(solution)/shard_map/dot_general | solution.py:35
  78.6 1.9 collective-permute-start.1
  84.3 6.3 %all-to-all-start.3 = ((f32[16,12,128]{2,1,0:T(8,128)}), f32[16,12,128]{2,1,0:T(8,128)}, u32[]{:S(2)}, u32[]{:S(2)}) async-start(f32[16,12,128]{2,1,0:T(8,128)} %broadcast_in_dim.17), calls=%async_computation.3 | async-start | bytes 262144 | tf_op jit(solution)/shard_map/all_to_all | solution.py:13
  91.3 5.2 %all-to-all-done.3 = f32[16,12,128]{2,1,0:T(8,128)} async-done(((f32[16,12,128]{2,1,0:T(8,128)}), f32[16,12,128]{2,1,0:T(8,128)}, u32[]{:S(2)}, u32[]{:S(2)}) %all-to-all-start.3) | async-done | bytes 98336 | tf_op jit(solution)/shard_map/all_to_all | solution.py:13
  97.1 8.1 %all-to-all-start.2 = ((f32[16,8,128]{2,1,0:T(8,128)}), f32[16,8,128]{2,1,0:T(8,128)}, u32[]{:S(2)}, u32[]{:S(2)}) async-start(f32[16,8,128]{2,1,0:T(8,128)} %broadcast_in_dim.16), calls=%async_computation.2 | async-start | bytes 131072 | tf_op jit(solution)/shard_map/all_to_all | solution.py:13
  105.2 1.6 reshape.121
  107.9 10.2 %all-to-all-done.2 = f32[16,8,128]{2,1,0:T(8,128)} async-done(((f32[16,8,128]{2,1,0:T(8,128)}), f32[16,8,128]{2,1,0:T(8,128)}, u32[]{:S(2)}, u32[]{:S(2)}) %all-to-all-start.2) | async-done | bytes 65568 | tf_op jit(solution)/shard_map/all_to_all | solution.py:13
  119.6 1.4 convert_element_type.21
  123.0 1.4 fusion.25
  126.5 1.9 collective-permute-start.2
  128.4 2.5 %collective-permute-done.2 = f32[384,512]{1,0:T(8,128)S(1)} collective-permute-done((f32[384,512]{1,0:T(8,128)}, f32[384,512]{1,0:T(8,128)S(1)}, u32[]{:S(2)}, u32[]{:S(2)}) %collective-permute-start.2) | collective-permute-done | bytes 786464 | tf_op jit(solution)/shard_map/ppermute | solution.py:75
  130.9 2.2 %bitcast_add_fusion = f32[384,512]{1,0:T(8,128)} fusion(f32[384,512]{1,0:T(8,128)S(1)} %collective-permute-done.2, f32[2,384,512]{2,1,0:T(8,128)} %copy-done, s32[]{:T(128)S(6)} %select_n.82), kind=kLoop, calls=%fused_computation.7 | loop fusion | flops 196608 | bytes 2359300 | tf_op jit(solution)/shard_map/add | solution.py:75
  133.1 5.6 %all-to-all-start.5 = ((f32[16,24,512]{2,1,0:T(8,128)}), f32[16,24,512]{2,1,0:T(8,128)S(1)}, u32[]{:S(2)}, u32[]{:S(2)}) async-start(f32[16,24,512]{2,1,0:T(8,128)} %bitcast.20), calls=%async_computation.5 | async-start | bytes 1572864 | tf_op jit(solution)/shard_map/all_to_all | solution.py:77
  138.7 2.2 %bitcast_subtract_fusion = f32[384,768]{0,1:T(8,128)} fusion(f32[768,384]{1,0:T(8,128)S(1)} %get-tuple-element.9, s32[384]{0:T(512)} %convert_element_type.21, f32[768]{0:T(1024)S(1)} %broadcast_divide_fusion, f32[768]{0:T(1024)S(1)} %get-tuple-element.6, f32[384]{0:T(512)} %copy-done.5, f32[384]{0:T(512)S(1)} %slice_reduce_fusion, s32[768]{0:T(1024)S(1)} %fusion.16), kind=kLoop, calls=%fused_computation.2 | loop fusion | flops 2359296 | bytes 2373120 | tf_op jit(solution)/shard_map/sub | solution.py:61
  140.9 1.6 copy.13
  142.5 2.0 %fusion.24 = f32[16,24,512]{2,1,0:T(8,128)} fusion(f32[16,24,768]{2,1,0:T(8,128)S(1)} %bitcast.62, f32[768,512,1]{1,0,2:T(8,128)S(1)} %bitcast.59), kind=kOutput, calls=%fused_computation.61 | convolution fusion | flops 905969664 | bytes 3538944 | tf_op jit(solution)/shard_map/dot_general | solution.py:65
  144.6 7.0 %all-to-all-done.5 = f32[16,24,512]{2,1,0:T(8,128)S(1)} async-done(((f32[16,24,512]{2,1,0:T(8,128)}), f32[16,24,512]{2,1,0:T(8,128)S(1)}, u32[]{:S(2)}, u32[]{:S(2)}) %all-to-all-start.5) | async-done | bytes 786464 | tf_op jit(solution)/shard_map/all_to_all | solution.py:77
  151.6 3.6 %all-to-all-start.4 = ((f32[16,24,512]{2,1,0:T(8,128)}), f32[16,24,512]{2,1,0:T(8,128)S(1)}, u32[]{:S(2)}, u32[]{:S(2)}) async-start(f32[16,24,512]{2,1,0:T(8,128)} %fusion.24), calls=%async_computation.4 | async-start | bytes 1572864 | tf_op jit(solution)/shard_map/all_to_all | solution.py:76
  155.9 37.4 %all-to-all-done.4 = f32[16,24,512]{2,1,0:T(8,128)S(1)} async-done(((f32[16,24,512]{2,1,0:T(8,128)}), f32[16,24,512]{2,1,0:T(8,128)S(1)}, u32[]{:S(2)}, u32[]{:S(2)}) %all-to-all-start.4) | async-done | bytes 786464 | tf_op jit(solution)/shard_map/all_to_all | solution.py:76
  (47 shorter events, 19.0 us)
Async XLA Ops:
  0.6 20.1 %copy-start.3 = (f32[24,512]{1,0:T(8,128)S(1)}, f32[24,512]{1,0:T(8,128)}, u32[]{:S(2)}) copy-start(f32[24,512]{1,0:T(8,128)} %param.4) | copy-start | bytes 147460
  20.8 18.8 %copy-start.6 = (s32[24]{0:T(128)S(1)}, s32[24]{0:T(128)}, u32[]{:S(2)}) copy-start(s32[24]{0:T(128)} %param.7) | copy-start | bytes 292
  21.7 52.6 %all-to-all-start.1 = ((f32[16,24,512]{2,1,0:T(8,128)}), f32[16,24,512]{2,1,0:T(8,128)S(1)}, u32[]{:S(2)}, u32[]{:S(2)}) async-start(f32[16,24,512]{2,1,0:T(8,128)} %broadcast_in_dim.13), calls=%async_computation.1 | async-start | bytes 1572864 | tf_op jit(solution)/shard_map/all_to_all | solution.py:13
  36.9 4.2 %collective-permute-start = (f32[384,512]{1,0:T(8,128)S(1)}, f32[384,512]{1,0:T(8,128)S(1)}, u32[]{:S(2)}, u32[]{:S(2)}) collective-permute-start(f32[384,512]{1,0:T(8,128)S(1)} %bitcast.64), channel_id=1, source_target_pairs={{0,1},{1,0},{2,3},{3,2},{4,5},{5,4},{6,7},{7,6},{8,9},{9,8},{10,11... | collective-permute-start | bytes 2359304 | tf_op jit(solution)/shard_map/ppermute | solution.py:22
  41.1 0.9 copy-start.1
  77.1 1.6 copy-start.4
  78.6 3.4 %collective-permute-start.1 = (f32[12,128]{1,0:T(8,128)}, f32[12,128]{1,0:T(8,128)}, u32[]{:S(2)}, u32[]{:S(2)}) collective-permute-start(f32[12,128]{1,0:T(8,128)} %pad_maximum_fusion.1), channel_id=1, source_target_pairs={{0,1},{1,0},{2,3},{3,2},{4,5},{5,4},{6,7},{7,6},{8,9},{9,8},{10,11... | collective-permute-start | bytes 18440 | tf_op jit(solution)/shard_map/ppermute | solution.py:22
  84.3 12.2 %all-to-all-start.3 = ((f32[16,12,128]{2,1,0:T(8,128)}), f32[16,12,128]{2,1,0:T(8,128)}, u32[]{:S(2)}, u32[]{:S(2)}) async-start(f32[16,12,128]{2,1,0:T(8,128)} %broadcast_in_dim.17), calls=%async_computation.3 | async-start | bytes 262144 | tf_op jit(solution)/shard_map/all_to_all | solution.py:13
  97.1 21.0 %all-to-all-start.2 = ((f32[16,8,128]{2,1,0:T(8,128)}), f32[16,8,128]{2,1,0:T(8,128)}, u32[]{:S(2)}, u32[]{:S(2)}) async-start(f32[16,8,128]{2,1,0:T(8,128)} %broadcast_in_dim.16), calls=%async_computation.2 | async-start | bytes 131072 | tf_op jit(solution)/shard_map/all_to_all | solution.py:13
  119.0 0.6 copy-start.2
  121.8 1.2 copy-start.5
  124.4 1.2 copy-start
  126.5 4.4 %collective-permute-start.2 = (f32[384,512]{1,0:T(8,128)}, f32[384,512]{1,0:T(8,128)S(1)}, u32[]{:S(2)}, u32[]{:S(2)}) collective-permute-start(f32[384,512]{1,0:T(8,128)} %dynamic-slice_bitcast_fusion), channel_id=1, source_target_pairs={{0,1},{1,0},{2,3},{3,2},{4,5},{5,4},{6,7},{7,6},{8,9},{9,8},{10,11... | collective-permute-start | bytes 2359304 | tf_op jit(solution)/shard_map/ppermute | solution.py:75
  133.1 18.5 %all-to-all-start.5 = ((f32[16,24,512]{2,1,0:T(8,128)}), f32[16,24,512]{2,1,0:T(8,128)S(1)}, u32[]{:S(2)}, u32[]{:S(2)}) async-start(f32[16,24,512]{2,1,0:T(8,128)} %bitcast.20), calls=%async_computation.5 | async-start | bytes 1572864 | tf_op jit(solution)/shard_map/all_to_all | solution.py:77
  151.6 41.7 %all-to-all-start.4 = ((f32[16,24,512]{2,1,0:T(8,128)}), f32[16,24,512]{2,1,0:T(8,128)S(1)}, u32[]{:S(2)}, u32[]{:S(2)}) async-start(f32[16,24,512]{2,1,0:T(8,128)} %fusion.24), calls=%async_computation.4 | async-start | bytes 1572864 | tf_op jit(solution)/shard_map/all_to_all | solution.py:76

commit v2 on v1

v2 whole, which is shorter than its diff:
```python
import jax
import jax.numpy as jnp
from jax import lax
from jax.sharding import Mesh, PartitionSpec as P

ALL = ("z", "x", "y", "core")
Z, SIDE, CORE = 16, 4, 2


def shift(block, axis, count, by):
    return lax.ppermute(block, axis, [(i, (i + by) % count) for i in range(count)])


def around(block, axis, count):
    return jnp.stack([block] + [shift(block, axis, count, by) for by in range(1, count)])


def home(parts, axis, count):
    total = parts[0]
    for by in range(1, count):
        total = total + shift(parts[by], axis, count, -by)
    return total


def combine(tops, totals):
    top = jnp.max(tops, axis=0)
    return top, jnp.sum(totals * jnp.exp(tops - top[None]), axis=0)


def local(row_embed, col_embed, logit_scale, targets):
    own, width = row_embed.shape
    plane, across, along, core = (lax.axis_index(a) for a in ALL)
    rows = lax.all_to_all(
        jnp.broadcast_to(row_embed[None], (Z, own, width)), "z", 0, 0, tiled=True
    ).reshape(Z * own, width)
    cols = around(col_embed, "x", SIDE)
    cols = around(cols, "y", SIDE)
    cols = around(cols, "core", CORE).reshape(CORE * SIDE * SIDE * own, width)
    row_count, col_count = rows.shape[0], cols.shape[0]

    scores = logit_scale * lax.dot_general(
        rows, cols, (((1,), (1,)), ((), ())),
        precision=lax.Precision.HIGHEST, preferred_element_type=jnp.float32,
    )
    row_top = jnp.max(scores, axis=1)
    row_total = jnp.sum(jnp.exp(scores - row_top[:, None]), axis=1)
    col_top = jnp.max(scores, axis=0)
    col_total = jnp.sum(jnp.exp(scores - col_top[None, :]), axis=0)

    row_message = jnp.concatenate(
        [row_top, row_total, targets.astype(jnp.float32), jnp.zeros((1024 - 2 * row_count - own,), jnp.float32)]
    ).reshape(8, 128)
    row_stats = lax.all_to_all(
        jnp.broadcast_to(row_message[None], (Z, 8, 128)), "z", 0, 0, tiled=True
    ).reshape(Z, 1024)

    stats = jnp.stack([col_top, col_total]).reshape(2, CORE, SIDE, SIDE, own)
    for place, axis, count in ((1, "core", CORE), (3, "x", SIDE), (2, "y", SIDE)):
        messages = [stats] + [
            jnp.roll(shift(stats, axis, count, by), by, axis=place) for by in range(1, count)
        ]
        messages = jnp.stack(messages)
        stats = jnp.stack(combine(messages[:, 0], messages[:, 1]))
    stats = stats.reshape(2, col_count)
    col_top, col_total = stats[0], stats[1]

    row_top, row_total = combine(row_stats[:, :row_count], row_stats[:, row_count:2 * row_count])
    row_targets = row_stats[:, 2 * row_count:2 * row_count + own].reshape(row_count).astype(jnp.int32)

    place = jnp.arange(col_count, dtype=jnp.int32)
    place_own, place = place % own, place // own
    place_x, place = (across - place % SIDE + SIDE) % SIDE, place // SIDE
    place_y, place = (along - place % SIDE + SIDE) % SIDE, place // SIDE
    place_core = (core - place + CORE) % CORE
    column_ids = (((plane * SIDE + place_x) * SIDE + place_y) * CORE + place_core) * own + place_own
    weights = (
        jnp.exp(scores - row_top[:, None]) * (0.5 / row_total)[:, None]
        + jnp.exp(scores - col_top[None, :]) * (0.5 / col_total)[None, :]
        - (row_targets[:, None] == column_ids[None, :]).astype(jnp.float32)
    )
    grad_rows = lax.dot_general(
        weights, cols, (((1,), (0,)), ((), ())),
        precision=lax.Precision.HIGH, preferred_element_type=jnp.float32,
    )
    row_parts = lax.all_to_all(grad_rows.reshape(Z, own, width), "z", 0, 0, tiled=True)
    grad_cols = lax.dot_general(
        weights, rows, (((0,), (0,)), ((), ())),
        precision=lax.Precision.HIGH, preferred_element_type=jnp.float32,
    ).reshape(CORE, SIDE, SIDE, own, width)
    col_sum = home(home(home(grad_cols, "core", CORE), "y", SIDE), "x", SIDE)
    return logit_scale * jnp.sum(row_parts, axis=0), logit_scale * col_sum


def solution(mesh):
    grid = Mesh(mesh.devices.reshape(Z, SIDE, SIDE, CORE), ALL)
    placed = P(ALL, None)
    return jax.shard_map(
        local, mesh=grid, in_specs=(placed, placed, P(), P(ALL)), out_specs=(placed, placed), check_vma=False
    )
```

time: 196 us -> 169 us (0.86)
  starting transfers between devices: 44.5 us -> 98.9 us
  waiting for transfers between devices: 94.9 us -> 40.6 us
  blocking collectives: 19.2 us -> 0 us
  local copies, waits for them, and re-layouts: 12.9 us -> 8.57 us
  other arithmetic: 14.8 us -> 11 us
    ppermute x3 -> x21, starting transfers between devices: 5.74 us -> 67.6 us  [shift(): lax.ppermute(block, axis, [(i, (i + by) % count) for i in range(count)])]
    all_to_all x4 -> x2, waiting for transfers between devices: 53.1 us -> 8.06 us  [the longest x1 4.76 us: local(): lax.all_to_all(jnp.broadcast_to(row_embed[None], (Z, own, width)), 'z', 0...]
    all_to_all x1, waiting for transfers between devices: 37.4 us -> 0.01 us  [local(): lax.all_to_all(grad_rows.reshape(Z, own, width), 'z', 0, 0, tiled=True)]
    ppermute x3 -> x21, waiting for transfers between devices: 4.35 us -> 32.5 us  [shift(): lax.ppermute(block, axis, [(i, (i + by) % count) for i in range(count)])]
    all_to_all x1 -> x0, blocking collectives: 19.2 us -> none  [to_all(): return lax.all_to_all(sent, axes, 0, 0, tiled=True)]
    all_to_all x4 -> x2, starting transfers between devices: 35.2 us -> 22.5 us  [the longest x1 15.2 us: local(): lax.all_to_all(jnp.broadcast_to(row_embed[None], (Z, own, width)), 'z', 0...]
    all_to_all x1, starting transfers between devices: 3.61 us -> 8.77 us  [local(): lax.all_to_all(grad_rows.reshape(Z, own, width), 'z', 0, 0, tiled=True)]
    another operation x0 -> x16, other arithmetic: none -> 3.81 us  [the longest x3 1.51 us: around(): jnp.stack([block] + [shift(block, axis, count, by) for by in range(1, cou...]
  transfers between devices with their start and end apart: 8 -> 24, of which waited for: 8 -> 13; matrix products, arithmetic and copies ran while one was open for 7% -> 5% of each run, Pallas kernels for 0% -> 0%
where the time goes in v2:
time: 169 us; the launch traced here: 167 us
  starting transfers between devices  98.9 us (59%)
  waiting for transfers between devices  40.6 us (24%)
  other arithmetic  11 us (7%)
  local copies, waits for them, and re-layouts  8.57 us (5%)
  matrix products  6.28 us (4%)
  between operations  1.86 us (1%)
    ppermute x21, starting transfers between devices, shift(): lax.ppermute(block, axis, [(i, (i + by) % count) for i in range(count)])  67.6 us
    ppermute x21, waiting for transfers between devices, shift(): lax.ppermute(block, axis, [(i, (i + by) % count) for i in range(count)])  32.5 us
    all_to_all x1, starting transfers between devices, local(): lax.all_to_all(jnp.broadcast_to(row_embed[None], (Z, own, width)), 'z', 0...  15.2 us
    all_to_all x1, starting transfers between devices, local(): lax.all_to_all(grad_rows.reshape(Z, own, width), 'z', 0, 0, tiled=True)  8.77 us
    all_to_all x1, starting transfers between devices, local(): lax.all_to_all(jnp.broadcast_to(row_message[None], (Z, 8, 128)), 'z', 0,...  7.31 us
    all_to_all x1, waiting for transfers between devices, local(): lax.all_to_all(jnp.broadcast_to(row_embed[None], (Z, own, width)), 'z', 0...  4.76 us
    another operation x4, local copies, waits for them, and re-layouts, local(): stats = jnp.stack([col_top, col_total]).reshape(2, CORE, SIDE, SIDE, own)  4.29 us
  transfers between devices with their start and end apart: 24, of which 13 were waited for; matrix products, arithmetic and copies ran while one was open for 5% of the time, Pallas kernels for 0%

profile of v2, /device:TPU:6, one launch (start us, length us, event | category | flops | bytes accessed | tf_op | source)
XLA Modules:
  0.0 167.2 jit_solution(722754984140782168)
XLA Ops:
  2.4 15.2 %all-to-all-start = ((f32[16,24,512]{2,1,0:T(8,128)}), f32[16,24,512]{2,1,0:T(8,128)S(1)}, u32[]{:S(2)}, u32[]{:S(2)}) async-start(f32[16,24,512]{2,1,0:T(8,128)} %broadcast_in_dim.8), calls=%async_computation | async-start | bytes 1572864 | tf_op jit(solution)/shard_map/all_to_all | solution.py:33
  17.6 2.4 %collective-permute-start = (f32[24,512]{1,0:T(8,128)S(1)}, f32[24,512]{1,0:T(8,128)S(1)}, u32[]{:S(2)}, u32[]{:S(2)}) collective-permute-start(f32[24,512]{1,0:T(8,128)S(1)} %copy-done.1), channel_id=1, source_target_pairs={{0,8},{8,16},{16,24},{24,0},{1,9},{9,17},{17,25},{25,1},{2,10},{10... | collective-permute-start | bytes 147464 | tf_op jit(solution)/shard_map/ppermute | solution.py:11
  20.0 3.5 %collective-permute-start.2 = (f32[24,512]{1,0:T(8,128)S(1)}, f32[24,512]{1,0:T(8,128)S(1)}, u32[]{:S(2)}, u32[]{:S(2)}) collective-permute-start(f32[24,512]{1,0:T(8,128)S(1)} %copy-done.1), channel_id=1, source_target_pairs={{0,24},{8,0},{16,8},{24,16},{1,25},{9,1},{17,9},{25,17},{2,26},{10... | collective-permute-start | bytes 147464 | tf_op jit(solution)/shard_map/ppermute | solution.py:11
  23.5 3.3 %collective-permute-start.1 = (f32[24,512]{1,0:T(8,128)S(1)}, f32[24,512]{1,0:T(8,128)S(1)}, u32[]{:S(2)}, u32[]{:S(2)}) collective-permute-start(f32[24,512]{1,0:T(8,128)S(1)} %copy-done.1), channel_id=1, source_target_pairs={{0,16},{8,24},{16,0},{24,8},{1,17},{9,25},{17,1},{25,9},{2,18},{10... | collective-permute-start | bytes 147464 | tf_op jit(solution)/shard_map/ppermute | solution.py:11
  27.2 3.8 %collective-permute-done.1 = f32[24,512]{1,0:T(8,128)S(1)} collective-permute-done((f32[24,512]{1,0:T(8,128)S(1)}, f32[24,512]{1,0:T(8,128)S(1)}, u32[]{:S(2)}, u32[]{:S(2)}) %collective-permute-start.1) | collective-permute-done | bytes 49184 | tf_op jit(solution)/shard_map/ppermute | solution.py:11
  31.0 5.1 %collective-permute-start.4 = (f32[4,24,512]{2,1,0:T(8,128)S(1)}, f32[4,24,512]{2,1,0:T(8,128)S(1)}, u32[]{:S(2)}, u32[]{:S(2)}) collective-permute-start(f32[4,24,512]{2,1,0:T(8,128)S(1)} %get-tuple-element.17), channel_id=1, source_target_pairs={{0,4},{2,6},{4,0},{6,2},{1,5},{3,7},{5,1},{7,3},{8,12},{10,14},{12... | collective-permute-start | bytes 589832 | tf_op jit(solution)/shard_map/ppermute | solution.py:11
  36.1 2.6 %collective-permute-start.3 = (f32[4,24,512]{2,1,0:T(8,128)S(1)}, f32[4,24,512]{2,1,0:T(8,128)S(1)}, u32[]{:S(2)}, u32[]{:S(2)}) collective-permute-start(f32[4,24,512]{2,1,0:T(8,128)S(1)} %get-tuple-element.17), channel_id=1, source_target_pairs={{0,2},{2,4},{4,6},{6,0},{1,3},{3,5},{5,7},{7,1},{8,10},{10,12},{12... | collective-permute-start | bytes 589832 | tf_op jit(solution)/shard_map/ppermute | solution.py:11
  38.7 4.5 %collective-permute-start.5 = (f32[4,24,512]{2,1,0:T(8,128)S(1)}, f32[4,24,512]{2,1,0:T(8,128)S(1)}, u32[]{:S(2)}, u32[]{:S(2)}) collective-permute-start(f32[4,24,512]{2,1,0:T(8,128)S(1)} %get-tuple-element.17), channel_id=1, source_target_pairs={{0,6},{2,0},{4,2},{6,4},{1,7},{3,1},{5,3},{7,5},{8,14},{10,8},{12,... | collective-permute-start | bytes 589832 | tf_op jit(solution)/shard_map/ppermute | solution.py:11
  52.2 4.8 %all-to-all-done = f32[16,24,512]{2,1,0:T(8,128)S(1)} async-done(((f32[16,24,512]{2,1,0:T(8,128)}), f32[16,24,512]{2,1,0:T(8,128)S(1)}, u32[]{:S(2)}, u32[]{:S(2)}) %all-to-all-start) | async-done | bytes 786464 | tf_op jit(solution)/shard_map/all_to_all | solution.py:33
  57.0 2.8 %fusion.48 = (f32[384]{0:T(512)}, f32[768]{0:T(1024)}, f32[768,384]{0,1:T(8,128)S(1)}) fusion(f32[768,512]{1,0:T(8,128)S(1)} %bitcast.128, f32[384,512]{1,0:T(8,128)S(1)} %bitcast.131, f32[]{:T(128)S(6)} %copy.16), kind=kOutput, calls=%fused_computation.118 | convolution fusion | flops 1812822912 | bytes 3543556 | tf_op jit(solution)/shard_map/dot_general | solution.py:41
  70.6 3.3 %collective-permute-start.9 = (f32[2,2,4,4,24]{4,3,2,1,0:T(4,128)S(1)}, f32[2,2,4,4,24]{4,3,2,1,0:T(4,128)S(1)}, u32[]{:S(2)}, u32[]{:S(2)}) collective-permute-start(f32[2,2,4,4,24]{4,3,2,1,0:T(4,128)S(1)} %get-tuple-element.23), channel_id=1, source_target_pairs={{0,16},{8,24},{16,0},{24,8},{1,17},{9,25},{17,1},{25,9},{2,18},{10... | collective-permute-start | bytes 18440 | tf_op jit(solution)/shard_map/ppermute | solution.py:11
  74.6 4.0 %collective-permute-start.8 = (f32[2,2,4,4,24]{4,3,2,1,0:T(4,128)S(1)}, f32[2,2,4,4,24]{4,3,2,1,0:T(4,128)S(1)}, u32[]{:S(2)}, u32[]{:S(2)}) collective-permute-start(f32[2,2,4,4,24]{4,3,2,1,0:T(4,128)S(1)} %get-tuple-element.23), channel_id=1, source_target_pairs={{0,8},{8,16},{16,24},{24,0},{1,9},{9,17},{17,25},{25,1},{2,10},{10... | collective-permute-start | bytes 18440 | tf_op jit(solution)/shard_map/ppermute | solution.py:11
  80.7 5.0 %collective-permute-done.10 = f32[2,2,4,4,24]{4,3,2,1,0:T(4,128)S(1)} collective-permute-done((f32[2,2,4,4,24]{4,3,2,1,0:T(4,128)S(1)}, f32[2,2,4,4,24]{4,3,2,1,0:T(4,128)S(1)}, u32[]{:S(2)}, u32[]{:S(2)}) %collective-permute-start.10) | collective-permute-done | bytes 6176 | tf_op jit(solution)/shard_map/ppermute | solution.py:11
  85.9 5.1 %collective-permute-start.12 = (f32[2,2,4,4,24]{4,3,2,1,0:T(4,128)S(1)}, f32[2,2,4,4,24]{4,3,2,1,0:T(4,128)S(1)}, u32[]{:S(2)}, u32[]{:S(2)}) collective-permute-start(f32[2,2,4,4,24]{4,3,2,1,0:T(4,128)S(1)} %get-tuple-element.19), channel_id=1, source_target_pairs={{0,4},{2,6},{4,0},{6,2},{1,5},{3,7},{5,1},{7,3},{8,12},{10,14},{12... | collective-permute-start | bytes 18440 | tf_op jit(solution)/shard_map/ppermute | solution.py:11
  91.7 7.3 %all-to-all-start.1 = ((f32[16,8,128]{2,1,0:T(8,128)}), f32[16,8,128]{2,1,0:T(8,128)S(1)}, u32[]{:S(2)}, u32[]{:S(2)}) async-start(f32[16,8,128]{2,1,0:T(8,128)} %broadcast_in_dim.11), calls=%async_computation.1 | async-start | bytes 131072 | tf_op jit(solution)/shard_map/all_to_all | solution.py:53
  99.0 3.4 %collective-permute-start.11 = (f32[2,2,4,4,24]{4,3,2,1,0:T(4,128)S(1)}, f32[2,2,4,4,24]{4,3,2,1,0:T(4,128)S(1)}, u32[]{:S(2)}, u32[]{:S(2)}) collective-permute-start(f32[2,2,4,4,24]{4,3,2,1,0:T(4,128)S(1)} %get-tuple-element.19), channel_id=1, source_target_pairs={{0,2},{2,4},{4,6},{6,0},{1,3},{3,5},{5,7},{7,1},{8,10},{10,12},{12... | collective-permute-start | bytes 18440 | tf_op jit(solution)/shard_map/ppermute | solution.py:11
  102.4 3.7 %collective-permute-start.13 = (f32[2,2,4,4,24]{4,3,2,1,0:T(4,128)S(1)}, f32[2,2,4,4,24]{4,3,2,1,0:T(4,128)S(1)}, u32[]{:S(2)}, u32[]{:S(2)}) collective-permute-start(f32[2,2,4,4,24]{4,3,2,1,0:T(4,128)S(1)} %get-tuple-element.19), channel_id=1, source_target_pairs={{0,6},{2,0},{4,2},{6,4},{1,7},{3,1},{5,3},{7,5},{8,14},{10,8},{12,... | collective-permute-start | bytes 18440 | tf_op jit(solution)/shard_map/ppermute | solution.py:11
  108.6 3.3 %all-to-all-done.1 = f32[16,8,128]{2,1,0:T(8,128)S(1)} async-done(((f32[16,8,128]{2,1,0:T(8,128)}), f32[16,8,128]{2,1,0:T(8,128)S(1)}, u32[]{:S(2)}, u32[]{:S(2)}) %all-to-all-start.1) | async-done | bytes 65568 | tf_op jit(solution)/shard_map/all_to_all | solution.py:53
  116.5 8.8 %all-to-all-start.2 = ((f32[16,24,512]{2,1,0:T(8,128)}), f32[16,24,512]{2,1,0:T(8,128)}, u32[]{:S(2)}, u32[]{:S(2)}) async-start(f32[16,24,512]{2,1,0:T(8,128)} %fusion.53), calls=%async_computation.2 | async-start | bytes 1572864 | tf_op jit(solution)/shard_map/all_to_all | solution.py:85
  131.2 4.9 %collective-permute-start.15 = (f32[4,24,512]{2,1,0:T(8,128)S(1)}, f32[4,24,512]{2,1,0:T(8,128)S(1)}, u32[]{:S(2)}, u32[]{:S(2)}) collective-permute-start(f32[4,24,512]{2,1,0:T(8,128)S(1)} %get-tuple-element.8), channel_id=1, source_target_pairs={{0,6},{2,0},{4,2},{6,4},{1,7},{3,1},{5,3},{7,5},{8,14},{10,8},{12,... | collective-permute-start | bytes 589832 | tf_op jit(solution)/shard_map/ppermute | solution.py:11
  138.0 3.4 %collective-permute-start.16 = (f32[4,24,512]{2,1,0:T(8,128)S(1)}, f32[4,24,512]{2,1,0:T(8,128)S(1)}, u32[]{:S(2)}, u32[]{:S(2)}) collective-permute-start(f32[4,24,512]{2,1,0:T(8,128)S(1)} %get-tuple-element.10), channel_id=1, source_target_pairs={{0,4},{2,6},{4,0},{6,2},{1,5},{3,7},{5,1},{7,3},{8,12},{10,14},{12... | collective-permute-start | bytes 589832 | tf_op jit(solution)/shard_map/ppermute | solution.py:11
  141.4 8.7 %collective-permute-done.17 = f32[4,24,512]{2,1,0:T(8,128)S(1)} collective-permute-done((f32[4,24,512]{2,1,0:T(8,128)S(1)}, f32[4,24,512]{2,1,0:T(8,128)S(1)}, u32[]{:S(2)}, u32[]{:S(2)}) %collective-permute-start.17) | collective-permute-done | bytes 196640 | tf_op jit(solution)/shard_map/ppermute | solution.py:11
  152.1 5.1 %collective-permute-start.20 = (f32[24,512]{1,0:T(8,128)S(1)}, f32[24,512]{1,0:T(8,128)S(1)}, u32[]{:S(2)}, u32[]{:S(2)}) collective-permute-start(f32[24,512]{1,0:T(8,128)S(1)} %get-tuple-element.14), channel_id=1, source_target_pairs={{0,8},{8,16},{16,24},{24,0},{1,9},{9,17},{17,25},{25,1},{2,10},{10... | collective-permute-start | bytes 147464 | tf_op jit(solution)/shard_map/ppermute | solution.py:11
  159.4 5.3 %collective-permute-done.19 = f32[24,512]{1,0:T(8,128)S(1)} collective-permute-done((f32[24,512]{1,0:T(8,128)S(1)}, f32[24,512]{1,0:T(8,128)S(1)}, u32[]{:S(2)}, u32[]{:S(2)}) %collective-permute-start.19) | collective-permute-done | bytes 49184 | tf_op jit(solution)/shard_map/ppermute | solution.py:11
  (96 shorter events, 46.3 us)
Async XLA Ops:
  2.4 54.5 %all-to-all-start = ((f32[16,24,512]{2,1,0:T(8,128)}), f32[16,24,512]{2,1,0:T(8,128)S(1)}, u32[]{:S(2)}, u32[]{:S(2)}) async-start(f32[16,24,512]{2,1,0:T(8,128)} %broadcast_in_dim.8), calls=%async_computation | async-start | bytes 1572864 | tf_op jit(solution)/shard_map/all_to_all | solution.py:33
  17.6 9.2 %collective-permute-start = (f32[24,512]{1,0:T(8,128)S(1)}, f32[24,512]{1,0:T(8,128)S(1)}, u32[]{:S(2)}, u32[]{:S(2)}) collective-permute-start(f32[24,512]{1,0:T(8,128)S(1)} %copy-done.1), channel_id=1, source_target_pairs={{0,8},{8,16},{16,24},{24,0},{1,9},{9,17},{17,25},{25,1},{2,10},{10... | collective-permute-start | bytes 147464 | tf_op jit(solution)/shard_map/ppermute | solution.py:11
  20.0 7.2 %collective-permute-start.2 = (f32[24,512]{1,0:T(8,128)S(1)}, f32[24,512]{1,0:T(8,128)S(1)}, u32[]{:S(2)}, u32[]{:S(2)}) collective-permute-start(f32[24,512]{1,0:T(8,128)S(1)} %copy-done.1), channel_id=1, source_target_pairs={{0,24},{8,0},{16,8},{24,16},{1,25},{9,1},{17,9},{25,17},{2,26},{10... | collective-permute-start | bytes 147464 | tf_op jit(solution)/shard_map/ppermute | solution.py:11
  23.5 7.5 %collective-permute-start.1 = (f32[24,512]{1,0:T(8,128)S(1)}, f32[24,512]{1,0:T(8,128)S(1)}, u32[]{:S(2)}, u32[]{:S(2)}) collective-permute-start(f32[24,512]{1,0:T(8,128)S(1)} %copy-done.1), channel_id=1, source_target_pairs={{0,16},{8,24},{16,0},{24,8},{1,17},{9,25},{17,1},{25,9},{2,18},{10... | collective-permute-start | bytes 147464 | tf_op jit(solution)/shard_map/ppermute | solution.py:11
  31.0 12.2 %collective-permute-start.4 = (f32[4,24,512]{2,1,0:T(8,128)S(1)}, f32[4,24,512]{2,1,0:T(8,128)S(1)}, u32[]{:S(2)}, u32[]{:S(2)}) collective-permute-start(f32[4,24,512]{2,1,0:T(8,128)S(1)} %get-tuple-element.17), channel_id=1, source_target_pairs={{0,4},{2,6},{4,0},{6,2},{1,5},{3,7},{5,1},{7,3},{8,12},{10,14},{12... | collective-permute-start | bytes 589832 | tf_op jit(solution)/shard_map/ppermute | solution.py:11
  36.1 8.8 %collective-permute-start.3 = (f32[4,24,512]{2,1,0:T(8,128)S(1)}, f32[4,24,512]{2,1,0:T(8,128)S(1)}, u32[]{:S(2)}, u32[]{:S(2)}) collective-permute-start(f32[4,24,512]{2,1,0:T(8,128)S(1)} %get-tuple-element.17), channel_id=1, source_target_pairs={{0,2},{2,4},{4,6},{6,0},{1,3},{3,5},{5,7},{7,1},{8,10},{10,12},{12... | collective-permute-start | bytes 589832 | tf_op jit(solution)/shard_map/ppermute | solution.py:11
  38.7 7.6 %collective-permute-start.5 = (f32[4,24,512]{2,1,0:T(8,128)S(1)}, f32[4,24,512]{2,1,0:T(8,128)S(1)}, u32[]{:S(2)}, u32[]{:S(2)}) collective-permute-start(f32[4,24,512]{2,1,0:T(8,128)S(1)} %get-tuple-element.17), channel_id=1, source_target_pairs={{0,6},{2,0},{4,2},{6,4},{1,7},{3,1},{5,3},{7,5},{8,14},{10,8},{12,... | collective-permute-start | bytes 589832 | tf_op jit(solution)/shard_map/ppermute | solution.py:11
  46.6 4.3 %collective-permute-start.6 = (f32[4,4,24,512]{3,2,1,0:T(8,128)S(1)}, f32[4,4,24,512]{3,2,1,0:T(8,128)}, u32[]{:S(2)}, u32[]{:S(2)}) collective-permute-start(f32[4,4,24,512]{3,2,1,0:T(8,128)S(1)} %get-tuple-element.12), channel_id=1, source_target_pairs={{0,1},{1,0},{2,3},{3,2},{4,5},{5,4},{6,7},{7,6},{8,9},{9,8},{10,11... | collective-permute-start | bytes 2359304 | tf_op jit(solution)/shard_map/ppermute | solution.py:11
  64.9 4.1 %collective-permute-start.7 = (f32[2,2,4,4,24]{4,3,2,1,0:T(4,128)}, f32[2,2,4,4,24]{4,3,2,1,0:T(4,128)}, u32[]{:S(2)}, u32[]{:S(2)}) collective-permute-start(f32[2,2,4,4,24]{4,3,2,1,0:T(4,128)} %pad_maximum_fusion.6), channel_id=1, source_target_pairs={{0,1},{1,0},{2,3},{3,2},{4,5},{5,4},{6,7},{7,6},{8,9},{9,8},{10,11... | collective-permute-start | bytes 18440 | tf_op jit(solution)/shard_map/ppermute | solution.py:11
  70.6 10.0 %collective-permute-start.9 = (f32[2,2,4,4,24]{4,3,2,1,0:T(4,128)S(1)}, f32[2,2,4,4,24]{4,3,2,1,0:T(4,128)S(1)}, u32[]{:S(2)}, u32[]{:S(2)}) collective-permute-start(f32[2,2,4,4,24]{4,3,2,1,0:T(4,128)S(1)} %get-tuple-element.23), channel_id=1, source_target_pairs={{0,16},{8,24},{16,0},{24,8},{1,17},{9,25},{17,1},{25,9},{2,18},{10... | collective-permute-start | bytes 18440 | tf_op jit(solution)/shard_map/ppermute | solution.py:11
  74.6 6.0 %collective-permute-start.8 = (f32[2,2,4,4,24]{4,3,2,1,0:T(4,128)S(1)}, f32[2,2,4,4,24]{4,3,2,1,0:T(4,128)S(1)}, u32[]{:S(2)}, u32[]{:S(2)}) collective-permute-start(f32[2,2,4,4,24]{4,3,2,1,0:T(4,128)S(1)} %get-tuple-element.23), channel_id=1, source_target_pairs={{0,8},{8,16},{16,24},{24,0},{1,9},{9,17},{17,25},{25,1},{2,10},{10... | collective-permute-start | bytes 18440 | tf_op jit(solution)/shard_map/ppermute | solution.py:11
  78.6 7.0 %collective-permute-start.10 = (f32[2,2,4,4,24]{4,3,2,1,0:T(4,128)S(1)}, f32[2,2,4,4,24]{4,3,2,1,0:T(4,128)S(1)}, u32[]{:S(2)}, u32[]{:S(2)}) collective-permute-start(f32[2,2,4,4,24]{4,3,2,1,0:T(4,128)S(1)} %get-tuple-element.23), channel_id=1, source_target_pairs={{0,24},{8,0},{16,8},{24,16},{1,25},{9,1},{17,9},{25,17},{2,26},{10... | collective-permute-start | bytes 18440 | tf_op jit(solution)/shard_map/ppermute | solution.py:11
  85.9 20.2 %collective-permute-start.12 = (f32[2,2,4,4,24]{4,3,2,1,0:T(4,128)S(1)}, f32[2,2,4,4,24]{4,3,2,1,0:T(4,128)S(1)}, u32[]{:S(2)}, u32[]{:S(2)}) collective-permute-start(f32[2,2,4,4,24]{4,3,2,1,0:T(4,128)S(1)} %get-tuple-element.19), channel_id=1, source_target_pairs={{0,4},{2,6},{4,0},{6,2},{1,5},{3,7},{5,1},{7,3},{8,12},{10,14},{12... | collective-permute-start | bytes 18440 | tf_op jit(solution)/shard_map/ppermute | solution.py:11
  91.7 20.1 %all-to-all-start.1 = ((f32[16,8,128]{2,1,0:T(8,128)}), f32[16,8,128]{2,1,0:T(8,128)S(1)}, u32[]{:S(2)}, u32[]{:S(2)}) async-start(f32[16,8,128]{2,1,0:T(8,128)} %broadcast_in_dim.11), calls=%async_computation.1 | async-start | bytes 131072 | tf_op jit(solution)/shard_map/all_to_all | solution.py:53
  99.0 7.1 %collective-permute-start.11 = (f32[2,2,4,4,24]{4,3,2,1,0:T(4,128)S(1)}, f32[2,2,4,4,24]{4,3,2,1,0:T(4,128)S(1)}, u32[]{:S(2)}, u32[]{:S(2)}) collective-permute-start(f32[2,2,4,4,24]{4,3,2,1,0:T(4,128)S(1)} %get-tuple-element.19), channel_id=1, source_target_pairs={{0,2},{2,4},{4,6},{6,0},{1,3},{3,5},{5,7},{7,1},{8,10},{10,12},{12... | collective-permute-start | bytes 18440 | tf_op jit(solution)/shard_map/ppermute | solution.py:11
  102.4 5.8 %collective-permute-start.13 = (f32[2,2,4,4,24]{4,3,2,1,0:T(4,128)S(1)}, f32[2,2,4,4,24]{4,3,2,1,0:T(4,128)S(1)}, u32[]{:S(2)}, u32[]{:S(2)}) collective-permute-start(f32[2,2,4,4,24]{4,3,2,1,0:T(4,128)S(1)} %get-tuple-element.19), channel_id=1, source_target_pairs={{0,6},{2,0},{4,2},{6,4},{1,7},{3,1},{5,3},{7,5},{8,14},{10,8},{12,... | collective-permute-start | bytes 18440 | tf_op jit(solution)/shard_map/ppermute | solution.py:11
  116.5 48.9 %all-to-all-start.2 = ((f32[16,24,512]{2,1,0:T(8,128)}), f32[16,24,512]{2,1,0:T(8,128)}, u32[]{:S(2)}, u32[]{:S(2)}) async-start(f32[16,24,512]{2,1,0:T(8,128)} %fusion.53), calls=%async_computation.2 | async-start | bytes 1572864 | tf_op jit(solution)/shard_map/all_to_all | solution.py:85
  126.8 4.2 %collective-permute-start.14 = (f32[4,4,24,512]{3,2,1,0:T(8,128)S(1)}, f32[4,4,24,512]{3,2,1,0:T(8,128)S(1)}, u32[]{:S(2)}, u32[]{:S(2)}) collective-permute-start(f32[4,4,24,512]{3,2,1,0:T(8,128)S(1)} %bitcast.134), channel_id=1, source_target_pairs={{0,1},{1,0},{2,3},{3,2},{4,5},{5,4},{6,7},{7,6},{8,9},{9,8},{10,11... | collective-permute-start | bytes 2359304 | tf_op jit(solution)/shard_map/ppermute | solution.py:11
  131.2 10.2 %collective-permute-start.15 = (f32[4,24,512]{2,1,0:T(8,128)S(1)}, f32[4,24,512]{2,1,0:T(8,128)S(1)}, u32[]{:S(2)}, u32[]{:S(2)}) collective-permute-start(f32[4,24,512]{2,1,0:T(8,128)S(1)} %get-tuple-element.8), channel_id=1, source_target_pairs={{0,6},{2,0},{4,2},{6,4},{1,7},{3,1},{5,3},{7,5},{8,14},{10,8},{12,... | collective-permute-start | bytes 589832 | tf_op jit(solution)/shard_map/ppermute | solution.py:11
  136.1 14.0 %collective-permute-start.17 = (f32[4,24,512]{2,1,0:T(8,128)S(1)}, f32[4,24,512]{2,1,0:T(8,128)S(1)}, u32[]{:S(2)}, u32[]{:S(2)}) collective-permute-start(f32[4,24,512]{2,1,0:T(8,128)S(1)} %get-tuple-element.9), channel_id=1, source_target_pairs={{0,2},{2,4},{4,6},{6,0},{1,3},{3,5},{5,7},{7,1},{8,10},{10,12},{12... | collective-permute-start | bytes 589832 | tf_op jit(solution)/shard_map/ppermute | solution.py:11
  138.0 12.1 %collective-permute-start.16 = (f32[4,24,512]{2,1,0:T(8,128)S(1)}, f32[4,24,512]{2,1,0:T(8,128)S(1)}, u32[]{:S(2)}, u32[]{:S(2)}) collective-permute-start(f32[4,24,512]{2,1,0:T(8,128)S(1)} %get-tuple-element.10), channel_id=1, source_target_pairs={{0,4},{2,6},{4,0},{6,2},{1,5},{3,7},{5,1},{7,3},{8,12},{10,14},{12... | collective-permute-start | bytes 589832 | tf_op jit(solution)/shard_map/ppermute | solution.py:11
  150.2 9.0 %collective-permute-start.18 = (f32[24,512]{1,0:T(8,128)S(1)}, f32[24,512]{1,0:T(8,128)S(1)}, u32[]{:S(2)}, u32[]{:S(2)}) collective-permute-start(f32[24,512]{1,0:T(8,128)S(1)} %get-tuple-element.13), channel_id=1, source_target_pairs={{0,24},{8,0},{16,8},{24,16},{1,25},{9,1},{17,9},{25,17},{2,26},{10... | collective-permute-start | bytes 147464 | tf_op jit(solution)/shard_map/ppermute | solution.py:11
  152.1 7.3 %collective-permute-start.20 = (f32[24,512]{1,0:T(8,128)S(1)}, f32[24,512]{1,0:T(8,128)S(1)}, u32[]{:S(2)}, u32[]{:S(2)}) collective-permute-start(f32[24,512]{1,0:T(8,128)S(1)} %get-tuple-element.14), channel_id=1, source_target_pairs={{0,8},{8,16},{16,24},{24,0},{1,9},{9,17},{17,25},{25,1},{2,10},{10... | collective-permute-start | bytes 147464 | tf_op jit(solution)/shard_map/ppermute | solution.py:11
  157.2 7.5 %collective-permute-start.19 = (f32[24,512]{1,0:T(8,128)S(1)}, f32[24,512]{1,0:T(8,128)S(1)}, u32[]{:S(2)}, u32[]{:S(2)}) collective-permute-start(f32[24,512]{1,0:T(8,128)S(1)} %get-tuple-element.15), channel_id=1, source_target_pairs={{0,16},{8,24},{16,0},{24,8},{1,17},{9,25},{17,1},{25,9},{2,18},{10... | collective-permute-start | bytes 147464 | tf_op jit(solution)/shard_map/ppermute | solution.py:11
  (4 other events, 87.0 us)

commit v3 on v2

v3 whole, which is shorter than its diff:
```python
import jax
import jax.numpy as jnp
from jax import lax
from jax.sharding import Mesh, PartitionSpec as P

ALL = ("z", "x", "y", "core")
Z, SIDE, CORE = 16, 4, 2


def to_all(block, axes, count):
    sent = jnp.broadcast_to(block[None], (count,) + block.shape)
    return lax.all_to_all(sent, axes, 0, 0, tiled=True)


def shift(block, axis, count, by):
    return lax.ppermute(block, axis, [(i, (i + by) % count) for i in range(count)])


def home(parts, axis, count, dim, me):
    def part(by):
        return lax.dynamic_index_in_dim(parts, (me - by + count) % count, dim, keepdims=False)

    total = part(0)
    for by in range(1, count):
        total = total + shift(part(by), axis, count, -by)
    return total


def combine(tops, totals):
    top = jnp.max(tops, axis=0)
    return top, jnp.sum(totals * jnp.exp(tops - top[None]), axis=0)


def local(row_embed, col_embed, logit_scale, targets):
    own, width = row_embed.shape
    plane, across, along, core = (lax.axis_index(a) for a in ALL)
    other = shift(col_embed, "core", CORE, 1)
    pair = jnp.where(core == 0, jnp.concatenate([col_embed, other]), jnp.concatenate([other, col_embed]))
    cols = to_all(pair, ("x", "y"), SIDE * SIDE).reshape(SIDE * SIDE * CORE * own, width)
    rows = lax.all_gather(row_embed, "z", axis=0, tiled=True)
    row_count, col_count = rows.shape[0], cols.shape[0]

    scores = logit_scale * lax.dot_general(
        rows, cols, (((1,), (1,)), ((), ())),
        precision=lax.Precision.HIGHEST, preferred_element_type=jnp.float32,
    )
    row_top = jnp.max(scores, axis=1)
    row_total = jnp.sum(jnp.exp(scores - row_top[:, None]), axis=1)
    col_top = jnp.max(scores, axis=0)
    col_total = jnp.sum(jnp.exp(scores - col_top[None, :]), axis=0)

    row_message = jnp.concatenate(
        [row_top, row_total, targets.astype(jnp.float32), jnp.zeros((1024 - 2 * row_count - own,), jnp.float32)]
    ).reshape(8, 128)
    row_stats = to_all(row_message, "z", Z).reshape(Z, 1024)
    col_message = jnp.concatenate([col_top, col_total]).reshape(12, 128)
    col_stats = lax.all_gather(col_message, "x", axis=0).reshape(SIDE, 2, col_count)
    col_message = jnp.concatenate(combine(col_stats[:, 0], col_stats[:, 1])).reshape(12, 128)
    row_stats, col_message = lax.optimization_barrier((row_stats, col_message))
    col_stats = to_all(col_message, ("y", "core"), SIDE * CORE).reshape(SIDE * CORE, 2, col_count)
    col_top, col_total = combine(col_stats[:, 0], col_stats[:, 1])
    row_top, row_total = combine(row_stats[:, :row_count], row_stats[:, row_count:2 * row_count])
    row_targets = row_stats[:, 2 * row_count:2 * row_count + own].reshape(row_count).astype(jnp.int32)

    column_ids = plane * col_count + jnp.arange(col_count, dtype=jnp.int32)
    weights = (
        jnp.exp(scores - row_top[:, None]) * (0.5 / row_total)[:, None]
        + jnp.exp(scores - col_top[None, :]) * (0.5 / col_total)[None, :]
        - (row_targets[:, None] == column_ids[None, :]).astype(jnp.float32)
    )
    grad_rows = lax.dot_general(
        weights, cols, (((1,), (0,)), ((), ())),
        precision=lax.Precision.HIGH, preferred_element_type=jnp.float32,
    )
    row_parts = lax.all_to_all(grad_rows.reshape(Z, own, width), "z", 0, 0, tiled=True)
    grad_cols = lax.dot_general(
        weights, rows, (((0,), (0,)), ((), ())),
        precision=lax.Precision.HIGH, preferred_element_type=jnp.float32,
    ).reshape(SIDE, SIDE, CORE, own, width)
    col_sum = home(grad_cols, "core", CORE, 2, core)
    col_sum = home(col_sum, "y", SIDE, 1, along)
    col_sum = home(col_sum, "x", SIDE, 0, across)
    return logit_scale * jnp.sum(row_parts, axis=0), logit_scale * col_sum


def solution(mesh):
    grid = Mesh(mesh.devices.reshape(Z, SIDE, SIDE, CORE), ALL)
    placed = P(ALL, None)
    return jax.shard_map(
        local, mesh=grid, in_specs=(placed, placed, P(), P(ALL)), out_specs=(placed, placed), check_vma=False
    )
```

time: 169 us -> 146 us (0.86)
  blocking collectives: 0 us -> 50 us
  starting transfers between devices: 98.9 us -> 53.5 us
  waiting for transfers between devices: 40.6 us -> 24.5 us
  other arithmetic: 11 us -> 6.05 us
  local copies, waits for them, and re-layouts: 8.57 us -> 3.9 us
    all_gather x0 -> x2, blocking collectives: none -> 50 us  [the longest x1 38.1 us: local(): rows = lax.all_gather(row_embed, 'z', axis=0, tiled=True)]
    ppermute x21 -> x8, starting transfers between devices: 67.6 us -> 21.8 us  [shift(): lax.ppermute(block, axis, [(i, (i + by) % count) for i in range(count)])]
    ppermute x21 -> x8, waiting for transfers between devices: 32.5 us -> 15 us  [shift(): lax.ppermute(block, axis, [(i, (i + by) % count) for i in range(count)])]
    another operation x4 -> x0, local copies, waits for them, and re-layouts: 4.29 us -> none  [local(): stats = jnp.stack([col_top, col_total]).reshape(2, CORE, SIDE, SIDE, own)]
    another operation x16 -> x1, other arithmetic: 3.81 us -> 0.01 us  [local(): lax.all_gather(col_message, 'x', axis=0).reshape(SIDE, 2, col_count)]
    all_to_all x1, waiting for transfers between devices: 0.01 us -> 3.19 us  [local(): lax.all_to_all(grad_rows.reshape(Z, own, width), 'z', 0, 0, tiled=True)]
    all_to_all x1, starting transfers between devices: 8.77 us -> 11.3 us  [local(): lax.all_to_all(grad_rows.reshape(Z, own, width), 'z', 0, 0, tiled=True)]
    all_to_all x2 -> x3, starting transfers between devices: 22.5 us -> 20.5 us  [to_all(): return lax.all_to_all(sent, axes, 0, 0, tiled=True)]
  transfers between devices with their start and end apart: 24 -> 12, of which waited for: 13 -> 9; matrix products, arithmetic and copies ran while one was open for 5% -> 2% of each run, Pallas kernels for 0% -> 0%
where the time goes in v3:
time: 146 us; the launch traced here: 145 us
  starting transfers between devices  53.5 us (37%)
  blocking collectives  50 us (34%)
  waiting for transfers between devices  24.5 us (17%)
  other arithmetic  6.05 us (4%)
  matrix products  5.69 us (4%)
  local copies, waits for them, and re-layouts  3.9 us (3%)
  between operations  1.71 us (1%)
    all_gather x1, blocking collectives, local(): rows = lax.all_gather(row_embed, 'z', axis=0, tiled=True)  38.1 us
    ppermute x8, starting transfers between devices, shift(): lax.ppermute(block, axis, [(i, (i + by) % count) for i in range(count)])  21.8 us
    all_to_all x3, starting transfers between devices, to_all(): return lax.all_to_all(sent, axes, 0, 0, tiled=True)  20.5 us
    ppermute x8, waiting for transfers between devices, shift(): lax.ppermute(block, axis, [(i, (i + by) % count) for i in range(count)])  15 us
    all_gather x1, blocking collectives, local(): lax.all_gather(col_message, 'x', axis=0).reshape(SIDE, 2, col_count)  11.9 us
    all_to_all x1, starting transfers between devices, local(): lax.all_to_all(grad_rows.reshape(Z, own, width), 'z', 0, 0, tiled=True)  11.3 us
    all_to_all x3, waiting for transfers between devices, to_all(): return lax.all_to_all(sent, axes, 0, 0, tiled=True)  6.32 us
    all_to_all x1, waiting for transfers between devices, local(): lax.all_to_all(grad_rows.reshape(Z, own, width), 'z', 0, 0, tiled=True)  3.19 us
  transfers between devices with their start and end apart: 12, of which 9 were waited for; matrix products, arithmetic and copies ran while one was open for 2% of the time, Pallas kernels for 0%

profile of v3, /device:TPU:6, one launch (start us, length us, event | category | flops | bytes accessed | tf_op | source)
XLA Modules:
  0.0 145.4 jit_solution(9163535264769298651)
XLA Ops:
  0.6 1.9 %collective-permute-start = (f32[24,512]{1,0:T(8,128)}, f32[24,512]{1,0:T(8,128)S(1)}, u32[]{:S(2)}, u32[]{:S(2)}) collective-permute-start(f32[24,512]{1,0:T(8,128)} %param.5), channel_id=1, source_target_pairs={{0,1},{1,0},{2,3},{3,2},{4,5},{5,4},{6,7},{7,6},{8,9},{9,8},{10,11... | collective-permute-start | bytes 147464 | tf_op jit(solution)/shard_map/ppermute | solution.py:16
  6.2 9.6 %all-to-all-start = ((f32[16,48,512]{2,1,0:T(8,128)}), f32[16,48,512]{2,1,0:T(8,128)S(1)}, u32[]{:S(2)}, u32[]{:S(2)}) async-start(f32[16,48,512]{2,1,0:T(8,128)} %broadcast_in_dim.10), calls=%async_computation | async-start | bytes 3145728 | tf_op jit(solution)/shard_map/all_to_all | solution.py:12
  16.5 38.1 %all_gather.6 = f32[384,512]{1,0:T(8,128)S(1)} all-gather(f32[24,512]{1,0:T(8,128)S(1)} %copy-done.1), channel_id=1, replica_groups=mesh['z'=16,'x'=4,'y'=4,'core'=2] {'z'}, dimensions={0}, use_global_device_ids=true | all-gather | bytes 835584 | tf_op jit(solution)/shard_map/all_gather | solution.py:40
  54.6 2.2 %fusion.13 = (f32[768]{0:T(1024)S(1)}, f32[384]{0:T(512)S(1)}, f32[768,384]{0,1:T(8,128)S(1)}) fusion(f32[768,512]{1,0:T(8,128)S(1)} %bitcast.77, f32[384,512]{1,0:T(8,128)S(1)} %all_gather.6, f32[]{:T(128)S(6)} %copy.43), kind=kOutput, calls=%fused_computation.43 | convolution fusion | flops 1812822912 | bytes 3543556 | tf_op jit(solution)/shard_map/dot_general | solution.py:43
  58.9 6.7 %all-to-all-start.1 = ((f32[16,8,128]{2,1,0:T(8,128)}), f32[16,8,128]{2,1,0:T(8,128)S(1)}, u32[]{:S(2)}, u32[]{:S(2)}) async-start(f32[16,8,128]{2,1,0:T(8,128)} %broadcast_in_dim.13), calls=%async_computation.1 | async-start | bytes 131072 | tf_op jit(solution)/shard_map/all_to_all | solution.py:12
  65.7 11.9 %all_gather.7 = f32[4,12,128]{2,1,0:T(8,128)S(1)} all-gather(f32[1,12,128]{2,1,0:T(8,128)S(1)} %maximum_bitcast_fusion), channel_id=1, replica_groups=mesh['z'=16,'x'=4,'y'=4,'core'=2] {'x'}, dimensions={0}, use_global_device_ids=true | all-gather | bytes 30720 | tf_op jit(solution)/shard_map/all_gather | solution.py:57
  79.2 4.2 %all-to-all-start.2 = ((f32[8,12,128]{2,1,0:T(8,128)}), f32[8,12,128]{2,1,0:T(8,128)S(1)}, u32[]{:S(2)}, u32[]{:S(2)}) async-start(f32[8,12,128]{2,1,0:T(8,128)} %broadcast_in_dim.14), calls=%async_computation.2 | async-start | bytes 131072 | tf_op jit(solution)/shard_map/all_to_all | solution.py:12
  83.5 5.5 %all-to-all-done.2 = f32[8,12,128]{2,1,0:T(8,128)S(1)} async-done(((f32[8,12,128]{2,1,0:T(8,128)}), f32[8,12,128]{2,1,0:T(8,128)S(1)}, u32[]{:S(2)}, u32[]{:S(2)}) %all-to-all-start.2) | async-done | bytes 49184 | tf_op jit(solution)/shard_map/all_to_all | solution.py:12
  89.1 1.8 %bitcast_subtract_fusion = f32[384,768]{1,0:T(8,128)S(1)} fusion(f32[768,384]{0,1:T(8,128)} %copy-done, s32[768]{0:T(1024)S(1)} %iota_add_fusion, f32[768]{0:T(1024)S(1)} %broadcast_divide_fusion, f32[768]{0:T(1024)S(1)} %get-tuple-element.16, f32[384]{0:T(512)S(1)} %broadcast_divide_fusion.1, f32[384]{0:T(512)S(1)} %slice_reduce_fusion, ...), kind=kLoop, calls=%fused_computation.1 | loop fusion | flops 2359296 | bytes 2373120 | tf_op jit(solution)/shard_map/sub | solution.py:67
  90.9 2.1 %fusion.14 = f32[16,24,512]{2,1,0:T(8,128)} fusion(f32[16,24,768]{2,1,0:T(8,128)S(1)} %bitcast.79, f32[768,512,1]{1,0,2:T(8,128)S(1)} %bitcast.78), kind=kOutput, calls=%fused_computation.44 | convolution fusion | flops 905969664 | bytes 3538944 | tf_op jit(solution)/shard_map/dot_general | solution.py:71
  93.0 11.3 %all-to-all-start.3 = ((f32[16,24,512]{2,1,0:T(8,128)}), f32[16,24,512]{2,1,0:T(8,128)}, u32[]{:S(2)}, u32[]{:S(2)}) async-start(f32[16,24,512]{2,1,0:T(8,128)} %fusion.14), calls=%async_computation.3 | async-start | bytes 1572864 | tf_op jit(solution)/shard_map/all_to_all | solution.py:75
  105.8 1.9 %collective-permute-start.1 = (f32[4,4,24,512]{3,2,1,0:T(8,128)S(1)}, f32[4,4,24,512]{3,2,1,0:T(8,128)S(1)}, u32[]{:S(2)}, u32[]{:S(2)}) collective-permute-start(f32[4,4,24,512]{3,2,1,0:T(8,128)S(1)} %dynamic-slice_bitcast_fusion), channel_id=1, source_target_pairs={{0,1},{1,0},{2,3},{3,2},{4,5},{5,4},{6,7},{7,6},{8,9},{9,8},{10,11... | collective-permute-start | bytes 2359304 | tf_op jit(solution)/shard_map/ppermute | solution.py:16
  107.8 2.2 %collective-permute-done.1 = f32[4,4,24,512]{3,2,1,0:T(8,128)S(1)} collective-permute-done((f32[4,4,24,512]{3,2,1,0:T(8,128)S(1)}, f32[4,4,24,512]{3,2,1,0:T(8,128)S(1)}, u32[]{:S(2)}, u32[]{:S(2)}) %collective-permute-start.1) | collective-permute-done | bytes 786464 | tf_op jit(solution)/shard_map/ppermute | solution.py:16
  110.2 2.5 %collective-permute-start.4 = (f32[4,24,512]{2,1,0:T(8,128)S(1)}, f32[4,24,512]{2,1,0:T(8,128)S(1)}, u32[]{:S(2)}, u32[]{:S(2)}) collective-permute-start(f32[4,24,512]{2,1,0:T(8,128)S(1)} %get-tuple-element.11), channel_id=1, source_target_pairs={{0,2},{2,4},{4,6},{6,0},{1,3},{3,5},{5,7},{7,1},{8,10},{10,12},{12... | collective-permute-start | bytes 589832 | tf_op jit(solution)/shard_map/ppermute | solution.py:16
  112.7 4.0 %collective-permute-start.3 = (f32[4,24,512]{2,1,0:T(8,128)S(1)}, f32[4,24,512]{2,1,0:T(8,128)S(1)}, u32[]{:S(2)}, u32[]{:S(2)}) collective-permute-start(f32[4,24,512]{2,1,0:T(8,128)S(1)} %get-tuple-element.12), channel_id=1, source_target_pairs={{0,4},{2,6},{4,0},{6,2},{1,5},{3,7},{5,1},{7,3},{8,12},{10,14},{12... | collective-permute-start | bytes 589832 | tf_op jit(solution)/shard_map/ppermute | solution.py:16
  116.7 2.9 %collective-permute-start.2 = (f32[4,24,512]{2,1,0:T(8,128)S(1)}, f32[4,24,512]{2,1,0:T(8,128)S(1)}, u32[]{:S(2)}, u32[]{:S(2)}) collective-permute-start(f32[4,24,512]{2,1,0:T(8,128)S(1)} %get-tuple-element.10), channel_id=1, source_target_pairs={{0,6},{2,0},{4,2},{6,4},{1,7},{3,1},{5,3},{7,5},{8,14},{10,8},{12,... | collective-permute-start | bytes 589832 | tf_op jit(solution)/shard_map/ppermute | solution.py:16
  119.6 4.8 %collective-permute-done.4 = f32[4,24,512]{2,1,0:T(8,128)S(1)} collective-permute-done((f32[4,24,512]{2,1,0:T(8,128)S(1)}, f32[4,24,512]{2,1,0:T(8,128)S(1)}, u32[]{:S(2)}, u32[]{:S(2)}) %collective-permute-start.4) | collective-permute-done | bytes 196640 | tf_op jit(solution)/shard_map/ppermute | solution.py:16
  124.4 2.5 %collective-permute-done.2 = f32[4,24,512]{2,1,0:T(8,128)S(1)} collective-permute-done((f32[4,24,512]{2,1,0:T(8,128)S(1)}, f32[4,24,512]{2,1,0:T(8,128)S(1)}, u32[]{:S(2)}, u32[]{:S(2)}) %collective-permute-start.2) | collective-permute-done | bytes 196640 | tf_op jit(solution)/shard_map/ppermute | solution.py:16
  127.0 2.8 %collective-permute-start.7 = (f32[24,512]{1,0:T(8,128)S(1)}, f32[24,512]{1,0:T(8,128)S(1)}, u32[]{:S(2)}, u32[]{:S(2)}) collective-permute-start(f32[24,512]{1,0:T(8,128)S(1)} %get-tuple-element.14), channel_id=1, source_target_pairs={{0,8},{8,16},{16,24},{24,0},{1,9},{9,17},{17,25},{25,1},{2,10},{10... | collective-permute-start | bytes 147464 | tf_op jit(solution)/shard_map/ppermute | solution.py:16
  129.8 2.8 %collective-permute-start.6 = (f32[24,512]{1,0:T(8,128)S(1)}, f32[24,512]{1,0:T(8,128)S(1)}, u32[]{:S(2)}, u32[]{:S(2)}) collective-permute-start(f32[24,512]{1,0:T(8,128)S(1)} %get-tuple-element.15), channel_id=1, source_target_pairs={{0,16},{8,24},{16,0},{24,8},{1,17},{9,25},{17,1},{25,9},{2,18},{10... | collective-permute-start | bytes 147464 | tf_op jit(solution)/shard_map/ppermute | solution.py:16
  132.6 3.1 %collective-permute-start.5 = (f32[24,512]{1,0:T(8,128)S(1)}, f32[24,512]{1,0:T(8,128)S(1)}, u32[]{:S(2)}, u32[]{:S(2)}) collective-permute-start(f32[24,512]{1,0:T(8,128)S(1)} %get-tuple-element.13), channel_id=1, source_target_pairs={{0,24},{8,0},{16,8},{24,16},{1,25},{9,1},{17,9},{25,17},{2,26},{10... | collective-permute-start | bytes 147464 | tf_op jit(solution)/shard_map/ppermute | solution.py:16
  135.7 1.6 %collective-permute-done.6 = f32[24,512]{1,0:T(8,128)S(1)} collective-permute-done((f32[24,512]{1,0:T(8,128)S(1)}, f32[24,512]{1,0:T(8,128)S(1)}, u32[]{:S(2)}, u32[]{:S(2)}) %collective-permute-start.6) | collective-permute-done | bytes 49184 | tf_op jit(solution)/shard_map/ppermute | solution.py:16
  137.3 2.4 %collective-permute-done.5 = f32[24,512]{1,0:T(8,128)S(1)} collective-permute-done((f32[24,512]{1,0:T(8,128)S(1)}, f32[24,512]{1,0:T(8,128)S(1)}, u32[]{:S(2)}, u32[]{:S(2)}) %collective-permute-start.5) | collective-permute-done | bytes 49184 | tf_op jit(solution)/shard_map/ppermute | solution.py:16
  140.4 3.2 %all-to-all-done.3 = f32[16,24,512]{2,1,0:T(8,128)} async-done(((f32[16,24,512]{2,1,0:T(8,128)}), f32[16,24,512]{2,1,0:T(8,128)}, u32[]{:S(2)}, u32[]{:S(2)}) %all-to-all-start.3) | async-done | bytes 786464 | tf_op jit(solution)/shard_map/all_to_all | solution.py:75
  (44 shorter events, 11.8 us)
Async XLA Ops:
  0.6 3.3 %collective-permute-start = (f32[24,512]{1,0:T(8,128)}, f32[24,512]{1,0:T(8,128)S(1)}, u32[]{:S(2)}, u32[]{:S(2)}) collective-permute-start(f32[24,512]{1,0:T(8,128)} %param.5), channel_id=1, source_target_pairs={{0,1},{1,0},{2,3},{3,2},{4,5},{5,4},{6,7},{7,6},{8,9},{9,8},{10,11... | collective-permute-start | bytes 147464 | tf_op jit(solution)/shard_map/ppermute | solution.py:16
  6.2 10.2 %copy-start.2 = (s32[24]{0:T(128)S(1)}, s32[24]{0:T(128)}, u32[]{:S(2)}) copy-start(s32[24]{0:T(128)} %param.7) | copy-start | bytes 292
  6.2 10.2 %copy-start.1 = (f32[24,512]{1,0:T(8,128)S(1)}, f32[24,512]{1,0:T(8,128)}, u32[]{:S(2)}) copy-start(f32[24,512]{1,0:T(8,128)} %param.4) | copy-start | bytes 147460
  6.2 48.4 %all-to-all-start = ((f32[16,48,512]{2,1,0:T(8,128)}), f32[16,48,512]{2,1,0:T(8,128)S(1)}, u32[]{:S(2)}, u32[]{:S(2)}) async-start(f32[16,48,512]{2,1,0:T(8,128)} %broadcast_in_dim.10), calls=%async_computation | async-start | bytes 3145728 | tf_op jit(solution)/shard_map/all_to_all | solution.py:12
  56.8 1.0 copy-start
  58.9 19.6 %all-to-all-start.1 = ((f32[16,8,128]{2,1,0:T(8,128)}), f32[16,8,128]{2,1,0:T(8,128)S(1)}, u32[]{:S(2)}, u32[]{:S(2)}) async-start(f32[16,8,128]{2,1,0:T(8,128)} %broadcast_in_dim.13), calls=%async_computation.1 | async-start | bytes 131072 | tf_op jit(solution)/shard_map/all_to_all | solution.py:12
  79.2 9.9 %all-to-all-start.2 = ((f32[8,12,128]{2,1,0:T(8,128)}), f32[8,12,128]{2,1,0:T(8,128)S(1)}, u32[]{:S(2)}, u32[]{:S(2)}) async-start(f32[8,12,128]{2,1,0:T(8,128)} %broadcast_in_dim.14), calls=%async_computation.2 | async-start | bytes 131072 | tf_op jit(solution)/shard_map/all_to_all | solution.py:12
  93.0 50.6 %all-to-all-start.3 = ((f32[16,24,512]{2,1,0:T(8,128)}), f32[16,24,512]{2,1,0:T(8,128)}, u32[]{:S(2)}, u32[]{:S(2)}) async-start(f32[16,24,512]{2,1,0:T(8,128)} %fusion.14), calls=%async_computation.3 | async-start | bytes 1572864 | tf_op jit(solution)/shard_map/all_to_all | solution.py:75
  105.8 4.2 %collective-permute-start.1 = (f32[4,4,24,512]{3,2,1,0:T(8,128)S(1)}, f32[4,4,24,512]{3,2,1,0:T(8,128)S(1)}, u32[]{:S(2)}, u32[]{:S(2)}) collective-permute-start(f32[4,4,24,512]{3,2,1,0:T(8,128)S(1)} %dynamic-slice_bitcast_fusion), channel_id=1, source_target_pairs={{0,1},{1,0},{2,3},{3,2},{4,5},{5,4},{6,7},{7,6},{8,9},{9,8},{10,11... | collective-permute-start | bytes 2359304 | tf_op jit(solution)/shard_map/ppermute | solution.py:16
  110.2 14.3 %collective-permute-start.4 = (f32[4,24,512]{2,1,0:T(8,128)S(1)}, f32[4,24,512]{2,1,0:T(8,128)S(1)}, u32[]{:S(2)}, u32[]{:S(2)}) collective-permute-start(f32[4,24,512]{2,1,0:T(8,128)S(1)} %get-tuple-element.11), channel_id=1, source_target_pairs={{0,2},{2,4},{4,6},{6,0},{1,3},{3,5},{5,7},{7,1},{8,10},{10,12},{12... | collective-permute-start | bytes 589832 | tf_op jit(solution)/shard_map/ppermute | solution.py:16
  112.7 11.8 %collective-permute-start.3 = (f32[4,24,512]{2,1,0:T(8,128)S(1)}, f32[4,24,512]{2,1,0:T(8,128)S(1)}, u32[]{:S(2)}, u32[]{:S(2)}) collective-permute-start(f32[4,24,512]{2,1,0:T(8,128)S(1)} %get-tuple-element.12), channel_id=1, source_target_pairs={{0,4},{2,6},{4,0},{6,2},{1,5},{3,7},{5,1},{7,3},{8,12},{10,14},{12... | collective-permute-start | bytes 589832 | tf_op jit(solution)/shard_map/ppermute | solution.py:16
  116.7 10.3 %collective-permute-start.2 = (f32[4,24,512]{2,1,0:T(8,128)S(1)}, f32[4,24,512]{2,1,0:T(8,128)S(1)}, u32[]{:S(2)}, u32[]{:S(2)}) collective-permute-start(f32[4,24,512]{2,1,0:T(8,128)S(1)} %get-tuple-element.10), channel_id=1, source_target_pairs={{0,6},{2,0},{4,2},{6,4},{1,7},{3,1},{5,3},{7,5},{8,14},{10,8},{12,... | collective-permute-start | bytes 589832 | tf_op jit(solution)/shard_map/ppermute | solution.py:16
  127.0 8.6 %collective-permute-start.7 = (f32[24,512]{1,0:T(8,128)S(1)}, f32[24,512]{1,0:T(8,128)S(1)}, u32[]{:S(2)}, u32[]{:S(2)}) collective-permute-start(f32[24,512]{1,0:T(8,128)S(1)} %get-tuple-element.14), channel_id=1, source_target_pairs={{0,8},{8,16},{16,24},{24,0},{1,9},{9,17},{17,25},{25,1},{2,10},{10... | collective-permute-start | bytes 147464 | tf_op jit(solution)/shard_map/ppermute | solution.py:16
  129.8 7.5 %collective-permute-start.6 = (f32[24,512]{1,0:T(8,128)S(1)}, f32[24,512]{1,0:T(8,128)S(1)}, u32[]{:S(2)}, u32[]{:S(2)}) collective-permute-start(f32[24,512]{1,0:T(8,128)S(1)} %get-tuple-element.15), channel_id=1, source_target_pairs={{0,16},{8,24},{16,0},{24,8},{1,17},{9,25},{17,1},{25,9},{2,18},{10... | collective-permute-start | bytes 147464 | tf_op jit(solution)/shard_map/ppermute | solution.py:16
  132.6 7.2 %collective-permute-start.5 = (f32[24,512]{1,0:T(8,128)S(1)}, f32[24,512]{1,0:T(8,128)S(1)}, u32[]{:S(2)}, u32[]{:S(2)}) collective-permute-start(f32[24,512]{1,0:T(8,128)S(1)} %get-tuple-element.13), channel_id=1, source_target_pairs={{0,24},{8,0},{16,8},{24,16},{1,25},{9,1},{17,9},{25,17},{2,26},{10... | collective-permute-start | bytes 147464 | tf_op jit(solution)/shard_map/ppermute | solution.py:16

commit v4 on v3

v4 whole, which is shorter than its diff:
```python
import jax
import jax.numpy as jnp
from jax import lax
from jax.sharding import Mesh, PartitionSpec as P

ALL = ("z", "x", "y", "core")
Z, SIDE, CORE = 16, 4, 2
XY = SIDE * SIDE
SWAP = [(0, 1), (1, 0)]


def to_all(block, axes, count):
    sent = jnp.broadcast_to(block[None], (count,) + block.shape)
    return lax.all_to_all(sent, axes, 0, 0, tiled=True)


def log_sum_exp(values, axis):
    top = jnp.max(values, axis=axis, keepdims=True)
    return jnp.squeeze(top, axis) + jnp.log(jnp.sum(jnp.exp(values - top), axis=axis))


def local(row_embed, col_embed, logit_scale, targets):
    own, width = row_embed.shape
    plane, across, along, core = (lax.axis_index(a) for a in ALL)
    spot = (across * SIDE + along) * CORE + core
    targets = targets.astype(jnp.float32)

    mine = jnp.stack([col_embed, row_embed])
    other = lax.ppermute(mine, "core", SWAP)
    pair = jnp.where(core == 0, jnp.stack([mine, other], 1), jnp.stack([other, mine], 1))
    planes = to_all(pair, ("x", "y"), XY)
    planes = planes.transpose(1, 0, 2, 3, 4).reshape(2, XY * CORE * own, width)
    lines = lax.all_gather(jnp.stack([row_embed, col_embed]), "z", axis=1, tiled=True)
    line_count, plane_count = lines.shape[1], planes.shape[1]

    scores = logit_scale * lax.dot_general(
        lines, planes, (((2,), (2,)), ((0,), (0,))),
        precision=lax.Precision.HIGHEST, preferred_element_type=jnp.float32,
    )

    message = jnp.concatenate([log_sum_exp(scores, 1).reshape(2 * plane_count), targets])
    message = jnp.pad(message, (0, 16 * 128 - message.shape[0])).reshape(16, 128)
    heard = to_all(message, ("x", "y", "core"), XY * CORE).reshape(XY * CORE, 16 * 128)
    plane_lse = log_sum_exp(heard[:, :2 * plane_count], 0).reshape(2, plane_count)
    plane_targets = heard[:, 2 * plane_count:2 * plane_count + own].reshape(plane_count)

    own_lse = lax.dynamic_slice(plane_lse, (0, spot * own), (2, own))
    message = jnp.pad(jnp.concatenate([own_lse[1], own_lse[0], targets]), (0, 128 - 3 * own)).reshape(1, 128)
    heard = to_all(message, "z", Z).reshape(Z, 128)
    line_lse = heard[:, :2 * own].reshape(Z, 2, own).transpose(1, 0, 2).reshape(2, line_count)
    line_targets = heard[:, 2 * own:3 * own].reshape(line_count)

    numbers = jnp.arange(own)
    plane_ids = (plane * plane_count + jnp.arange(plane_count)).astype(jnp.float32)
    line_ids = ((jnp.arange(Z)[:, None] * (XY * CORE) + spot) * own + numbers[None, :]).reshape(line_count)
    line_key = jnp.stack([line_targets, line_ids.astype(jnp.float32)])
    plane_key = jnp.stack([plane_ids, plane_targets])
    weights = (
        0.5 * jnp.exp(scores - line_lse[:, :, None])
        + 0.5 * jnp.exp(scores - plane_lse[:, None, :])
        - (line_key[:, :, None] == plane_key[:, None, :]).astype(jnp.float32)
    )
    grads = lax.dot_general(
        weights, lines, (((1,), (1,)), ((0,), (0,))),
        precision=lax.Precision.HIGH, preferred_element_type=jnp.float32,
    ).reshape(2, XY, CORE, own, width)
    kept = lax.dynamic_index_in_dim(grads, core, 2, keepdims=False)
    given = lax.dynamic_index_in_dim(grads, 1 - core, 2, keepdims=False)
    parts = (kept + lax.ppermute(given, "core", SWAP)).transpose(1, 0, 2, 3)
    parts = lax.all_to_all(parts, ("x", "y"), 0, 0, tiled=True)
    total = logit_scale * jnp.sum(parts, axis=0)
    return total[1], total[0]


def solution(mesh):
    grid = Mesh(mesh.devices.reshape(Z, SIDE, SIDE, CORE), ALL)
    placed = P(ALL, None)
    return jax.shard_map(
        local, mesh=grid, in_specs=(placed, placed, P(), P(ALL)), out_specs=(placed, placed), check_vma=False
    )
```

time: 146 us -> 191 us (1.31)
  waiting for transfers between devices: 24.5 us -> 98.2 us
  starting transfers between devices: 53.5 us -> 28.9 us
  blocking collectives: 50 us -> 26.3 us
  between operations: 1.71 us -> 14.9 us
  matrix products: 5.69 us -> 11.2 us
  other arithmetic: 6.05 us -> 2.72 us
  local copies, waits for them, and re-layouts: 3.9 us -> 7.2 us
    all_to_all x3, waiting for transfers between devices: 6.32 us -> 62.6 us  [to_all(): return lax.all_to_all(sent, axes, 0, 0, tiled=True)]
    all_gather x2 -> x0, blocking collectives: 50 us -> none  [the longest x1 38.1 us: local(): rows = lax.all_gather(row_embed, 'z', axis=0, tiled=True)]
    all_gather x0 -> x1, waiting for transfers between devices: none -> 30.3 us  [local(): lax.all_gather(jnp.stack([row_embed, col_embed]), 'z', axis=1, tiled=True)]
    all_to_all x0 -> x1, blocking collectives: none -> 26.3 us  [local(): parts = lax.all_to_all(parts, ('x', 'y'), 0, 0, tiled=True)]
    ppermute x8 -> x2, starting transfers between devices: 21.8 us -> 3.83 us  [the longest x1 1.92 us: local(): parts = (kept + lax.ppermute(given, 'core', SWAP)).transpose(1, 0, 2, 3)]
    all_to_all x1 -> x0, starting transfers between devices: 11.3 us -> none  [local(): lax.all_to_all(grad_rows.reshape(Z, own, width), 'z', 0, 0, tiled=True)]
    ppermute x8 -> x2, waiting for transfers between devices: 15 us -> 4.64 us  [the longest x1 3.38 us: local(): parts = (kept + lax.ppermute(given, 'core', SWAP)).transpose(1, 0, 2, 3)]
    dot_general x3 -> x2, matrix products: 5.69 us -> 11.2 us  [the longest x1 6.45 us: local(): lax.dot_general(lines, planes, (((2,), (2,)), ((0,), (0,))), precision=la...]
  transfers between devices with their start and end apart: 12 -> 6, of which waited for: 9 -> 6; matrix products, arithmetic and copies ran while one was open for 2% -> 1% of each run, Pallas kernels for 0% -> 0%
where the time goes in v4:
time: 191 us; the launch traced here: 189 us
  waiting for transfers between devices  98.2 us (51%)
  starting transfers between devices  28.9 us (15%)
  blocking collectives  26.3 us (14%)
  between operations  14.9 us (8%)
  matrix products  11.2 us (6%)
  local copies, waits for them, and re-layouts  7.2 us (4%)
  other arithmetic  2.72 us (1%)
    all_to_all x3, waiting for transfers between devices, to_all(): return lax.all_to_all(sent, axes, 0, 0, tiled=True)  62.6 us
    all_gather x1, waiting for transfers between devices, local(): lax.all_gather(jnp.stack([row_embed, col_embed]), 'z', axis=1, tiled=True)  30.3 us
    all_to_all x1, blocking collectives, local(): parts = lax.all_to_all(parts, ('x', 'y'), 0, 0, tiled=True)  26.3 us
    all_to_all x3, starting transfers between devices, to_all(): return lax.all_to_all(sent, axes, 0, 0, tiled=True)  25 us
    dot_general x1, matrix products, local(): lax.dot_general(lines, planes, (((2,), (2,)), ((0,), (0,))), precision=la...  6.45 us
    dot_general x1, matrix products, local(): lax.dot_general(weights, lines, (((1,), (1,)), ((0,), (0,))), precision=l...  4.72 us
  transfers between devices with their start and end apart: 6, of which 6 were waited for; matrix products, arithmetic and copies ran while one was open for 1% of the time, Pallas kernels for 0%

profile of v4, /device:TPU:6, one launch (start us, length us, event | category | flops | bytes accessed | tf_op | source)
XLA Modules:
  0.0 189.3 jit_solution(11792730187926931900)
XLA Ops:
  7.2 1.5 fusion.20
  8.7 1.9 %collective-permute-start = (f32[2,24,512]{2,1,0:T(8,128)S(1)}, f32[2,24,512]{2,1,0:T(8,128)S(1)}, u32[]{:S(2)}, u32[]{:S(2)}) collective-permute-start(f32[2,24,512]{2,1,0:T(8,128)S(1)} %get-tuple-element.7), channel_id=1, source_target_pairs={{0,1},{1,0},{2,3},{3,2},{4,5},{5,4},{6,7},{7,6},{8,9},{9,8},{10,11... | collective-permute-start | bytes 294920 | tf_op jit(solution)/shard_map/ppermute | solution.py:29
  10.6 1.3 collective-permute-done
  11.9 2.1 %broadcast_in_dim.8 = f32[16,2,2,24,512]{4,3,2,1,0:T(8,128)} broadcast(f32[2,2,24,512]{3,2,1,0:T(8,128)S(1)} %copy.12), dimensions={1,2,3,4} | broadcast | bytes 3342336 | tf_op jit(solution)/shard_map/broadcast_in_dim | solution.py:13
  14.0 9.6 %all-to-all-start = ((f32[16,2,2,24,512]{4,3,2,1,0:T(8,128)}), f32[16,2,2,24,512]{4,3,2,1,0:T(8,128)S(1)}, u32[]{:S(2)}, u32[]{:S(2)}) async-start(f32[16,2,2,24,512]{4,3,2,1,0:T(8,128)} %broadcast_in_dim.8), calls=%async_computation | async-start | bytes 6291456 | tf_op jit(solution)/shard_map/all_to_all | solution.py:14
  23.6 0.7 all-gather.2.cloned.1.call-update
  25.0 43.5 %all-to-all-done = f32[16,2,2,24,512]{4,3,2,1,0:T(8,128)S(1)} async-done(((f32[16,2,2,24,512]{4,3,2,1,0:T(8,128)}), f32[16,2,2,24,512]{4,3,2,1,0:T(8,128)S(1)}, u32[]{:S(2)}, u32[]{:S(2)}) %all-to-all-start) | async-done | bytes 3145760 | tf_op jit(solution)/shard_map/all_to_all | solution.py:14
  68.5 2.0 %copy.13 = f32[2,16,2,24,512]{4,3,2,1,0:T(8,128)} copy(f32[2,16,2,24,512]{4,3,2,0,1:T(8,128)S(1)} %bitcast.37) | data formatting | bytes 6291456 | tf_op jit(solution)/shard_map/transpose | solution.py:32
  70.5 30.3 %all-gather.2.cloned.1.call-done = f32[2,384,512]{2,1,0:T(8,128)} async-done(((f32[2,24,512]{2,1,0:T(8,128)}), f32[2,384,512]{2,1,0:T(8,128)}) %all-gather.2.cloned.1.call-update) | async-done | bytes 1572880 | tf_op jit(solution)/shard_map/all_gather | solution.py:33
  100.8 6.5 %multiply_reduce_fusion = (f32[2,768]{1,0:T(2,128)S(1)}, f32[2,384,768]{2,1,0:T(8,128)S(1)}) fusion(f32[]{:T(128)S(6)} %copy.25, f32[2,384,512]{2,1,0:T(8,128)} %all-gather.2.cloned.1.call-done, f32[2,768,512]{2,1,0:T(8,128)} %bitcast.38), kind=kOutput, calls=%fused_computation.12 | convolution fusion | flops 3625056768 | bytes 7084036 | tf_op jit(solution)/shard_map/dot_general | solution.py:36
  107.3 0.4 exponential_reduce_fusion
  107.7 0.7 broadcast_in_dim.10
  108.4 7.4 %all-to-all-start.1 = ((f32[32,16,128]{2,1,0:T(8,128)}), f32[32,16,128]{2,1,0:T(8,128)S(1)}, u32[]{:S(2)}, u32[]{:S(2)}) async-start(f32[32,16,128]{2,1,0:T(8,128)} %broadcast_in_dim.10), calls=%async_computation.1 | async-start | bytes 524288 | tf_op jit(solution)/shard_map/all_to_all | solution.py:14
  116.0 6.8 %all-to-all-done.1 = f32[32,16,128]{2,1,0:T(8,128)S(1)} async-done(((f32[32,16,128]{2,1,0:T(8,128)}), f32[32,16,128]{2,1,0:T(8,128)S(1)}, u32[]{:S(2)}, u32[]{:S(2)}) %all-to-all-start.1) | async-done | bytes 262176 | tf_op jit(solution)/shard_map/all_to_all | solution.py:14
  123.2 0.6 broadcast_in_dim.11
  123.8 8.0 %all-to-all-start.2 = ((f32[16,1,128]{2,1,0:T(1,128)}), f32[16,1,128]{2,1,0:T(1,128)S(1)}, u32[]{:S(2)}, u32[]{:S(2)}) async-start(f32[16,1,128]{2,1,0:T(1,128)} %broadcast_in_dim.11), calls=%async_computation.2 | async-start | bytes 16384 | tf_op jit(solution)/shard_map/all_to_all | solution.py:14
  132.0 12.3 %all-to-all-done.2 = f32[16,1,128]{2,1,0:T(1,128)S(1)} async-done(((f32[16,1,128]{2,1,0:T(1,128)}), f32[16,1,128]{2,1,0:T(1,128)S(1)}, u32[]{:S(2)}, u32[]{:S(2)}) %all-to-all-start.2) | async-done | bytes 8224 | tf_op jit(solution)/shard_map/all_to_all | solution.py:14
  144.6 4.7 %fusion = f32[2,768,512]{2,1,0:T(8,128)S(1)} fusion(f32[2,384,512]{2,1,0:T(8,128)} %all-gather.2.cloned.1.call-done, f32[2,384,768]{2,1,0:T(8,128)S(1)} %get-tuple-element.12, f32[2,768]{1,0:T(2,128)S(1)} %pad_maximum_fusion.2, f32[2,384]{1,0:T(2,128)S(1)} %pad_maximum_fusion.3, f32[2,768]{1,0:T(2,128)S(1)} %add.95, f32[2,384]{1,0:T(2,128)S(1)} %sub.44, ...), kind=kOutput, calls=%fused_computation | convolution fusion | flops 1816657920 | bytes 7096324 | tf_op jit(solution)/shard_map/dot_general | solution.py:63
  149.3 0.3 constant_dynamic-slice_fusion.1
  149.8 1.9 %collective-permute-start.1 = (f32[2,16,24,512]{3,2,0,1:T(8,128)S(1)}, f32[2,16,24,512]{3,2,0,1:T(8,128)S(1)}, u32[]{:S(2)}, u32[]{:S(2)}) collective-permute-start(f32[2,16,24,512]{3,2,0,1:T(8,128)S(1)} %bitcast.43), channel_id=1, source_target_pairs={{0,1},{1,0},{2,3},{3,2},{4,5},{5,4},{6,7},{7,6},{8,9},{9,8},{10,11... | collective-permute-start | bytes 4718600 | tf_op jit(solution)/shard_map/ppermute | solution.py:69
  151.7 3.4 %collective-permute-done.1 = f32[2,16,24,512]{3,2,0,1:T(8,128)S(1)} collective-permute-done((f32[2,16,24,512]{3,2,0,1:T(8,128)S(1)}, f32[2,16,24,512]{3,2,0,1:T(8,128)S(1)}, u32[]{:S(2)}, u32[]{:S(2)}) %collective-permute-start.1) | collective-permute-done | bytes 1572896 | tf_op jit(solution)/shard_map/ppermute | solution.py:69
  155.1 0.3 fusion.11
  155.5 26.3 %all_to_all.20 = f32[16,2,24,512]{3,2,1,0:T(8,128)S(1)} all-to-all(f32[16,2,24,512]{3,2,1,0:T(8,128)S(1)} %fusion.11), channel_id=1, replica_groups=mesh['z'=16,'x'=4,'y'=4,'core'=2] {'x','y'}, dimensions={0} | all-to-all | bytes 3145728 | tf_op jit(solution)/shard_map/all_to_all | solution.py:70
  181.8 0.6 slice_bitcast_fusion
  (33 shorter events, 1.3 us)
Async XLA Ops:
  8.7 3.2 %collective-permute-start = (f32[2,24,512]{2,1,0:T(8,128)S(1)}, f32[2,24,512]{2,1,0:T(8,128)S(1)}, u32[]{:S(2)}, u32[]{:S(2)}) collective-permute-start(f32[2,24,512]{2,1,0:T(8,128)S(1)} %get-tuple-element.7), channel_id=1, source_target_pairs={{0,1},{1,0},{2,3},{3,2},{4,5},{5,4},{6,7},{7,6},{8,9},{9,8},{10,11... | collective-permute-start | bytes 294920 | tf_op jit(solution)/shard_map/ppermute | solution.py:29
  14.0 11.0 %copy-start = (s32[24]{0:T(128)S(1)}, s32[24]{0:T(128)}, u32[]{:S(2)}) copy-start(s32[24]{0:T(128)} %param.7) | copy-start | bytes 292
  14.0 54.5 %all-to-all-start = ((f32[16,2,2,24,512]{4,3,2,1,0:T(8,128)}), f32[16,2,2,24,512]{4,3,2,1,0:T(8,128)S(1)}, u32[]{:S(2)}, u32[]{:S(2)}) async-start(f32[16,2,2,24,512]{4,3,2,1,0:T(8,128)} %broadcast_in_dim.8), calls=%async_computation | async-start | bytes 6291456 | tf_op jit(solution)/shard_map/all_to_all | solution.py:14
  23.6 77.2 %all-gather.2.cloned.1.call-start = ((), (), s32[]{:S(2)}) async-start(), calls=%async_computation.4 | async-start | bytes 1671168 | tf_op jit(solution)/shard_map/all_gather | solution.py:33
  108.4 14.4 %all-to-all-start.1 = ((f32[32,16,128]{2,1,0:T(8,128)}), f32[32,16,128]{2,1,0:T(8,128)S(1)}, u32[]{:S(2)}, u32[]{:S(2)}) async-start(f32[32,16,128]{2,1,0:T(8,128)} %broadcast_in_dim.10), calls=%async_computation.1 | async-start | bytes 524288 | tf_op jit(solution)/shard_map/all_to_all | solution.py:14
  123.8 20.4 %all-to-all-start.2 = ((f32[16,1,128]{2,1,0:T(1,128)}), f32[16,1,128]{2,1,0:T(1,128)S(1)}, u32[]{:S(2)}, u32[]{:S(2)}) async-start(f32[16,1,128]{2,1,0:T(1,128)} %broadcast_in_dim.11), calls=%async_computation.2 | async-start | bytes 16384 | tf_op jit(solution)/shard_map/all_to_all | solution.py:14
  149.8 5.3 %collective-permute-start.1 = (f32[2,16,24,512]{3,2,0,1:T(8,128)S(1)}, f32[2,16,24,512]{3,2,0,1:T(8,128)S(1)}, u32[]{:S(2)}, u32[]{:S(2)}) collective-permute-start(f32[2,16,24,512]{3,2,0,1:T(8,128)S(1)} %bitcast.43), channel_id=1, source_target_pairs={{0,1},{1,0},{2,3},{3,2},{4,5},{5,4},{6,7},{7,6},{8,9},{9,8},{10,11... | collective-permute-start | bytes 4718600 | tf_op jit(solution)/shard_map/ppermute | solution.py:69
Sparse Core Ops, SparseCore 0:
  26.5 74.2 all-gather.1

commit v5 on v4

v5 whole, which is shorter than its diff:
```python
import jax
import jax.numpy as jnp
from jax import lax
from jax.experimental import pallas as pl
from jax.experimental.pallas import tpu as pltpu
from jax.sharding import Mesh, PartitionSpec as P

ALL = ("far", "pair", "x", "y", "core")
FAR, PAIR, SIDE, CORE = 8, 2, 4, 2
Z, XY = FAR * PAIR, SIDE * SIDE
SWAP = [(0, 1), (1, 0)]
VMEM = pl.BlockSpec(memory_space=pltpu.VMEM)
PARAMS = pltpu.CompilerParams(vmem_limit_bytes=48 * 1024 * 1024)


def to_all(block, axes, count):
    sent = jnp.broadcast_to(block[None], (count,) + block.shape)
    return lax.all_to_all(sent, axes, 0, 0, tiled=True)


def log_sum_exp(values, axis):
    top = jnp.max(values, axis=axis, keepdims=True)
    return jnp.squeeze(top, axis) + jnp.log(jnp.sum(jnp.exp(values - top), axis=axis))


def flat(ref, which):
    block = ref[:, which]
    return block.reshape(block.shape[0] * block.shape[1], block.shape[2])


def score_kernel(scale_ref, line0_ref, line1_ref, near_ref, far_ref, near_out, far_out, lse_out):
    scale = scale_ref[0]
    half = near_out.shape[1] // 2
    for side, (plane_ref, out) in enumerate(((near_ref, near_out), (far_ref, far_out))):
        for b in range(2):
            plane = flat(plane_ref, b)
            tops = []
            for k, line_ref in enumerate((line0_ref, line1_ref)):
                block = scale * lax.dot_general(
                    flat(line_ref, 1 - b), plane, (((1,), (1,)), ((), ())),
                    precision=lax.Precision.HIGHEST, preferred_element_type=jnp.float32,
                )
                out[b, k * half:(k + 1) * half, :] = block
                tops.append(jnp.max(block, axis=0, keepdims=True))
            top = jnp.maximum(tops[0], tops[1])
            total = jnp.sum(jnp.exp(out[b] - top), axis=0, keepdims=True)
            row = side * 2 + b
            lse_out[row:row + 1, :] = top + jnp.log(total)


def split(values):
    high = values.astype(jnp.bfloat16)
    return high, (values - high.astype(jnp.float32)).astype(jnp.bfloat16)


def upright(row):
    return jnp.transpose(jnp.broadcast_to(row, (128, row.shape[1])))[:, :1]


def grad_kernel(scale_ref, score_ref, line0_ref, line1_ref, line_ref, plane_ref, out):
    scale = scale_ref[0]
    count = score_ref.shape[1]
    for b in range(2):
        scores = score_ref[b]
        line_lse, line_key = upright(line_ref[b:b + 1, :]), upright(line_ref[2 + b:3 + b, :])
        plane_lse, plane_key = plane_ref[b:b + 1, :], plane_ref[2 + b:3 + b, :]
        weights = (
            0.5 * jnp.exp(scores - line_lse)
            + 0.5 * jnp.exp(scores - plane_lse)
            - jnp.where(line_key == plane_key, 1.0, 0.0)
        )
        total = None
        for k, ref in enumerate((line0_ref, line1_ref)):
            high, low = split(weights[k * count // 2:(k + 1) * count // 2])
            line_high, line_low = split(flat(ref, 1 - b))
            for left, right in ((high, line_high), (high, line_low), (low, line_high)):
                term = lax.dot_general(
                    left, right, (((0,), (0,)), ((), ())), preferred_element_type=jnp.float32
                )
                total = term if total is None else total + term
        out[:, b] = (scale * total).reshape(out.shape[0], out.shape[2], out.shape[3])


def local(row_embed, col_embed, logit_scale, targets):
    own, width = row_embed.shape
    far, pair, across, along, core = (lax.axis_index(a) for a in ALL)
    chip = across * SIDE + along
    spot = chip * CORE + core
    scale = logit_scale.reshape(1)
    targets = targets.astype(jnp.float32)
    line_count, plane_count = Z * own, XY * own

    def mine_first(first, second, me):
        return jnp.where(me == 0, first, second), jnp.where(me == 0, second, first)

    mine = jnp.stack([col_embed, row_embed])
    near = to_all(mine, ("x", "y"), XY)
    line0 = lax.all_gather(mine, "far", axis=0)
    line1 = lax.ppermute(line0, "pair", SWAP)
    away = lax.ppermute(near, "core", SWAP)

    smem = pl.BlockSpec(memory_space=pltpu.SMEM)
    block = jax.ShapeDtypeStruct((2, line_count, plane_count), jnp.float32)
    near_scores, away_scores, lse = pl.pallas_call(
        score_kernel,
        out_shape=(block, block, jax.ShapeDtypeStruct((4, plane_count), jnp.float32)),
        in_specs=[smem, VMEM, VMEM, VMEM, VMEM],
        out_specs=(VMEM, VMEM, VMEM),
        compiler_params=PARAMS,
        name="scores",
    )(scale, line0, line1, near, away)

    message = jnp.concatenate(mine_first(lse[:2], lse[2:], core)).reshape(4 * plane_count)
    message = jnp.concatenate([message, targets])
    message = jnp.pad(message, (0, 16 * 128 - message.shape[0])).reshape(16, 128)
    heard = to_all(message, ("x", "y", "core"), XY * CORE).reshape(XY * CORE, 16 * 128)
    plane_lse = log_sum_exp(heard[:, :4 * plane_count], 0).reshape(CORE, 2, plane_count)
    plane_targets = heard[:, 4 * plane_count:4 * plane_count + own].reshape(XY, CORE, own)
    plane_targets = plane_targets.transpose(1, 0, 2).reshape(CORE, plane_count)
    near_lse, away_lse = mine_first(plane_lse[0], plane_lse[1], core)
    near_targets, away_targets = mine_first(plane_targets[0], plane_targets[1], core)

    own_lse = lax.dynamic_slice(near_lse, (0, chip * own), (2, own)).reshape(2 * own)
    message = jnp.pad(jnp.concatenate([own_lse, targets]), (0, 128 - 3 * own)).reshape(1, 128)
    heard = to_all(message, ("far", "pair"), Z).reshape(FAR, PAIR, 128)[:, :, :3 * own].reshape(FAR, PAIR, 3, own)
    heard = jnp.stack(mine_first(heard[:, 0], heard[:, 1], pair)).transpose(2, 0, 1, 3).reshape(3, line_count)

    numbers = jnp.arange(own)
    line_z = jnp.arange(FAR)[None, :] * PAIR + jnp.stack([pair, 1 - pair])[:, None]
    line_ids = ((line_z[:, :, None] * (XY * CORE) + spot) * own + numbers).reshape(line_count).astype(jnp.float32)
    line_info = jnp.stack([heard[1], heard[0], heard[2], line_ids])

    def plane_info(plane_lse, plane_targets, which):
        ids = (((far * PAIR + pair) * XY + jnp.arange(XY)[:, None]) * CORE + which) * own + numbers[None, :]
        ids = ids.reshape(1, plane_count).astype(jnp.float32)
        return jnp.concatenate([plane_lse, ids, plane_targets[None]])

    def grads(scores, info):
        return pl.pallas_call(
            grad_kernel,
            out_shape=jax.ShapeDtypeStruct((XY, 2, own, width), jnp.float32),
            in_specs=[smem, VMEM, VMEM, VMEM, VMEM, VMEM],
            out_specs=VMEM,
            compiler_params=PARAMS,
            name="grads",
        )(scale, scores, line0, line1, line_info, info)

    given = grads(away_scores, plane_info(away_lse, away_targets, 1 - core))
    taken = lax.ppermute(given, "core", SWAP)
    parts = grads(near_scores, plane_info(near_lse, near_targets, core)) + taken
    total = jnp.sum(lax.all_to_all(parts, ("x", "y"), 0, 0, tiled=True), axis=0)
    return total[1], total[0]


def solution(mesh):
    grid = Mesh(mesh.devices.reshape(FAR, PAIR, SIDE, SIDE, CORE), ALL)
    placed = P(ALL, None)
    return jax.shard_map(
        local, mesh=grid, in_specs=(placed, placed, P(), P(ALL)), out_specs=(placed, placed), check_vma=False
    )
```

time: 191 us -> 172 us (0.901)
  blocking collectives: 26.3 us -> 93.3 us
  waiting for transfers between devices: 98.2 us -> 31.6 us
  between operations: 14.9 us -> 1.58 us
  matrix products: 11.2 us -> 0 us
  Pallas kernels: 0 us -> 11.2 us
  starting transfers between devices: 28.9 us -> 21.2 us
    all_to_all x3 -> x2, waiting for transfers between devices: 62.6 us -> 19 us  [to_all(): return lax.all_to_all(sent, axes, 0, 0, tiled=True)]
    all_gather x0 -> x1, blocking collectives: none -> 39 us  [local(): line0 = lax.all_gather(mine, 'far', axis=0)]
    all_gather x1 -> x0, waiting for transfers between devices: 30.3 us -> none  [local(): lax.all_gather(jnp.stack([row_embed, col_embed]), 'z', axis=1, tiled=True)]
    all_to_all x1 -> x2, blocking collectives: 26.3 us -> 54.3 us  [the longest x1 27.9 us: to_all(): return lax.all_to_all(sent, axes, 0, 0, tiled=True)]
    all_to_all x3 -> x2, starting transfers between devices: 25 us -> 12.9 us  [to_all(): return lax.all_to_all(sent, axes, 0, 0, tiled=True)]
    pallas_call x0 -> x3, Pallas kernels: none -> 11.2 us  [the longest x1 7.73 us: local(): pl.pallas_call(score_kernel, out_shape=(block, block, jax.ShapeDtypeStruc...]
    dot_general x2 -> x0, matrix products: 11.2 us -> none  [the longest x1 6.45 us: local(): lax.dot_general(lines, planes, (((2,), (2,)), ((0,), (0,))), precision=la...]
    ppermute x2 -> x3, waiting for transfers between devices: 4.64 us -> 12.6 us  [the longest x1 12.4 us: local(): line1 = lax.ppermute(line0, 'pair', SWAP)]
  transfers between devices with their start and end apart: 6 -> 5, of which waited for: 6 -> 4; matrix products, arithmetic and copies ran while one was open for 1% -> 0% of each run, Pallas kernels for 0% -> 1%
where the time goes in v5:
time: 172 us; the launch traced here: 170 us
  blocking collectives  93.3 us (54%)
  waiting for transfers between devices  31.6 us (18%)
  starting transfers between devices  21.2 us (12%)
  Pallas kernels  11.2 us (7%)
  local copies, waits for them, and re-layouts  7.83 us (5%)
  other arithmetic  3.47 us (2%)
    all_gather x1, blocking collectives, local(): line0 = lax.all_gather(mine, 'far', axis=0)  39 us
    all_to_all x1, blocking collectives, to_all(): return lax.all_to_all(sent, axes, 0, 0, tiled=True)  27.9 us
    all_to_all x1, blocking collectives, local(): total = jnp.sum(lax.all_to_all(parts, ('x', 'y'), 0, 0, tiled=True), axis=0)  26.4 us
    all_to_all x2, waiting for transfers between devices, to_all(): return lax.all_to_all(sent, axes, 0, 0, tiled=True)  19 us
    all_to_all x2, starting transfers between devices, to_all(): return lax.all_to_all(sent, axes, 0, 0, tiled=True)  12.9 us
    ppermute x1, waiting for transfers between devices, local(): line1 = lax.ppermute(line0, 'pair', SWAP)  12.4 us
    pallas_call x1, Pallas kernels, local(): pl.pallas_call(score_kernel, out_shape=(block, block, jax.ShapeDtypeStruc...  7.73 us
    unnamed x11, local copies, waits for them, and re-layouts  4.64 us
  transfers between devices with their start and end apart: 5, of which 4 were waited for; matrix products, arithmetic and copies ran while one was open for 0% of the time, Pallas kernels for 1%

profile of v5, /device:TPU:6, one launch (start us, length us, event | category | flops | bytes accessed | tf_op | source)
XLA Modules:
  0.0 170.2 jit_solution(932937285276720837)
XLA Ops:
  0.6 0.8 pad_maximum_fusion
  1.7 27.9 %all_to_all.20.near_ref = f32[16,2,24,512]{3,2,1,0:T(8,128)S(1)} all-to-all(f32[16,2,24,512]{3,2,1,0:T(8,128)S(1)} %broadcast_in_dim.8), channel_id=1, replica_groups=mesh['far'=8,'pair'=2,'x'=4,'y'=4,'core'=2] {'x','y'}, dimensions={0} | all-to-all | bytes 3145728 | tf_op jit(solution)/shard_map/all_to_all | solution.py:18
  29.6 1.9 %collective-permute-start.1 = (f32[16,2,24,512]{3,2,1,0:T(8,128)S(1)}, f32[16,2,24,512]{3,2,1,0:T(8,128)}, u32[]{:S(2)}, u32[]{:S(2)}) collective-permute-start(f32[16,2,24,512]{3,2,1,0:T(8,128)S(1)} %all_to_all.20.near_ref), channel_id=1, source_target_pairs={{0,1},{1,0},{2,3},{3,2},{4,5},{5,4},{6,7},{7,6},{8,9},{9,8},{10,11... | collective-permute-start | bytes 4718600 | tf_op jit(solution)/shard_map/ppermute | solution.py:100
  31.5 39.0 %all-gather = f32[16,24,512]{2,1,0:T(8,128)S(1)} all-gather(f32[2,24,512]{2,1,0:T(8,128)S(1)} %pad_maximum_fusion), channel_id=2, replica_groups=mesh['far'=8,'pair'=2,'x'=4,'y'=4,'core'=2] {'far'}, dimensions={0}, use_global_device_ids=true | all-gather | bytes 884736 | tf_op jit(solution)/shard_map/all_gather | solution.py:98
  70.4 4.5 %collective-permute-start = (f32[8,2,24,512]{3,2,1,0:T(8,128)S(1)}, f32[8,2,24,512]{3,2,1,0:T(8,128)S(1)}, u32[]{:S(2)}, u32[]{:S(2)}) collective-permute-start(f32[8,2,24,512]{3,2,1,0:T(8,128)S(1)} %bitcast.32), channel_id=1, source_target_pairs={{0,32},{32,0},{1,33},{33,1},{2,34},{34,2},{3,35},{35,3},{4,36},{36... | collective-permute-start | bytes 2359304 | tf_op jit(solution)/shard_map/ppermute | solution.py:99
  75.8 12.4 %collective-permute-done.line1_ref = f32[8,2,24,512]{3,2,1,0:T(8,128)S(1)} collective-permute-done((f32[8,2,24,512]{3,2,1,0:T(8,128)S(1)}, f32[8,2,24,512]{3,2,1,0:T(8,128)S(1)}, u32[]{:S(2)}, u32[]{:S(2)}) %collective-permute-start) | collective-permute-done | bytes 786464 | tf_op jit(solution)/shard_map/ppermute | solution.py:99
  88.2 7.7 %scores.1 = (f32[2,384,384]{2,1,0:T(8,128)S(1)}, f32[2,384,384]{2,1,0:T(8,128)S(1)}, f32[4,384]{1,0:T(4,128)S(1)}) custom-call(f32[1]{0:T(128)} %bitcast.29.scale_ref, f32[8,2,24,512]{3,2,1,0:T(8,128)S(1)} %bitcast.33, f32[8,2,24,512]{3,2,1,0:T(8,128)S(1)} %collective-permute-done.line1_ref, f32[16,2,24,512]{3,2,1,0:T(8,128)S(1)} %all_to_all.20.near_ref, ...), custom_call_target="tpu_custom_call" | custom-call | tf_op jit(solution)/shard_map/scores/pallas_call | solution.py:104
  96.0 1.0 copy-done
  97.0 1.0 copy-done.2
  98.0 0.7 broadcast_in_dim.10
  98.8 5.7 %all-to-all-start.1 = ((f32[32,16,128]{2,1,0:T(8,128)}), f32[32,16,128]{2,1,0:T(8,128)S(1)}, u32[]{:S(2)}, u32[]{:S(2)}) async-start(f32[32,16,128]{2,1,0:T(8,128)} %broadcast_in_dim.10), calls=%async_computation.1 | async-start | bytes 524288 | tf_op jit(solution)/shard_map/all_to_all | solution.py:18
  104.8 6.7 %all-to-all-done.1 = f32[32,16,128]{2,1,0:T(8,128)S(1)} async-done(((f32[32,16,128]{2,1,0:T(8,128)}), f32[32,16,128]{2,1,0:T(8,128)S(1)}, u32[]{:S(2)}, u32[]{:S(2)}) %all-to-all-start.1) | async-done | bytes 262176 | tf_op jit(solution)/shard_map/all_to_all | solution.py:18
  112.1 0.6 broadcast_in_dim.11
  112.7 7.2 %all-to-all-start.2 = ((f32[16,1,128]{2,1,0:T(1,128)}), f32[16,1,128]{2,1,0:T(1,128)S(1)}, u32[]{:S(2)}, u32[]{:S(2)}) async-start(f32[16,1,128]{2,1,0:T(1,128)} %broadcast_in_dim.11), calls=%async_computation.2 | async-start | bytes 16384 | tf_op jit(solution)/shard_map/all_to_all | solution.py:18
  119.9 12.3 %all-to-all-done.2 = f32[16,1,128]{2,1,0:T(1,128)S(1)} async-done(((f32[16,1,128]{2,1,0:T(1,128)}), f32[16,1,128]{2,1,0:T(1,128)S(1)}, u32[]{:S(2)}, u32[]{:S(2)}) %all-to-all-start.2) | async-done | bytes 8224 | tf_op jit(solution)/shard_map/all_to_all | solution.py:18
  132.7 1.3 copy-done.3
  134.0 1.7 %grads.3 = f32[16,2,24,512]{3,2,1,0:T(8,128)S(1)} custom-call(f32[1]{0:T(128)} %bitcast.31.scale_ref, f32[2,384,384]{2,1,0:T(8,128)S(1)} %copy-done.3, f32[8,2,24,512]{3,2,1,0:T(8,128)S(1)} %bitcast.34, f32[8,2,24,512]{3,2,1,0:T(8,128)S(1)} %collective-permute-done.line1_ref, f32[4,384]{1,0:T(4,128)S(1)} %pad_maximum_fusion.2.line_ref, ...), custom_call_target="tpu_custom_call" | custom-call | tf_op jit(solution)/shard_map/grads/pallas_call | solution.py:139
  135.7 1.9 %collective-permute-start.2 = (f32[16,2,24,512]{3,2,1,0:T(8,128)S(1)}, f32[16,2,24,512]{3,2,1,0:T(8,128)}, u32[]{:S(2)}, u32[]{:S(2)}) collective-permute-start(f32[16,2,24,512]{3,2,1,0:T(8,128)S(1)} %grads.3), channel_id=1, source_target_pairs={{0,1},{1,0},{2,3},{3,2},{4,5},{5,4},{6,7},{7,6},{8,9},{9,8},{10,11... | collective-permute-start | bytes 4718600 | tf_op jit(solution)/shard_map/ppermute | solution.py:149
  138.0 1.3 copy-done.1
  139.2 1.7 %grads.2 = f32[16,2,24,512]{3,2,1,0:T(8,128)S(1)} custom-call(f32[1]{0:T(128)} %bitcast.30.scale_ref, f32[2,384,384]{2,1,0:T(8,128)S(1)} %copy-done.1, f32[8,2,24,512]{3,2,1,0:T(8,128)S(1)} %bitcast.35, f32[8,2,24,512]{3,2,1,0:T(8,128)S(1)} %collective-permute-done.line1_ref, f32[4,384]{1,0:T(4,128)S(1)} %pad_maximum_fusion.2.line_ref, ...), custom_call_target="tpu_custom_call" | custom-call | tf_op jit(solution)/shard_map/grads/pallas_call | solution.py:139
  140.9 0.2 collective-permute-done.2
  141.2 1.8 %add.183 = f32[16,2,24,512]{3,2,1,0:T(8,128)S(1)} add(f32[16,2,24,512]{3,2,1,0:T(8,128)S(1)} %grads.2, f32[16,2,24,512]{3,2,1,0:T(8,128)} %collective-permute-done.2) | non-fusion elementwise | flops 393216 | bytes 4718592 | tf_op jit(solution)/shard_map/add | solution.py:150
  143.0 26.4 %all_to_all.21 = f32[16,2,24,512]{3,2,1,0:T(8,128)S(1)} all-to-all(f32[16,2,24,512]{3,2,1,0:T(8,128)S(1)} %add.183), channel_id=1, replica_groups=mesh['far'=8,'pair'=2,'x'=4,'y'=4,'core'=2] {'x','y'}, dimensions={0} | all-to-all | bytes 3145728 | tf_op jit(solution)/shard_map/all_to_all | solution.py:151
  169.5 0.6 slice_bitcast_fusion
  (49 shorter events, 2.1 us)
Async XLA Ops:
  1.6 74.0 %copy-start.4 = (s32[24]{0:T(128)S(1)}, s32[24]{0:T(128)}, u32[]{:S(2)}) copy-start(s32[24]{0:T(128)} %param.7) | copy-start | bytes 292
  29.6 58.7 %collective-permute-start.1 = (f32[16,2,24,512]{3,2,1,0:T(8,128)S(1)}, f32[16,2,24,512]{3,2,1,0:T(8,128)}, u32[]{:S(2)}, u32[]{:S(2)}) collective-permute-start(f32[16,2,24,512]{3,2,1,0:T(8,128)S(1)} %all_to_all.20.near_ref), channel_id=1, source_target_pairs={{0,1},{1,0},{2,3},{3,2},{4,5},{5,4},{6,7},{7,6},{8,9},{9,8},{10,11... | collective-permute-start | bytes 4718600 | tf_op jit(solution)/shard_map/ppermute | solution.py:100
  70.4 17.8 %collective-permute-start = (f32[8,2,24,512]{3,2,1,0:T(8,128)S(1)}, f32[8,2,24,512]{3,2,1,0:T(8,128)S(1)}, u32[]{:S(2)}, u32[]{:S(2)}) collective-permute-start(f32[8,2,24,512]{3,2,1,0:T(8,128)S(1)} %bitcast.32), channel_id=1, source_target_pairs={{0,32},{32,0},{1,33},{33,1},{2,34},{34,2},{3,35},{35,3},{4,36},{36... | collective-permute-start | bytes 2359304 | tf_op jit(solution)/shard_map/ppermute | solution.py:99
  96.0 1.0 copy-start
  97.0 1.0 copy-start.2
  98.8 12.7 %all-to-all-start.1 = ((f32[32,16,128]{2,1,0:T(8,128)}), f32[32,16,128]{2,1,0:T(8,128)S(1)}, u32[]{:S(2)}, u32[]{:S(2)}) async-start(f32[32,16,128]{2,1,0:T(8,128)} %broadcast_in_dim.10), calls=%async_computation.1 | async-start | bytes 524288 | tf_op jit(solution)/shard_map/all_to_all | solution.py:18
  112.7 19.5 %all-to-all-start.2 = ((f32[16,1,128]{2,1,0:T(1,128)}), f32[16,1,128]{2,1,0:T(1,128)S(1)}, u32[]{:S(2)}, u32[]{:S(2)}) async-start(f32[16,1,128]{2,1,0:T(1,128)} %broadcast_in_dim.11), calls=%async_computation.2 | async-start | bytes 16384 | tf_op jit(solution)/shard_map/all_to_all | solution.py:18
  132.7 1.3 copy-start.3
  135.7 5.4 %collective-permute-start.2 = (f32[16,2,24,512]{3,2,1,0:T(8,128)S(1)}, f32[16,2,24,512]{3,2,1,0:T(8,128)}, u32[]{:S(2)}, u32[]{:S(2)}) collective-permute-start(f32[16,2,24,512]{3,2,1,0:T(8,128)S(1)} %grads.3), channel_id=1, source_target_pairs={{0,1},{1,0},{2,3},{3,2},{4,5},{5,4},{6,7},{7,6},{8,9},{9,8},{10,11... | collective-permute-start | bytes 4718600 | tf_op jit(solution)/shard_map/ppermute | solution.py:149
  137.9 1.3 copy-start.1

commit v6 on v3

--- a/solution.py
+++ b/solution.py
@@ -34,9 +34,7 @@
 def local(row_embed, col_embed, logit_scale, targets):
     own, width = row_embed.shape
     plane, across, along, core = (lax.axis_index(a) for a in ALL)
-    other = shift(col_embed, "core", CORE, 1)
-    pair = jnp.where(core == 0, jnp.concatenate([col_embed, other]), jnp.concatenate([other, col_embed]))
-    cols = to_all(pair, ("x", "y"), SIDE * SIDE).reshape(SIDE * SIDE * CORE * own, width)
+    cols = to_all(col_embed, ("x", "y", "core"), SIDE * SIDE * CORE).reshape(SIDE * SIDE * CORE * own, width)
     rows = lax.all_gather(row_embed, "z", axis=0, tiled=True)
     row_count, col_count = rows.shape[0], cols.shape[0]
 
@@ -52,12 +50,11 @@
     row_message = jnp.concatenate(
         [row_top, row_total, targets.astype(jnp.float32), jnp.zeros((1024 - 2 * row_count - own,), jnp.float32)]
     ).reshape(8, 128)
+    col_message = jnp.concatenate([col_top, col_total]).reshape(12, 128)
+    col_stats = to_all(col_message, ("x", "y", "core"), SIDE * SIDE * CORE)
+    col_stats, row_message = lax.optimization_barrier((col_stats, row_message))
     row_stats = to_all(row_message, "z", Z).reshape(Z, 1024)
-    col_message = jnp.concatenate([col_top, col_total]).reshape(12, 128)
-    col_stats = lax.all_gather(col_message, "x", axis=0).reshape(SIDE, 2, col_count)
-    col_message = jnp.concatenate(combine(col_stats[:, 0], col_stats[:, 1])).reshape(12, 128)
-    row_stats, col_message = lax.optimization_barrier((row_stats, col_message))
-    col_stats = to_all(col_message, ("y", "core"), SIDE * CORE).reshape(SIDE * CORE, 2, col_count)
+    col_stats = col_stats.reshape(SIDE * SIDE * CORE, 2, col_count)
     col_top, col_total = combine(col_stats[:, 0], col_stats[:, 1])
     row_top, row_total = combine(row_stats[:, :row_count], row_stats[:, row_count:2 * row_count])
     row_targets = row_stats[:, 2 * row_count:2 * row_count + own].reshape(row_count).astype(jnp.int32)

time: 146 us -> 142 us (0.973); the launches traced: 145 us -> 140 us
  blocking collectives: 50 us -> 38.1 us
  waiting for transfers between devices: 24.5 us -> 34.5 us
  starting transfers between devices: 53.5 us -> 48.7 us
  local copies, waits for them, and re-layouts: 3.9 us -> 5.44 us
    all_to_all x3, waiting for transfers between devices: 6.32 us -> 20 us  [to_all(): return lax.all_to_all(sent, axes, 0, 0, tiled=True)]
    all_gather x1 -> x0, blocking collectives: 11.9 us -> none  [local(): lax.all_gather(col_message, 'x', axis=0).reshape(SIDE, 2, col_count)]
    all_to_all x1, starting transfers between devices: 11.3 us -> 4.29 us  [local(): lax.all_to_all(grad_rows.reshape(Z, own, width), 'z', 0, 0, tiled=True)]
    all_to_all x3, starting transfers between devices: 20.5 us -> 23.9 us  [to_all(): return lax.all_to_all(sent, axes, 0, 0, tiled=True)]
    all_to_all x1, waiting for transfers between devices: 3.19 us -> 0.43 us  [local(): lax.all_to_all(grad_rows.reshape(Z, own, width), 'z', 0, 0, tiled=True)]
    ppermute x8 -> x7, starting transfers between devices: 21.8 us -> 20.5 us  [shift(): lax.ppermute(block, axis, [(i, (i + by) % count) for i in range(count)])]
    ppermute x8 -> x7, waiting for transfers between devices: 15 us -> 14.2 us  [shift(): lax.ppermute(block, axis, [(i, (i + by) % count) for i in range(count)])]
  transfers between devices with their start and end apart: 12 -> 11, of which waited for: 9 -> 8; matrix products, arithmetic and copies ran while one was open for 2% -> 2% of each run, Pallas kernels for 0% -> 0%
where the time goes in v6:
time: 142 us; the launch traced here: 140 us
  starting transfers between devices  48.7 us (34%)
  blocking collectives  38.1 us (27%)
  waiting for transfers between devices  34.5 us (24%)
  other arithmetic  5.84 us (4%)
  matrix products  5.74 us (4%)
  local copies, waits for them, and re-layouts  5.44 us (4%)
  between operations  1.66 us (1%)
    all_gather x1, blocking collectives, local(): rows = lax.all_gather(row_embed, 'z', axis=0, tiled=True)  38.1 us
    all_to_all x3, starting transfers between devices, to_all(): return lax.all_to_all(sent, axes, 0, 0, tiled=True)  23.9 us
    ppermute x7, starting transfers between devices, shift(): lax.ppermute(block, axis, [(i, (i + by) % count) for i in range(count)])  20.5 us
    all_to_all x3, waiting for transfers between devices, to_all(): return lax.all_to_all(sent, axes, 0, 0, tiled=True)  20 us
    ppermute x7, waiting for transfers between devices, shift(): lax.ppermute(block, axis, [(i, (i + by) % count) for i in range(count)])  14.2 us
    all_to_all x1, starting transfers between devices, local(): lax.all_to_all(grad_rows.reshape(Z, own, width), 'z', 0, 0, tiled=True)  4.29 us
    broadcast_in_dim x3, local copies, waits for them, and re-layouts, to_all(): sent = jnp.broadcast_to(block[None], (count,) + block.shape)  3.49 us
  transfers between devices with their start and end apart: 11, of which 8 were waited for; matrix products, arithmetic and copies ran while one was open for 2% of the time, Pallas kernels for 0%

profile of v6, /device:TPU:6, one launch (start us, length us, event | category | flops | bytes accessed | tf_op | source)
XLA Modules:
  0.0 139.9 jit_solution(2662515411901058913)
XLA Ops:
  0.6 2.1 %broadcast_in_dim.8 = f32[32,24,512]{2,1,0:T(8,128)} broadcast(f32[24,512]{1,0:T(8,128)} %param.5), dimensions={1,2} | broadcast | bytes 1622016 | tf_op jit(solution)/shard_map/broadcast_in_dim | solution.py:11
  2.8 9.8 %all-to-all-start = ((f32[32,24,512]{2,1,0:T(8,128)}), f32[32,24,512]{2,1,0:T(8,128)S(1)}, u32[]{:S(2)}, u32[]{:S(2)}) async-start(f32[32,24,512]{2,1,0:T(8,128)} %broadcast_in_dim.8), calls=%async_computation | async-start | bytes 3145728 | tf_op jit(solution)/shard_map/all_to_all | solution.py:12
  13.2 38.1 %all_gather.3 = f32[384,512]{1,0:T(8,128)S(1)} all-gather(f32[24,512]{1,0:T(8,128)S(1)} %copy-done.1), channel_id=1, replica_groups=mesh['z'=16,'x'=4,'y'=4,'core'=2] {'z'}, dimensions={0}, use_global_device_ids=true | all-gather | bytes 835584 | tf_op jit(solution)/shard_map/all_gather | solution.py:38
  51.3 2.2 %fusion.10 = (f32[384]{0:T(512)S(1)}, f32[768]{0:T(1024)S(1)}, f32[384,768]{1,0:T(8,128)S(1)}) fusion(f32[384,512]{1,0:T(8,128)S(1)} %all_gather.3, f32[768,512]{1,0:T(8,128)S(1)} %bitcast.61, f32[]{:T(128)S(6)} %copy.25), kind=kOutput, calls=%fused_computation.36 | convolution fusion | flops 1812822912 | bytes 3543556 | tf_op jit(solution)/shard_map/dot_general | solution.py:41
  55.7 7.3 %all-to-all-start.1 = ((f32[32,12,128]{2,1,0:T(8,128)}), f32[32,12,128]{2,1,0:T(8,128)S(1)}, u32[]{:S(2)}, u32[]{:S(2)}) async-start(f32[32,12,128]{2,1,0:T(8,128)} %broadcast_in_dim.9), calls=%async_computation.1 | async-start | bytes 524288 | tf_op jit(solution)/shard_map/all_to_all | solution.py:12
  63.1 6.9 %all-to-all-done.1 = f32[32,12,128]{2,1,0:T(8,128)S(1)} async-done(((f32[32,12,128]{2,1,0:T(8,128)}), f32[32,12,128]{2,1,0:T(8,128)S(1)}, u32[]{:S(2)}, u32[]{:S(2)}) %all-to-all-start.1) | async-done | bytes 196640 | tf_op jit(solution)/shard_map/all_to_all | solution.py:12
  70.9 6.8 %all-to-all-start.2 = ((f32[16,8,128]{2,1,0:T(8,128)}), f32[16,8,128]{2,1,0:T(8,128)S(1)}, u32[]{:S(2)}, u32[]{:S(2)}) async-start(f32[16,8,128]{2,1,0:T(8,128)} %broadcast_in_dim.11), calls=%async_computation.2 | async-start | bytes 131072 | tf_op jit(solution)/shard_map/all_to_all | solution.py:12
  77.8 13.1 %all-to-all-done.2 = f32[16,8,128]{2,1,0:T(8,128)S(1)} async-done(((f32[16,8,128]{2,1,0:T(8,128)}), f32[16,8,128]{2,1,0:T(8,128)S(1)}, u32[]{:S(2)}, u32[]{:S(2)}) %all-to-all-start.2) | async-done | bytes 65568 | tf_op jit(solution)/shard_map/all_to_all | solution.py:12
  92.2 1.8 %convert_subtract_fusion = f32[384,768]{1,0:T(8,128)S(1)} fusion(f32[384,768]{1,0:T(8,128)} %copy-done, s32[768]{0:T(1024)S(1)} %iota_add_fusion, f32[768]{0:T(1024)S(1)} %broadcast_divide_fusion, f32[768]{0:T(1024)S(1)} %get-tuple-element.16, f32[384]{0:T(512)} %broadcast_divide_fusion.1, f32[384]{0:T(512)S(1)} %slice_reduce_fusion, s32[384]{0:T(512)} %convert_element_type.18), kind=kLoop, calls=%fused_computation.1 | loop fusion | flops 2359296 | bytes 2373120 | tf_op jit(solution)/shard_map/sub | solution.py:64
  94.0 2.1 %fusion.11 = f32[16,24,512]{2,1,0:T(8,128)} fusion(f32[16,24,768]{2,1,0:T(8,128)S(1)} %bitcast.63, f32[768,512,1]{1,0,2:T(8,128)S(1)} %bitcast.62), kind=kOutput, calls=%fused_computation.37 | convolution fusion | flops 905969664 | bytes 3538944 | tf_op jit(solution)/shard_map/dot_general | solution.py:68
  96.1 4.3 %all-to-all-start.3 = ((f32[16,24,512]{2,1,0:T(8,128)}), f32[16,24,512]{2,1,0:T(8,128)}, u32[]{:S(2)}, u32[]{:S(2)}) async-start(f32[16,24,512]{2,1,0:T(8,128)} %fusion.11), calls=%async_computation.3 | async-start | bytes 1572864 | tf_op jit(solution)/shard_map/all_to_all | solution.py:72
  100.4 1.4 %fusion.12 = f32[768,512]{1,0:T(8,128)S(1)} fusion(f32[384,768]{1,0:T(8,128)S(1)} %convert_subtract_fusion, f32[384,512]{1,0:T(8,128)S(1)} %all_gather.3), kind=kOutput, calls=%fused_computation.38 | convolution fusion | flops 905969664 | bytes 3538944 | tf_op jit(solution)/shard_map/dot_general | solution.py:73
  101.9 1.9 %collective-permute-start = (f32[4,4,24,512]{3,2,1,0:T(8,128)S(1)}, f32[4,4,24,512]{3,2,1,0:T(8,128)S(1)}, u32[]{:S(2)}, u32[]{:S(2)}) collective-permute-start(f32[4,4,24,512]{3,2,1,0:T(8,128)S(1)} %dynamic-slice_bitcast_fusion), channel_id=1, source_target_pairs={{0,1},{1,0},{2,3},{3,2},{4,5},{5,4},{6,7},{7,6},{8,9},{9,8},{10,11... | collective-permute-start | bytes 2359304 | tf_op jit(solution)/shard_map/ppermute | solution.py:16
  103.9 2.2 %collective-permute-done = f32[4,4,24,512]{3,2,1,0:T(8,128)S(1)} collective-permute-done((f32[4,4,24,512]{3,2,1,0:T(8,128)S(1)}, f32[4,4,24,512]{3,2,1,0:T(8,128)S(1)}, u32[]{:S(2)}, u32[]{:S(2)}) %collective-permute-start) | collective-permute-done | bytes 786464 | tf_op jit(solution)/shard_map/ppermute | solution.py:16
  106.3 2.2 %collective-permute-start.3 = (f32[4,24,512]{2,1,0:T(8,128)S(1)}, f32[4,24,512]{2,1,0:T(8,128)S(1)}, u32[]{:S(2)}, u32[]{:S(2)}) collective-permute-start(f32[4,24,512]{2,1,0:T(8,128)S(1)} %get-tuple-element.11), channel_id=1, source_target_pairs={{0,2},{2,4},{4,6},{6,0},{1,3},{3,5},{5,7},{7,1},{8,10},{10,12},{12... | collective-permute-start | bytes 589832 | tf_op jit(solution)/shard_map/ppermute | solution.py:16
  108.5 4.5 %collective-permute-start.2 = (f32[4,24,512]{2,1,0:T(8,128)S(1)}, f32[4,24,512]{2,1,0:T(8,128)S(1)}, u32[]{:S(2)}, u32[]{:S(2)}) collective-permute-start(f32[4,24,512]{2,1,0:T(8,128)S(1)} %get-tuple-element.12), channel_id=1, source_target_pairs={{0,4},{2,6},{4,0},{6,2},{1,5},{3,7},{5,1},{7,3},{8,12},{10,14},{12... | collective-permute-start | bytes 589832 | tf_op jit(solution)/shard_map/ppermute | solution.py:16
  113.0 2.6 %collective-permute-start.1 = (f32[4,24,512]{2,1,0:T(8,128)S(1)}, f32[4,24,512]{2,1,0:T(8,128)S(1)}, u32[]{:S(2)}, u32[]{:S(2)}) collective-permute-start(f32[4,24,512]{2,1,0:T(8,128)S(1)} %get-tuple-element.10), channel_id=1, source_target_pairs={{0,6},{2,0},{4,2},{6,4},{1,7},{3,1},{5,3},{7,5},{8,14},{10,8},{12,... | collective-permute-start | bytes 589832 | tf_op jit(solution)/shard_map/ppermute | solution.py:16
  115.7 4.9 %collective-permute-done.3 = f32[4,24,512]{2,1,0:T(8,128)S(1)} collective-permute-done((f32[4,24,512]{2,1,0:T(8,128)S(1)}, f32[4,24,512]{2,1,0:T(8,128)S(1)}, u32[]{:S(2)}, u32[]{:S(2)}) %collective-permute-start.3) | collective-permute-done | bytes 196640 | tf_op jit(solution)/shard_map/ppermute | solution.py:16
  120.5 2.5 %collective-permute-done.1 = f32[4,24,512]{2,1,0:T(8,128)S(1)} collective-permute-done((f32[4,24,512]{2,1,0:T(8,128)S(1)}, f32[4,24,512]{2,1,0:T(8,128)S(1)}, u32[]{:S(2)}, u32[]{:S(2)}) %collective-permute-start.1) | collective-permute-done | bytes 196640 | tf_op jit(solution)/shard_map/ppermute | solution.py:16
  123.1 4.0 %collective-permute-start.6 = (f32[24,512]{1,0:T(8,128)S(1)}, f32[24,512]{1,0:T(8,128)S(1)}, u32[]{:S(2)}, u32[]{:S(2)}) collective-permute-start(f32[24,512]{1,0:T(8,128)S(1)} %get-tuple-element.14), channel_id=1, source_target_pairs={{0,8},{8,16},{16,24},{24,0},{1,9},{9,17},{17,25},{25,1},{2,10},{10... | collective-permute-start | bytes 147464 | tf_op jit(solution)/shard_map/ppermute | solution.py:16
  127.2 2.7 %collective-permute-start.5 = (f32[24,512]{1,0:T(8,128)S(1)}, f32[24,512]{1,0:T(8,128)S(1)}, u32[]{:S(2)}, u32[]{:S(2)}) collective-permute-start(f32[24,512]{1,0:T(8,128)S(1)} %get-tuple-element.15), channel_id=1, source_target_pairs={{0,16},{8,24},{16,0},{24,8},{1,17},{9,25},{17,1},{25,9},{2,18},{10... | collective-permute-start | bytes 147464 | tf_op jit(solution)/shard_map/ppermute | solution.py:16
  129.8 2.6 %collective-permute-start.4 = (f32[24,512]{1,0:T(8,128)S(1)}, f32[24,512]{1,0:T(8,128)S(1)}, u32[]{:S(2)}, u32[]{:S(2)}) collective-permute-start(f32[24,512]{1,0:T(8,128)S(1)} %get-tuple-element.13), channel_id=1, source_target_pairs={{0,24},{8,0},{16,8},{24,16},{1,25},{9,1},{17,9},{25,17},{2,26},{10... | collective-permute-start | bytes 147464 | tf_op jit(solution)/shard_map/ppermute | solution.py:16
  132.5 2.7 %collective-permute-done.5 = f32[24,512]{1,0:T(8,128)S(1)} collective-permute-done((f32[24,512]{1,0:T(8,128)S(1)}, f32[24,512]{1,0:T(8,128)S(1)}, u32[]{:S(2)}, u32[]{:S(2)}) %collective-permute-start.5) | collective-permute-done | bytes 49184 | tf_op jit(solution)/shard_map/ppermute | solution.py:16
  135.2 1.9 %collective-permute-done.4 = f32[24,512]{1,0:T(8,128)S(1)} collective-permute-done((f32[24,512]{1,0:T(8,128)S(1)}, f32[24,512]{1,0:T(8,128)S(1)}, u32[]{:S(2)}, u32[]{:S(2)}) %collective-permute-start.4) | collective-permute-done | bytes 49184 | tf_op jit(solution)/shard_map/ppermute | solution.py:16
  (36 shorter events, 7.8 us)
Async XLA Ops:
  2.8 10.4 %copy-start.2 = (s32[24]{0:T(128)S(1)}, s32[24]{0:T(128)}, u32[]{:S(2)}) copy-start(s32[24]{0:T(128)} %param.7) | copy-start | bytes 292
  2.8 10.5 %copy-start.1 = (f32[24,512]{1,0:T(8,128)S(1)}, f32[24,512]{1,0:T(8,128)}, u32[]{:S(2)}) copy-start(f32[24,512]{1,0:T(8,128)} %param.4) | copy-start | bytes 147460
  2.8 48.5 %all-to-all-start = ((f32[32,24,512]{2,1,0:T(8,128)}), f32[32,24,512]{2,1,0:T(8,128)S(1)}, u32[]{:S(2)}, u32[]{:S(2)}) async-start(f32[32,24,512]{2,1,0:T(8,128)} %broadcast_in_dim.8), calls=%async_computation | async-start | bytes 3145728 | tf_op jit(solution)/shard_map/all_to_all | solution.py:12
  53.5 1.0 copy-start
  55.7 14.4 %all-to-all-start.1 = ((f32[32,12,128]{2,1,0:T(8,128)}), f32[32,12,128]{2,1,0:T(8,128)S(1)}, u32[]{:S(2)}, u32[]{:S(2)}) async-start(f32[32,12,128]{2,1,0:T(8,128)} %broadcast_in_dim.9), calls=%async_computation.1 | async-start | bytes 524288 | tf_op jit(solution)/shard_map/all_to_all | solution.py:12
  70.9 19.9 %all-to-all-start.2 = ((f32[16,8,128]{2,1,0:T(8,128)}), f32[16,8,128]{2,1,0:T(8,128)S(1)}, u32[]{:S(2)}, u32[]{:S(2)}) async-start(f32[16,8,128]{2,1,0:T(8,128)} %broadcast_in_dim.11), calls=%async_computation.2 | async-start | bytes 131072 | tf_op jit(solution)/shard_map/all_to_all | solution.py:12
  96.1 42.0 %all-to-all-start.3 = ((f32[16,24,512]{2,1,0:T(8,128)}), f32[16,24,512]{2,1,0:T(8,128)}, u32[]{:S(2)}, u32[]{:S(2)}) async-start(f32[16,24,512]{2,1,0:T(8,128)} %fusion.11), calls=%async_computation.3 | async-start | bytes 1572864 | tf_op jit(solution)/shard_map/all_to_all | solution.py:72
  101.9 4.2 %collective-permute-start = (f32[4,4,24,512]{3,2,1,0:T(8,128)S(1)}, f32[4,4,24,512]{3,2,1,0:T(8,128)S(1)}, u32[]{:S(2)}, u32[]{:S(2)}) collective-permute-start(f32[4,4,24,512]{3,2,1,0:T(8,128)S(1)} %dynamic-slice_bitcast_fusion), channel_id=1, source_target_pairs={{0,1},{1,0},{2,3},{3,2},{4,5},{5,4},{6,7},{7,6},{8,9},{9,8},{10,11... | collective-permute-start | bytes 2359304 | tf_op jit(solution)/shard_map/ppermute | solution.py:16
  106.3 14.3 %collective-permute-start.3 = (f32[4,24,512]{2,1,0:T(8,128)S(1)}, f32[4,24,512]{2,1,0:T(8,128)S(1)}, u32[]{:S(2)}, u32[]{:S(2)}) collective-permute-start(f32[4,24,512]{2,1,0:T(8,128)S(1)} %get-tuple-element.11), channel_id=1, source_target_pairs={{0,2},{2,4},{4,6},{6,0},{1,3},{3,5},{5,7},{7,1},{8,10},{10,12},{12... | collective-permute-start | bytes 589832 | tf_op jit(solution)/shard_map/ppermute | solution.py:16
  108.5 12.1 %collective-permute-start.2 = (f32[4,24,512]{2,1,0:T(8,128)S(1)}, f32[4,24,512]{2,1,0:T(8,128)S(1)}, u32[]{:S(2)}, u32[]{:S(2)}) collective-permute-start(f32[4,24,512]{2,1,0:T(8,128)S(1)} %get-tuple-element.12), channel_id=1, source_target_pairs={{0,4},{2,6},{4,0},{6,2},{1,5},{3,7},{5,1},{7,3},{8,12},{10,14},{12... | collective-permute-start | bytes 589832 | tf_op jit(solution)/shard_map/ppermute | solution.py:16
  113.0 10.0 %collective-permute-start.1 = (f32[4,24,512]{2,1,0:T(8,128)S(1)}, f32[4,24,512]{2,1,0:T(8,128)S(1)}, u32[]{:S(2)}, u32[]{:S(2)}) collective-permute-start(f32[4,24,512]{2,1,0:T(8,128)S(1)} %get-tuple-element.10), channel_id=1, source_target_pairs={{0,6},{2,0},{4,2},{6,4},{1,7},{3,1},{5,3},{7,5},{8,14},{10,8},{12,... | collective-permute-start | bytes 589832 | tf_op jit(solution)/shard_map/ppermute | solution.py:16
  123.1 9.3 %collective-permute-start.6 = (f32[24,512]{1,0:T(8,128)S(1)}, f32[24,512]{1,0:T(8,128)S(1)}, u32[]{:S(2)}, u32[]{:S(2)}) collective-permute-start(f32[24,512]{1,0:T(8,128)S(1)} %get-tuple-element.14), channel_id=1, source_target_pairs={{0,8},{8,16},{16,24},{24,0},{1,9},{9,17},{17,25},{25,1},{2,10},{10... | collective-permute-start | bytes 147464 | tf_op jit(solution)/shard_map/ppermute | solution.py:16
  127.2 8.0 %collective-permute-start.5 = (f32[24,512]{1,0:T(8,128)S(1)}, f32[24,512]{1,0:T(8,128)S(1)}, u32[]{:S(2)}, u32[]{:S(2)}) collective-permute-start(f32[24,512]{1,0:T(8,128)S(1)} %get-tuple-element.15), channel_id=1, source_target_pairs={{0,16},{8,24},{16,0},{24,8},{1,17},{9,25},{17,1},{25,9},{2,18},{10... | collective-permute-start | bytes 147464 | tf_op jit(solution)/shard_map/ppermute | solution.py:16
  129.8 7.2 %collective-permute-start.4 = (f32[24,512]{1,0:T(8,128)S(1)}, f32[24,512]{1,0:T(8,128)S(1)}, u32[]{:S(2)}, u32[]{:S(2)}) collective-permute-start(f32[24,512]{1,0:T(8,128)S(1)} %get-tuple-element.13), channel_id=1, source_target_pairs={{0,24},{8,0},{16,8},{24,16},{1,25},{9,1},{17,9},{25,17},{2,26},{10... | collective-permute-start | bytes 147464 | tf_op jit(solution)/shard_map/ppermute | solution.py:16

commit v7 on v6

v7 whole, which is shorter than its diff:
```python
import jax
import jax.numpy as jnp
from jax import lax
from jax.experimental import pallas as pl
from jax.experimental.pallas import tpu as pltpu
from jax.sharding import Mesh, PartitionSpec as P

ALL = ("z", "x", "y", "core")
Z, SIDE, CORE = 16, 4, 2
PLANE = SIDE * SIDE * CORE
LANES = 128
SMEM = pl.BlockSpec(memory_space=pltpu.SMEM)
VMEM = pl.BlockSpec(memory_space=pltpu.VMEM)
PARAMS = pltpu.CompilerParams(vmem_limit_bytes=48 * 1024 * 1024)


def to_all(block, axes, count):
    sent = jnp.broadcast_to(block[None], (count,) + block.shape)
    return lax.all_to_all(sent, axes, 0, 0, tiled=True)


def shift(block, axis, count, by):
    return lax.ppermute(block, axis, [(i, (i + by) % count) for i in range(count)])


def home(parts, axis, count, dim, me):
    def part(by):
        return lax.dynamic_index_in_dim(parts, (me - by + count) % count, dim, keepdims=False)

    total = part(0)
    for by in range(1, count):
        total = total + shift(part(by), axis, count, -by)
    return total


def score_kernel(scale_ref, row_ref, col_ref, target_ref, score_out, col_out, row_out):
    scores = scale_ref[0] * lax.dot_general(
        row_ref[...], col_ref[...], (((1,), (1,)), ((), ())),
        precision=lax.Precision.HIGHEST, preferred_element_type=jnp.float32,
    )
    score_out[...] = scores
    top = jnp.max(scores, axis=0, keepdims=True)
    lse = top + jnp.log(jnp.sum(jnp.exp(scores - top), axis=0, keepdims=True))
    used = lse.shape[1] // LANES
    for k in range(used):
        col_out[:, k, :] = jnp.broadcast_to(lse[:, k * LANES:(k + 1) * LANES], (col_out.shape[0], LANES))
    col_out[:, used:, :] = jnp.zeros_like(col_out[:, used:, :])
    used = score_out.shape[0] // LANES
    for k in range(used):
        part = scores[k * LANES:(k + 1) * LANES]
        top = jnp.max(part, axis=1, keepdims=True)
        lse = top + jnp.log(jnp.sum(jnp.exp(part - top), axis=1, keepdims=True))
        lse = jnp.transpose(jnp.broadcast_to(lse, (LANES, LANES)))[:1]
        row_out[:, k, :] = jnp.broadcast_to(lse, (row_out.shape[0], LANES))
    row_out[:, used, :] = jnp.broadcast_to(target_ref[...], (row_out.shape[0], LANES))
    row_out[:, used + 1:, :] = jnp.zeros_like(row_out[:, used + 1:, :])


def split(values):
    high = values.astype(jnp.bfloat16)
    return high, (values - high.astype(jnp.float32)).astype(jnp.bfloat16)


def combined(heard):
    top = jnp.max(heard, axis=0)
    return top + jnp.log(jnp.sum(jnp.exp(heard - top[None]), axis=0))


def weight_kernel(scale_ref, base_ref, score_ref, col_ref, heard_col_ref, heard_row_ref, weight_out, grad_out):
    row_count, col_count = score_ref.shape
    own = grad_out.shape[1]
    col_lse = combined(heard_col_ref[...])
    col_lse = jnp.concatenate([col_lse[k:k + 1] for k in range(col_count // LANES)], axis=1)
    row_lse = combined(heard_row_ref[...])
    row_lse = jnp.concatenate(
        [jnp.transpose(jnp.broadcast_to(row_lse[k:k + 1], (LANES, LANES))) for k in range(row_count // LANES)], axis=0
    )[:, :1]
    targets = jnp.transpose(
        jnp.concatenate([heard_row_ref[:, row_count // LANES, :], jnp.zeros((LANES - Z, LANES), jnp.float32)], axis=0)
    )
    ids = lax.broadcasted_iota(jnp.int32, (own, col_count), 1).astype(jnp.float32)
    base = base_ref[0]
    for z in range(Z):
        here = slice(z * own, (z + 1) * own)
        scores = score_ref[here, :]
        weight_out[here, :] = (
            0.5 * jnp.exp(scores - row_lse[here])
            + 0.5 * jnp.exp(scores - col_lse)
            - jnp.where(targets[:own, z:z + 1] - base == ids, 1.0, 0.0)
        )
    high, low = split(weight_out[...])
    col_high, col_low = split(col_ref[...])
    total = None
    for left, right in ((high, col_high), (high, col_low), (low, col_high)):
        term = jnp.dot(left, right, preferred_element_type=jnp.float32)
        total = term if total is None else total + term
    grad_out[...] = (scale_ref[0] * total).reshape(grad_out.shape)


def local(row_embed, col_embed, logit_scale, targets):
    own, width = row_embed.shape
    plane, across, along, core = (lax.axis_index(a) for a in ALL)
    scale = logit_scale.reshape(1)
    cols = to_all(col_embed, ("x", "y", "core"), PLANE).reshape(PLANE * own, width)
    rows = lax.all_gather(row_embed, "z", axis=0, tiled=True)
    row_count, col_count = rows.shape[0], cols.shape[0]

    numbers = jnp.pad(targets.astype(jnp.float32), (0, LANES - own)).reshape(1, LANES)
    scores, col_message, row_message = pl.pallas_call(
        score_kernel,
        out_shape=(
            jax.ShapeDtypeStruct((row_count, col_count), jnp.float32),
            jax.ShapeDtypeStruct((PLANE, 8, LANES), jnp.float32),
            jax.ShapeDtypeStruct((Z, 8, LANES), jnp.float32),
        ),
        in_specs=[SMEM, VMEM, VMEM, VMEM],
        out_specs=(VMEM, VMEM, VMEM),
        compiler_params=PARAMS,
        name="scores",
    )(scale, rows, cols, numbers)

    heard_col = lax.all_to_all(col_message, ("x", "y", "core"), 0, 0, tiled=True)
    heard_col, row_message = lax.optimization_barrier((heard_col, row_message))
    heard_row = lax.all_to_all(row_message, "z", 0, 0, tiled=True)

    weights, grad_rows = pl.pallas_call(
        weight_kernel,
        out_shape=(
            jax.ShapeDtypeStruct((row_count, col_count), jnp.float32),
            jax.ShapeDtypeStruct((Z, own, width), jnp.float32),
        ),
        in_specs=[SMEM, SMEM, VMEM, VMEM, VMEM, VMEM],
        out_specs=(VMEM, VMEM),
        compiler_params=PARAMS,
        name="weights",
    )(scale, (plane * col_count).astype(jnp.float32).reshape(1), scores, cols, heard_col, heard_row)
    row_parts = lax.all_to_all(grad_rows, "z", 0, 0, tiled=True)
    grad_cols = lax.dot_general(
        weights, rows, (((0,), (0,)), ((), ())),
        precision=lax.Precision.HIGH, preferred_element_type=jnp.float32,
    ).reshape(SIDE, SIDE, CORE, own, width)
    col_sum = home(grad_cols, "core", CORE, 2, core)
    col_sum = home(col_sum, "y", SIDE, 1, along)
    col_sum = home(col_sum, "x", SIDE, 0, across)
    return jnp.sum(row_parts, axis=0), logit_scale * col_sum


def solution(mesh):
    grid = Mesh(mesh.devices.reshape(Z, SIDE, SIDE, CORE), ALL)
    placed = P(ALL, None)
    return jax.shard_map(
        local, mesh=grid, in_specs=(placed, placed, P(), P(ALL)), out_specs=(placed, placed), check_vma=False
    )
```

time: 142 us -> 141 us (level)
  blocking collectives: 38.1 us -> 51.2 us
  starting transfers between devices: 48.7 us -> 41.3 us
  waiting for transfers between devices: 34.5 us -> 27.4 us
  Pallas kernels: 0 us -> 4.92 us
  matrix products: 5.74 us -> 1.43 us
  other arithmetic: 5.84 us -> 2.65 us
  local copies, waits for them, and re-layouts: 5.44 us -> 7.88 us
    all_to_all x3 -> x1, waiting for transfers between devices: 20 us -> 0.01 us  [to_all(): return lax.all_to_all(sent, axes, 0, 0, tiled=True)]
    all_to_all x3 -> x1, starting transfers between devices: 23.9 us -> 9.76 us  [to_all(): return lax.all_to_all(sent, axes, 0, 0, tiled=True)]
    all_to_all x0 -> x1, blocking collectives: none -> 13.2 us  [local(): lax.all_to_all(col_message, ('x', 'y', 'core'), 0, 0, tiled=True)]
    all_to_all x1 -> x2, waiting for transfers between devices: 0.43 us -> 13.4 us  [the longest x1 13 us: local(): heard_row = lax.all_to_all(row_message, 'z', 0, 0, tiled=True)]
    all_to_all x1 -> x2, starting transfers between devices: 4.29 us -> 11 us  [the longest x1 6.76 us: local(): heard_row = lax.all_to_all(row_message, 'z', 0, 0, tiled=True)]
    pallas_call x0 -> x2, Pallas kernels: none -> 4.92 us  [the longest x1 3.21 us: local(): pl.pallas_call(score_kernel, out_shape=(jax.ShapeDtypeStruct((row_count,...]
    unnamed x7 -> x16, local copies, waits for them, and re-layouts: 1.03 us -> 5.58 us
    dot_general x2 -> x0, matrix products: 4.29 us -> none  [the longest x1 2.21 us: local(): lax.dot_general(rows, cols, (((1,), (1,)), ((), ())), precision=lax.Preci...]
  transfers between devices with their start and end apart: 11 -> 10, of which waited for: 8 -> 7; matrix products, arithmetic and copies ran while one was open for 2% -> 2% of each run, Pallas kernels for 0% -> 0%
where the time goes in v7:
time: 141 us; the launch traced here: 138 us
  blocking collectives  51.2 us (36%)
  starting transfers between devices  41.3 us (29%)
  waiting for transfers between devices  27.4 us (19%)
  local copies, waits for them, and re-layouts  7.88 us (6%)
  Pallas kernels  4.92 us (3%)
  other arithmetic  2.65 us (2%)
  between operations  1.62 us (1%)
  matrix products  1.43 us (1%)
    all_gather x1, blocking collectives, local(): rows = lax.all_gather(row_embed, 'z', axis=0, tiled=True)  38.1 us
    ppermute x7, starting transfers between devices, shift(): lax.ppermute(block, axis, [(i, (i + by) % count) for i in range(count)])  20.5 us
    ppermute x7, waiting for transfers between devices, shift(): lax.ppermute(block, axis, [(i, (i + by) % count) for i in range(count)])  14 us
    all_to_all x1, blocking collectives, local(): lax.all_to_all(col_message, ('x', 'y', 'core'), 0, 0, tiled=True)  13.2 us
    all_to_all x1, waiting for transfers between devices, local(): heard_row = lax.all_to_all(row_message, 'z', 0, 0, tiled=True)  13 us
    all_to_all x1, starting transfers between devices, to_all(): return lax.all_to_all(sent, axes, 0, 0, tiled=True)  9.76 us
    all_to_all x1, starting transfers between devices, local(): heard_row = lax.all_to_all(row_message, 'z', 0, 0, tiled=True)  6.76 us
    unnamed x16, local copies, waits for them, and re-layouts  5.58 us
  transfers between devices with their start and end apart: 10, of which 7 were waited for; matrix products, arithmetic and copies ran while one was open for 2% of the time, Pallas kernels for 0%

profile of v7, /device:TPU:6, one launch (start us, length us, event | category | flops | bytes accessed | tf_op | source)
XLA Modules:
  0.0 138.5 jit_solution(1653067421779962110)
XLA Ops:
  0.6 2.2 %broadcast_in_dim.2 = f32[32,24,512]{2,1,0:T(8,128)} broadcast(f32[24,512]{1,0:T(8,128)} %param.5), dimensions={1,2} | broadcast | bytes 1622016 | tf_op jit(solution)/shard_map/broadcast_in_dim | solution.py:18
  2.8 9.8 %all-to-all-start = ((f32[32,24,512]{2,1,0:T(8,128)}), f32[32,24,512]{2,1,0:T(8,128)S(1)}, u32[]{:S(2)}, u32[]{:S(2)}) async-start(f32[32,24,512]{2,1,0:T(8,128)} %broadcast_in_dim.2), calls=%async_computation | async-start | bytes 3145728 | tf_op jit(solution)/shard_map/all_to_all | solution.py:19
  13.3 38.1 %all_gather.3.row_ref = f32[384,512]{1,0:T(8,128)S(1)} all-gather(f32[24,512]{1,0:T(8,128)S(1)} %copy-done.6), channel_id=1, replica_groups=mesh['z'=16,'x'=4,'y'=4,'core'=2] {'z'}, dimensions={0}, use_global_device_ids=true | all-gather | bytes 835584 | tf_op jit(solution)/shard_map/all_gather | solution.py:105
  51.3 3.2 %scores.1 = (f32[384,768]{1,0:T(8,128)S(1)}, f32[32,8,128]{2,1,0:T(8,128)S(1)}, f32[16,8,128]{2,1,0:T(8,128)}) custom-call(f32[1]{0:T(128)} %bitcast.38.scale_ref, f32[384,512]{1,0:T(8,128)S(1)} %all_gather.3.row_ref, f32[768,512]{1,0:T(8,128)S(1)} %bitcast.40, f32[1,128]{1,0:T(1,128)S(1)} %pad_bitcast_fusion.target_ref), custom_call_target="tpu_custom_call" | custom-call | tf_op jit(solution)/shard_map/scores/pallas_call | solution.py:109
  55.6 13.2 %all_to_all.20.heard_col_ref = f32[32,8,128]{2,1,0:T(8,128)} all-to-all(f32[32,8,128]{2,1,0:T(8,128)S(1)} %get-tuple-element.10), channel_id=1, replica_groups=mesh['z'=16,'x'=4,'y'=4,'core'=2] {'x','y','core'}, dimensions={0} | all-to-all | bytes 262144 | tf_op jit(solution)/shard_map/all_to_all | solution.py:122
  68.7 6.8 %all-to-all-start.2 = ((f32[16,8,128]{2,1,0:T(8,128)}), f32[16,8,128]{2,1,0:T(8,128)S(1)}, u32[]{:S(2)}, u32[]{:S(2)}) async-start(f32[16,8,128]{2,1,0:T(8,128)} %get-tuple-element.13), calls=%async_computation.2 | async-start | bytes 131072 | tf_op jit(solution)/shard_map/all_to_all | solution.py:124
  75.5 13.0 %all-to-all-done.2.heard_row_ref = f32[16,8,128]{2,1,0:T(8,128)S(1)} async-done(((f32[16,8,128]{2,1,0:T(8,128)}), f32[16,8,128]{2,1,0:T(8,128)S(1)}, u32[]{:S(2)}, u32[]{:S(2)}) %all-to-all-start.2) | async-done | bytes 65568 | tf_op jit(solution)/shard_map/all_to_all | solution.py:124
  89.1 1.3 copy-done.1
  92.2 1.7 %weights.1 = (f32[384,768]{1,0:T(8,128)S(1)}, f32[16,24,512]{2,1,0:T(8,128)S(1)}) custom-call(f32[1]{0:T(128)} %bitcast.39.scale_ref, f32[1]{0:T(128)} %bitcast.1.base_ref, f32[384,768]{1,0:T(8,128)S(1)} %copy-done.1, f32[768,512]{1,0:T(8,128)S(1)} %bitcast.41, f32[32,8,128]{2,1,0:T(8,128)S(1)} %copy-done.3, f32[16,8,128]{2,1,0:T(8,128)S(1)} %copy-done.5), custom_call_target="tpu_custom_call" | custom-call | tf_op jit(solution)/shard_map/weights/pallas_call | solution.py:126
  94.8 4.3 %all-to-all-start.3 = ((f32[16,24,512]{2,1,0:T(8,128)}), f32[16,24,512]{2,1,0:T(8,128)}, u32[]{:S(2)}, u32[]{:S(2)}) async-start(f32[16,24,512]{2,1,0:T(8,128)} %copy-done.2), calls=%async_computation.3 | async-start | bytes 1572864 | tf_op jit(solution)/shard_map/all_to_all | solution.py:137
  99.1 1.4 %fusion.5 = f32[768,512]{1,0:T(8,128)S(1)} fusion(f32[384,768]{1,0:T(8,128)S(1)} %get-tuple-element.15, f32[384,512]{1,0:T(8,128)S(1)} %all_gather.3.row_ref), kind=kOutput, calls=%fused_computation.16 | convolution fusion | flops 905969664 | bytes 3538944 | tf_op jit(solution)/shard_map/dot_general | solution.py:138
  100.6 1.9 %collective-permute-start = (f32[4,4,24,512]{3,2,1,0:T(8,128)S(1)}, f32[4,4,24,512]{3,2,1,0:T(8,128)S(1)}, u32[]{:S(2)}, u32[]{:S(2)}) collective-permute-start(f32[4,4,24,512]{3,2,1,0:T(8,128)S(1)} %dynamic-slice_bitcast_fusion), channel_id=1, source_target_pairs={{0,1},{1,0},{2,3},{3,2},{4,5},{5,4},{6,7},{7,6},{8,9},{9,8},{10,11... | collective-permute-start | bytes 2359304 | tf_op jit(solution)/shard_map/ppermute | solution.py:23
  102.6 2.2 %collective-permute-done = f32[4,4,24,512]{3,2,1,0:T(8,128)S(1)} collective-permute-done((f32[4,4,24,512]{3,2,1,0:T(8,128)S(1)}, f32[4,4,24,512]{3,2,1,0:T(8,128)S(1)}, u32[]{:S(2)}, u32[]{:S(2)}) %collective-permute-start) | collective-permute-done | bytes 786464 | tf_op jit(solution)/shard_map/ppermute | solution.py:23
  105.0 2.5 %collective-permute-start.3 = (f32[4,24,512]{2,1,0:T(8,128)S(1)}, f32[4,24,512]{2,1,0:T(8,128)S(1)}, u32[]{:S(2)}, u32[]{:S(2)}) collective-permute-start(f32[4,24,512]{2,1,0:T(8,128)S(1)} %get-tuple-element.17), channel_id=1, source_target_pairs={{0,2},{2,4},{4,6},{6,0},{1,3},{3,5},{5,7},{7,1},{8,10},{10,12},{12... | collective-permute-start | bytes 589832 | tf_op jit(solution)/shard_map/ppermute | solution.py:23
  107.5 4.1 %collective-permute-start.2 = (f32[4,24,512]{2,1,0:T(8,128)S(1)}, f32[4,24,512]{2,1,0:T(8,128)S(1)}, u32[]{:S(2)}, u32[]{:S(2)}) collective-permute-start(f32[4,24,512]{2,1,0:T(8,128)S(1)} %get-tuple-element.18), channel_id=1, source_target_pairs={{0,4},{2,6},{4,0},{6,2},{1,5},{3,7},{5,1},{7,3},{8,12},{10,14},{12... | collective-permute-start | bytes 589832 | tf_op jit(solution)/shard_map/ppermute | solution.py:23
  111.5 2.8 %collective-permute-start.1 = (f32[4,24,512]{2,1,0:T(8,128)S(1)}, f32[4,24,512]{2,1,0:T(8,128)S(1)}, u32[]{:S(2)}, u32[]{:S(2)}) collective-permute-start(f32[4,24,512]{2,1,0:T(8,128)S(1)} %get-tuple-element.16), channel_id=1, source_target_pairs={{0,6},{2,0},{4,2},{6,4},{1,7},{3,1},{5,3},{7,5},{8,14},{10,8},{12,... | collective-permute-start | bytes 589832 | tf_op jit(solution)/shard_map/ppermute | solution.py:23
  114.4 4.8 %collective-permute-done.3 = f32[4,24,512]{2,1,0:T(8,128)S(1)} collective-permute-done((f32[4,24,512]{2,1,0:T(8,128)S(1)}, f32[4,24,512]{2,1,0:T(8,128)S(1)}, u32[]{:S(2)}, u32[]{:S(2)}) %collective-permute-start.3) | collective-permute-done | bytes 196640 | tf_op jit(solution)/shard_map/ppermute | solution.py:23
  119.2 2.5 %collective-permute-done.1 = f32[4,24,512]{2,1,0:T(8,128)S(1)} collective-permute-done((f32[4,24,512]{2,1,0:T(8,128)S(1)}, f32[4,24,512]{2,1,0:T(8,128)S(1)}, u32[]{:S(2)}, u32[]{:S(2)}) %collective-permute-start.1) | collective-permute-done | bytes 196640 | tf_op jit(solution)/shard_map/ppermute | solution.py:23
  121.8 4.0 %collective-permute-start.6 = (f32[24,512]{1,0:T(8,128)S(1)}, f32[24,512]{1,0:T(8,128)S(1)}, u32[]{:S(2)}, u32[]{:S(2)}) collective-permute-start(f32[24,512]{1,0:T(8,128)S(1)} %get-tuple-element.20), channel_id=1, source_target_pairs={{0,8},{8,16},{16,24},{24,0},{1,9},{9,17},{17,25},{25,1},{2,10},{10... | collective-permute-start | bytes 147464 | tf_op jit(solution)/shard_map/ppermute | solution.py:23
  125.9 2.6 %collective-permute-start.5 = (f32[24,512]{1,0:T(8,128)S(1)}, f32[24,512]{1,0:T(8,128)S(1)}, u32[]{:S(2)}, u32[]{:S(2)}) collective-permute-start(f32[24,512]{1,0:T(8,128)S(1)} %get-tuple-element.21), channel_id=1, source_target_pairs={{0,16},{8,24},{16,0},{24,8},{1,17},{9,25},{17,1},{25,9},{2,18},{10... | collective-permute-start | bytes 147464 | tf_op jit(solution)/shard_map/ppermute | solution.py:23
  128.4 2.7 %collective-permute-start.4 = (f32[24,512]{1,0:T(8,128)S(1)}, f32[24,512]{1,0:T(8,128)S(1)}, u32[]{:S(2)}, u32[]{:S(2)}) collective-permute-start(f32[24,512]{1,0:T(8,128)S(1)} %get-tuple-element.19), channel_id=1, source_target_pairs={{0,24},{8,0},{16,8},{24,16},{1,25},{9,1},{17,9},{25,17},{2,26},{10... | collective-permute-start | bytes 147464 | tf_op jit(solution)/shard_map/ppermute | solution.py:23
  131.2 2.7 %collective-permute-done.5 = f32[24,512]{1,0:T(8,128)S(1)} collective-permute-done((f32[24,512]{1,0:T(8,128)S(1)}, f32[24,512]{1,0:T(8,128)S(1)}, u32[]{:S(2)}, u32[]{:S(2)}) %collective-permute-start.5) | collective-permute-done | bytes 49184 | tf_op jit(solution)/shard_map/ppermute | solution.py:23
  133.8 1.8 %collective-permute-done.4 = f32[24,512]{1,0:T(8,128)S(1)} collective-permute-done((f32[24,512]{1,0:T(8,128)S(1)}, f32[24,512]{1,0:T(8,128)S(1)}, u32[]{:S(2)}, u32[]{:S(2)}) %collective-permute-start.4) | collective-permute-done | bytes 49184 | tf_op jit(solution)/shard_map/ppermute | solution.py:23
  136.7 1.8 %reduce_sum.9 = f32[24,512]{1,0:T(8,128)} reduce(f32[16,24,512]{2,1,0:T(8,128)} %all-to-all-done.3, f32[]{:T(128)} %constant.112.clone.1), dimensions={0}, to_apply=%region_0.1 | reduce | flops 184320 | bytes 835588 | tf_op jit(solution)/shard_map/reduce_sum | solution.py:145
  (27 shorter events, 5.7 us)
Async XLA Ops:
  2.8 10.4 %copy-start.7 = (s32[24]{0:T(128)S(1)}, s32[24]{0:T(128)}, u32[]{:S(2)}) copy-start(s32[24]{0:T(128)} %param.7) | copy-start | bytes 292
  2.8 10.5 %copy-start.6 = (f32[24,512]{1,0:T(8,128)S(1)}, f32[24,512]{1,0:T(8,128)}, u32[]{:S(2)}) copy-start(f32[24,512]{1,0:T(8,128)} %param.4) | copy-start | bytes 147460
  2.8 48.5 %all-to-all-start = ((f32[32,24,512]{2,1,0:T(8,128)}), f32[32,24,512]{2,1,0:T(8,128)S(1)}, u32[]{:S(2)}, u32[]{:S(2)}) async-start(f32[32,24,512]{2,1,0:T(8,128)} %broadcast_in_dim.2), calls=%async_computation | async-start | bytes 3145728 | tf_op jit(solution)/shard_map/all_to_all | solution.py:19
  54.5 1.0 copy-start
  68.7 19.8 %all-to-all-start.2 = ((f32[16,8,128]{2,1,0:T(8,128)}), f32[16,8,128]{2,1,0:T(8,128)S(1)}, u32[]{:S(2)}, u32[]{:S(2)}) async-start(f32[16,8,128]{2,1,0:T(8,128)} %get-tuple-element.13), calls=%async_computation.2 | async-start | bytes 131072 | tf_op jit(solution)/shard_map/all_to_all | solution.py:124
  88.5 0.6 copy-start.4
  89.1 1.3 copy-start.1
  90.4 0.9 copy-start.3
  91.3 0.8 copy-start.5
  93.9 0.9 copy-start.2
  94.8 41.9 %all-to-all-start.3 = ((f32[16,24,512]{2,1,0:T(8,128)}), f32[16,24,512]{2,1,0:T(8,128)}, u32[]{:S(2)}, u32[]{:S(2)}) async-start(f32[16,24,512]{2,1,0:T(8,128)} %copy-done.2), calls=%async_computation.3 | async-start | bytes 1572864 | tf_op jit(solution)/shard_map/all_to_all | solution.py:137
  100.6 4.2 %collective-permute-start = (f32[4,4,24,512]{3,2,1,0:T(8,128)S(1)}, f32[4,4,24,512]{3,2,1,0:T(8,128)S(1)}, u32[]{:S(2)}, u32[]{:S(2)}) collective-permute-start(f32[4,4,24,512]{3,2,1,0:T(8,128)S(1)} %dynamic-slice_bitcast_fusion), channel_id=1, source_target_pairs={{0,1},{1,0},{2,3},{3,2},{4,5},{5,4},{6,7},{7,6},{8,9},{9,8},{10,11... | collective-permute-start | bytes 2359304 | tf_op jit(solution)/shard_map/ppermute | solution.py:23
  105.0 14.3 %collective-permute-start.3 = (f32[4,24,512]{2,1,0:T(8,128)S(1)}, f32[4,24,512]{2,1,0:T(8,128)S(1)}, u32[]{:S(2)}, u32[]{:S(2)}) collective-permute-start(f32[4,24,512]{2,1,0:T(8,128)S(1)} %get-tuple-element.17), channel_id=1, source_target_pairs={{0,2},{2,4},{4,6},{6,0},{1,3},{3,5},{5,7},{7,1},{8,10},{10,12},{12... | collective-permute-start | bytes 589832 | tf_op jit(solution)/shard_map/ppermute | solution.py:23
  107.5 11.8 %collective-permute-start.2 = (f32[4,24,512]{2,1,0:T(8,128)S(1)}, f32[4,24,512]{2,1,0:T(8,128)S(1)}, u32[]{:S(2)}, u32[]{:S(2)}) collective-permute-start(f32[4,24,512]{2,1,0:T(8,128)S(1)} %get-tuple-element.18), channel_id=1, source_target_pairs={{0,4},{2,6},{4,0},{6,2},{1,5},{3,7},{5,1},{7,3},{8,12},{10,14},{12... | collective-permute-start | bytes 589832 | tf_op jit(solution)/shard_map/ppermute | solution.py:23
  111.5 10.2 %collective-permute-start.1 = (f32[4,24,512]{2,1,0:T(8,128)S(1)}, f32[4,24,512]{2,1,0:T(8,128)S(1)}, u32[]{:S(2)}, u32[]{:S(2)}) collective-permute-start(f32[4,24,512]{2,1,0:T(8,128)S(1)} %get-tuple-element.16), channel_id=1, source_target_pairs={{0,6},{2,0},{4,2},{6,4},{1,7},{3,1},{5,3},{7,5},{8,14},{10,8},{12,... | collective-permute-start | bytes 589832 | tf_op jit(solution)/shard_map/ppermute | solution.py:23
  121.8 9.3 %collective-permute-start.6 = (f32[24,512]{1,0:T(8,128)S(1)}, f32[24,512]{1,0:T(8,128)S(1)}, u32[]{:S(2)}, u32[]{:S(2)}) collective-permute-start(f32[24,512]{1,0:T(8,128)S(1)} %get-tuple-element.20), channel_id=1, source_target_pairs={{0,8},{8,16},{16,24},{24,0},{1,9},{9,17},{17,25},{25,1},{2,10},{10... | collective-permute-start | bytes 147464 | tf_op jit(solution)/shard_map/ppermute | solution.py:23
  125.9 8.0 %collective-permute-start.5 = (f32[24,512]{1,0:T(8,128)S(1)}, f32[24,512]{1,0:T(8,128)S(1)}, u32[]{:S(2)}, u32[]{:S(2)}) collective-permute-start(f32[24,512]{1,0:T(8,128)S(1)} %get-tuple-element.21), channel_id=1, source_target_pairs={{0,16},{8,24},{16,0},{24,8},{1,17},{9,25},{17,1},{25,9},{2,18},{10... | collective-permute-start | bytes 147464 | tf_op jit(solution)/shard_map/ppermute | solution.py:23
  128.4 7.2 %collective-permute-start.4 = (f32[24,512]{1,0:T(8,128)S(1)}, f32[24,512]{1,0:T(8,128)S(1)}, u32[]{:S(2)}, u32[]{:S(2)}) collective-permute-start(f32[24,512]{1,0:T(8,128)S(1)} %get-tuple-element.19), channel_id=1, source_target_pairs={{0,24},{8,0},{16,8},{24,16},{1,25},{9,1},{17,9},{25,17},{2,26},{10... | collective-permute-start | bytes 147464 | tf_op jit(solution)/shard_map/ppermute | solution.py:23

commit v8 on v7

v8 whole, which is shorter than its diff:
```python
import jax
import jax.numpy as jnp
from jax import lax
from jax.experimental import pallas as pl
from jax.experimental.pallas import tpu as pltpu
from jax.sharding import Mesh, PartitionSpec as P

ALL = ("z", "x", "y", "core")
Z, SIDE, CORE = 16, 4, 2
PLANE = SIDE * SIDE * CORE
LANES = 128
SMEM = pl.BlockSpec(memory_space=pltpu.SMEM)
VMEM = pl.BlockSpec(memory_space=pltpu.VMEM)
ANY = pl.BlockSpec(memory_space=pl.ANY)
HBM = pl.BlockSpec(memory_space=pltpu.HBM)
PARAMS = pltpu.CompilerParams(vmem_limit_bytes=48 * 1024 * 1024)


def to_all(block, axes, count):
    sent = jnp.broadcast_to(block[None], (count,) + block.shape)
    return lax.all_to_all(sent, axes, 0, 0, tiled=True)


def shift(block, axis, count, by):
    return lax.ppermute(block, axis, [(i, (i + by) % count) for i in range(count)])


def home(parts, axis, count, dim, me):
    def part(by):
        return lax.dynamic_index_in_dim(parts, (me - by + count) % count, dim, keepdims=False)

    total = part(0)
    for by in range(1, count):
        total = total + shift(part(by), axis, count, -by)
    return total


def score_kernel(
    scale_ref, row_ref, col_ref, target_ref, score_out, col_out, row_out, score_ref, col_part, row_part, sems
):
    stores = [
        pltpu.make_async_copy(source, target, sems.at[k])
        for k, (source, target) in enumerate(((score_ref, score_out), (row_part, row_out), (col_part, col_out)))
    ]
    scores = scale_ref[0] * lax.dot_general(
        row_ref[...], col_ref[...], (((1,), (1,)), ((), ())),
        precision=lax.Precision.HIGHEST, preferred_element_type=jnp.float32,
    )
    score_ref[...] = scores
    stores[0].start()
    used = scores.shape[0] // LANES
    for k in range(used):
        part = scores[k * LANES:(k + 1) * LANES]
        top = jnp.max(part, axis=1, keepdims=True)
        lse = top + jnp.log(jnp.sum(jnp.exp(part - top), axis=1, keepdims=True))
        lse = jnp.transpose(jnp.broadcast_to(lse, (LANES, LANES)))[:1]
        row_part[:, k, :] = jnp.broadcast_to(lse, (row_part.shape[0], LANES))
    row_part[:, used, :] = jnp.broadcast_to(target_ref[...], (row_part.shape[0], LANES))
    row_part[:, used + 1:, :] = jnp.zeros_like(row_part[:, used + 1:, :])
    stores[1].start()
    top = jnp.max(scores, axis=0, keepdims=True)
    lse = top + jnp.log(jnp.sum(jnp.exp(scores - top), axis=0, keepdims=True))
    used = lse.shape[1] // LANES
    for k in range(used):
        col_part[:, k, :] = jnp.broadcast_to(lse[:, k * LANES:(k + 1) * LANES], (col_part.shape[0], LANES))
    col_part[:, used:, :] = jnp.zeros_like(col_part[:, used:, :])
    stores[2].start()
    for store in stores:
        store.wait()


def split(values):
    high = values.astype(jnp.bfloat16)
    return high, (values - high.astype(jnp.float32)).astype(jnp.bfloat16)


def combined(heard):
    top = jnp.max(heard, axis=0)
    return top + jnp.log(jnp.sum(jnp.exp(heard - top[None]), axis=0))


def weight_kernel(
    scale_ref, base_ref, col_ref, score_in, heard_col_in, heard_row_in,
    weight_out, grad_out, score_ref, heard_col_ref, heard_row_ref, weight_ref, grad_ref, sems, out_sems,
):
    fetches = [
        pltpu.make_async_copy(source, target, sems.at[k])
        for k, (source, target) in enumerate(
            ((heard_row_in, heard_row_ref), (heard_col_in, heard_col_ref), (score_in, score_ref))
        )
    ]
    for fetch in fetches:
        fetch.start()
    row_count, col_count = score_ref.shape
    own = grad_ref.shape[1]
    col_high, col_low = split(col_ref[...])
    ids = lax.broadcasted_iota(jnp.int32, (own, col_count), 1).astype(jnp.float32)
    base = base_ref[0]
    for fetch in fetches:
        fetch.wait()
    col_lse = combined(heard_col_ref[...])
    col_lse = jnp.concatenate([col_lse[k:k + 1] for k in range(col_count // LANES)], axis=1)
    row_lse = combined(heard_row_ref[...])
    row_lse = jnp.concatenate(
        [jnp.transpose(jnp.broadcast_to(row_lse[k:k + 1], (LANES, LANES))) for k in range(row_count // LANES)], axis=0
    )[:, :1]
    targets = jnp.transpose(
        jnp.concatenate([heard_row_ref[:, row_count // LANES, :], jnp.zeros((LANES - Z, LANES), jnp.float32)], axis=0)
    )
    stores = []
    for part in range(2):
        first, count = part * Z // 2, Z // 2
        for z in range(first, first + count):
            here = slice(z * own, (z + 1) * own)
            scores = score_ref[here, :]
            weight_ref[here, :] = (
                0.5 * jnp.exp(scores - row_lse[here])
                + 0.5 * jnp.exp(scores - col_lse)
                - jnp.where(targets[:own, z:z + 1] - base == ids, 1.0, 0.0)
            )
        here = pl.ds(first * own, count * own)
        stores.append(pltpu.make_async_copy(weight_ref.at[here], weight_out.at[here], out_sems.at[0, part]))
        stores[-1].start()
        high, low = split(weight_ref[first * own:(first + count) * own, :])
        total = None
        for left, right in ((high, col_high), (high, col_low), (low, col_high)):
            term = jnp.dot(left, right, preferred_element_type=jnp.float32)
            total = term if total is None else total + term
        here = pl.ds(first, count)
        grad_ref[here] = (scale_ref[0] * total).reshape(count, own, total.shape[1])
        stores.append(pltpu.make_async_copy(grad_ref.at[here], grad_out.at[here], out_sems.at[1, part]))
        stores[-1].start()
    for store in stores:
        store.wait()


def local(row_embed, col_embed, logit_scale, targets):
    own, width = row_embed.shape
    plane, across, along, core = (lax.axis_index(a) for a in ALL)
    scale = logit_scale.reshape(1)
    cols = to_all(col_embed, ("x", "y", "core"), PLANE).reshape(PLANE * own, width)
    rows = lax.all_gather(row_embed, "z", axis=0, tiled=True)
    row_count, col_count = rows.shape[0], cols.shape[0]

    numbers = jnp.pad(targets.astype(jnp.float32), (0, LANES - own)).reshape(1, LANES)
    scores, col_message, row_message = pl.pallas_call(
        score_kernel,
        out_shape=(
            jax.ShapeDtypeStruct((row_count, col_count), jnp.float32),
            pltpu.HBM((SIDE * CORE, 8, LANES), jnp.float32),
            pltpu.HBM((Z, 8, LANES), jnp.float32),
        ),
        in_specs=[SMEM, VMEM, VMEM, VMEM],
        out_specs=(ANY, HBM, HBM),
        scratch_shapes=[
            pltpu.VMEM((row_count, col_count), jnp.float32),
            pltpu.VMEM((SIDE * CORE, 8, LANES), jnp.float32),
            pltpu.VMEM((Z, 8, LANES), jnp.float32),
            pltpu.SemaphoreType.DMA((3,)),
        ],
        compiler_params=PARAMS,
        name="scores",
    )(scale, rows, cols, numbers)

    heard_col = lax.all_to_all(col_message, ("y", "core"), 0, 0, tiled=True)
    heard_col, row_message = lax.optimization_barrier((heard_col, row_message))
    top = jnp.max(heard_col, axis=0)
    heard_col = lax.all_gather(top + jnp.log(jnp.sum(jnp.exp(heard_col - top[None]), axis=0)), "x", axis=0)
    heard_row = lax.all_to_all(row_message, "z", 0, 0, tiled=True)

    weights, grad_rows = pl.pallas_call(
        weight_kernel,
        out_shape=(
            pltpu.HBM((row_count, col_count), jnp.float32),
            pltpu.HBM((Z, own, width), jnp.float32),
        ),
        in_specs=[SMEM, SMEM, VMEM, ANY, ANY, ANY],
        out_specs=(HBM, HBM),
        scratch_shapes=[
            pltpu.VMEM((row_count, col_count), jnp.float32),
            pltpu.VMEM((SIDE, 8, LANES), jnp.float32),
            pltpu.VMEM((Z, 8, LANES), jnp.float32),
            pltpu.VMEM((row_count, col_count), jnp.float32),
            pltpu.VMEM((Z, own, width), jnp.float32),
            pltpu.SemaphoreType.DMA((3,)),
            pltpu.SemaphoreType.DMA((2, 2)),
        ],
        compiler_params=PARAMS,
        name="weights",
    )(scale, (plane * col_count).astype(jnp.float32).reshape(1), cols, scores, heard_col, heard_row)
    row_parts = lax.all_to_all(grad_rows, "z", 0, 0, tiled=True)
    grad_cols = lax.dot_general(
        weights, rows, (((0,), (0,)), ((), ())),
        precision=lax.Precision.HIGH, preferred_element_type=jnp.float32,
    ).reshape(SIDE, SIDE, CORE, own, width)
    col_sum = home(grad_cols, "core", CORE, 2, core)
    col_sum = home(col_sum, "y", SIDE, 1, along)
    col_sum = home(col_sum, "x", SIDE, 0, across)
    return jnp.sum(row_parts, axis=0), logit_scale * col_sum


def solution(mesh):
    grid = Mesh(mesh.devices.reshape(Z, SIDE, SIDE, CORE), ALL)
    placed = P(ALL, None)
    return jax.shard_map(
        local, mesh=grid, in_specs=(placed, placed, P(), P(ALL)), out_specs=(placed, placed), check_vma=False
    )
```

time: 141 us -> 142 us (level)
  starting transfers between devices: 41.3 us -> 52.5 us
  waiting for transfers between devices: 27.4 us -> 19.4 us
  local copies, waits for them, and re-layouts: 7.88 us -> 2.31 us
  Pallas kernels: 4.92 us -> 6.75 us
  other arithmetic: 2.65 us -> 4.2 us
    all_to_all x1 -> x0, blocking collectives: 13.2 us -> none  [local(): lax.all_to_all(col_message, ('x', 'y', 'core'), 0, 0, tiled=True)]
    all_to_all x1, waiting for transfers between devices: 13 us -> 0.01 us  [local(): heard_row = lax.all_to_all(row_message, 'z', 0, 0, tiled=True)]
    all_gather x0 -> x1, blocking collectives: none -> 11.9 us  [local(): lax.all_gather(top + jnp.log(jnp.sum(jnp.exp(heard_col - top[None]), axis...]
    all_to_all x1, starting transfers between devices: 4.27 us -> 12 us  [local(): row_parts = lax.all_to_all(grad_rows, 'z', 0, 0, tiled=True)]
    unnamed x16 -> x4, local copies, waits for them, and re-layouts: 5.58 us -> 0.01 us
    all_to_all x0 -> x1, waiting for transfers between devices: none -> 5.55 us  [local(): heard_col = lax.all_to_all(col_message, ('y', 'core'), 0, 0, tiled=True)]
    all_to_all x0 -> x1, starting transfers between devices: none -> 4.13 us  [local(): heard_col = lax.all_to_all(col_message, ('y', 'core'), 0, 0, tiled=True)]
    pallas_call x1, Pallas kernels: 1.7 us -> 3.17 us  [local(): pl.pallas_call(weight_kernel, out_shape=(pltpu.HBM((row_count, col_count)...]
  transfers between devices with their start and end apart: 10 -> 11, of which waited for: 7 -> 6; matrix products, arithmetic and copies ran while one was open for 2% -> 5% of each run, Pallas kernels for 0% -> 0%
where the time goes in v8:
time: 142 us; the launch traced here: 139 us
  starting transfers between devices  52.5 us (37%)
  blocking collectives  50 us (35%)
  waiting for transfers between devices  19.4 us (14%)
  Pallas kernels  6.75 us (5%)
  other arithmetic  4.2 us (3%)
  matrix products  2.71 us (2%)
  local copies, waits for them, and re-layouts  2.31 us (2%)
  between operations  1.62 us (1%)
    all_gather x1, blocking collectives, local(): rows = lax.all_gather(row_embed, 'z', axis=0, tiled=True)  38.1 us
    ppermute x7, starting transfers between devices, shift(): lax.ppermute(block, axis, [(i, (i + by) % count) for i in range(count)])  20 us
    ppermute x7, waiting for transfers between devices, shift(): lax.ppermute(block, axis, [(i, (i + by) % count) for i in range(count)])  13.9 us
    all_to_all x1, starting transfers between devices, local(): row_parts = lax.all_to_all(grad_rows, 'z', 0, 0, tiled=True)  12 us
    all_gather x1, blocking collectives, local(): lax.all_gather(top + jnp.log(jnp.sum(jnp.exp(heard_col - top[None]), axis...  11.9 us
    all_to_all x1, starting transfers between devices, to_all(): return lax.all_to_all(sent, axes, 0, 0, tiled=True)  9.76 us
    all_to_all x1, starting transfers between devices, local(): heard_row = lax.all_to_all(row_message, 'z', 0, 0, tiled=True)  6.66 us
    all_to_all x1, waiting for transfers between devices, local(): heard_col = lax.all_to_all(col_message, ('y', 'core'), 0, 0, tiled=True)  5.55 us
  transfers between devices with their start and end apart: 11, of which 6 were waited for; matrix products, arithmetic and copies ran while one was open for 5% of the time, Pallas kernels for 0%

profile of v8, /device:TPU:6, one launch (start us, length us, event | category | flops | bytes accessed | tf_op | source)
XLA Modules:
  0.0 139.5 jit_solution(25622075612803035)
XLA Ops:
  0.6 2.2 %broadcast_in_dim.2 = f32[32,24,512]{2,1,0:T(8,128)} broadcast(f32[24,512]{1,0:T(8,128)} %param.5), dimensions={1,2} | broadcast | bytes 1622016 | tf_op jit(solution)/shard_map/broadcast_in_dim | solution.py:20
  2.8 9.8 %all-to-all-start = ((f32[32,24,512]{2,1,0:T(8,128)}), f32[32,24,512]{2,1,0:T(8,128)S(1)}, u32[]{:S(2)}, u32[]{:S(2)}) async-start(f32[32,24,512]{2,1,0:T(8,128)} %broadcast_in_dim.2), calls=%async_computation | async-start | bytes 3145728 | tf_op jit(solution)/shard_map/all_to_all | solution.py:21
  13.3 38.1 %all_gather.7.row_ref = f32[384,512]{1,0:T(8,128)S(1)} all-gather(f32[24,512]{1,0:T(8,128)S(1)} %copy-done), channel_id=1, replica_groups=mesh['z'=16,'x'=4,'y'=4,'core'=2] {'z'}, dimensions={0}, use_global_device_ids=true | all-gather | bytes 835584 | tf_op jit(solution)/shard_map/all_gather | solution.py:142
  51.3 3.6 %scores.1 = (f32[384,768]{1,0:T(8,128)S(1)}, f32[8,8,128]{2,1,0:T(8,128)}, f32[16,8,128]{2,1,0:T(8,128)}) custom-call(f32[1]{0:T(128)} %bitcast.39.scale_ref, f32[384,512]{1,0:T(8,128)S(1)} %all_gather.7.row_ref, f32[768,512]{1,0:T(8,128)S(1)} %bitcast.41, f32[1,128]{1,0:T(1,128)S(1)} %pad_bitcast_fusion.target_ref), custom_call_target="tpu_custom_call" | custom-call | tf_op jit(solution)/shard_map/scores/pallas_call | solution.py:146
  54.9 4.1 %all-to-all-start.1 = ((f32[8,8,128]{2,1,0:T(8,128)}), f32[8,8,128]{2,1,0:T(8,128)}, u32[]{:S(2)}, u32[]{:S(2)}) async-start(f32[8,8,128]{2,1,0:T(8,128)} %get-tuple-element.10), calls=%async_computation.1 | async-start | bytes 65536 | tf_op jit(solution)/shard_map/all_to_all | solution.py:165
  59.0 5.6 %all-to-all-done.1 = f32[8,8,128]{2,1,0:T(8,128)} async-done(((f32[8,8,128]{2,1,0:T(8,128)}), f32[8,8,128]{2,1,0:T(8,128)}, u32[]{:S(2)}, u32[]{:S(2)}) %all-to-all-start.1) | async-done | bytes 32800 | tf_op jit(solution)/shard_map/all_to_all | solution.py:165
  64.6 6.7 %all-to-all-start.2 = ((f32[16,8,128]{2,1,0:T(8,128)}), f32[16,8,128]{2,1,0:T(8,128)}, u32[]{:S(2)}, u32[]{:S(2)}) async-start(f32[16,8,128]{2,1,0:T(8,128)} %get-tuple-element.13), calls=%async_computation.2 | async-start | bytes 131072 | tf_op jit(solution)/shard_map/all_to_all | solution.py:169
  72.8 11.9 %all-gather = f32[32,128]{1,0:T(8,128)S(1)} all-gather(f32[8,128]{1,0:T(8,128)S(1)} %log_add_fusion), channel_id=2, replica_groups=mesh['z'=16,'x'=4,'y'=4,'core'=2] {'x'}, dimensions={0}, use_global_device_ids=true | all-gather | bytes 20480 | tf_op jit(solution)/shard_map/all_gather | solution.py:168
  84.7 3.2 %weights.1 = (f32[384,768]{1,0:T(8,128)}, f32[16,24,512]{2,1,0:T(8,128)}) custom-call(f32[1]{0:T(128)} %bitcast.40.scale_ref, f32[1]{0:T(128)} %bitcast.1.base_ref, f32[768,512]{1,0:T(8,128)S(1)} %bitcast.42, f32[384,768]{1,0:T(8,128)S(1)} %get-tuple-element.9.score_in, f32[4,8,128]{2,1,0:T(8,128)S(1)} %bitcast.43, f32[16,8,128]{2,1,0:T(8,128)} %all-to-all-done.2.heard_row_in), custom_call_target="tpu_custom_call" | custom-call | tf_op jit(solution)/shard_map/weights/pallas_call | solution.py:171
  87.9 12.0 %all-to-all-start.3 = ((f32[16,24,512]{2,1,0:T(8,128)}), f32[16,24,512]{2,1,0:T(8,128)S(1)}, u32[]{:S(2)}, u32[]{:S(2)}) async-start(f32[16,24,512]{2,1,0:T(8,128)} %get-tuple-element.14), calls=%async_computation.3 | async-start | bytes 1572864 | tf_op jit(solution)/shard_map/all_to_all | solution.py:191
  99.9 2.7 %fusion.5 = f32[768,512]{1,0:T(8,128)S(1)} fusion(f32[384,768]{1,0:T(8,128)} %get-tuple-element.15, f32[384,512]{1,0:T(8,128)S(1)} %all_gather.7.row_ref), kind=kOutput, calls=%fused_computation.18 | convolution fusion | flops 905969664 | bytes 3538944 | tf_op jit(solution)/shard_map/dot_general | solution.py:192
  102.7 1.9 %collective-permute-start = (f32[4,4,24,512]{3,2,1,0:T(8,128)S(1)}, f32[4,4,24,512]{3,2,1,0:T(8,128)}, u32[]{:S(2)}, u32[]{:S(2)}) collective-permute-start(f32[4,4,24,512]{3,2,1,0:T(8,128)S(1)} %dynamic-slice_bitcast_fusion), channel_id=1, source_target_pairs={{0,1},{1,0},{2,3},{3,2},{4,5},{5,4},{6,7},{7,6},{8,9},{9,8},{10,11... | collective-permute-start | bytes 2359304 | tf_op jit(solution)/shard_map/ppermute | solution.py:25
  104.7 2.3 %collective-permute-done = f32[4,4,24,512]{3,2,1,0:T(8,128)} collective-permute-done((f32[4,4,24,512]{3,2,1,0:T(8,128)S(1)}, f32[4,4,24,512]{3,2,1,0:T(8,128)}, u32[]{:S(2)}, u32[]{:S(2)}) %collective-permute-start) | collective-permute-done | bytes 786464 | tf_op jit(solution)/shard_map/ppermute | solution.py:25
  107.0 1.3 bitcast_add_fusion
  108.4 2.5 %collective-permute-start.3 = (f32[4,24,512]{2,1,0:T(8,128)S(1)}, f32[4,24,512]{2,1,0:T(8,128)S(1)}, u32[]{:S(2)}, u32[]{:S(2)}) collective-permute-start(f32[4,24,512]{2,1,0:T(8,128)S(1)} %get-tuple-element.17), channel_id=1, source_target_pairs={{0,2},{2,4},{4,6},{6,0},{1,3},{3,5},{5,7},{7,1},{8,10},{10,12},{12... | collective-permute-start | bytes 589832 | tf_op jit(solution)/shard_map/ppermute | solution.py:25
  110.8 4.0 %collective-permute-start.2 = (f32[4,24,512]{2,1,0:T(8,128)S(1)}, f32[4,24,512]{2,1,0:T(8,128)S(1)}, u32[]{:S(2)}, u32[]{:S(2)}) collective-permute-start(f32[4,24,512]{2,1,0:T(8,128)S(1)} %get-tuple-element.18), channel_id=1, source_target_pairs={{0,4},{2,6},{4,0},{6,2},{1,5},{3,7},{5,1},{7,3},{8,12},{10,14},{12... | collective-permute-start | bytes 589832 | tf_op jit(solution)/shard_map/ppermute | solution.py:25
  114.8 3.0 %collective-permute-start.1 = (f32[4,24,512]{2,1,0:T(8,128)S(1)}, f32[4,24,512]{2,1,0:T(8,128)S(1)}, u32[]{:S(2)}, u32[]{:S(2)}) collective-permute-start(f32[4,24,512]{2,1,0:T(8,128)S(1)} %get-tuple-element.16), channel_id=1, source_target_pairs={{0,6},{2,0},{4,2},{6,4},{1,7},{3,1},{5,3},{7,5},{8,14},{10,8},{12,... | collective-permute-start | bytes 589832 | tf_op jit(solution)/shard_map/ppermute | solution.py:25
  117.9 4.7 %collective-permute-done.3 = f32[4,24,512]{2,1,0:T(8,128)S(1)} collective-permute-done((f32[4,24,512]{2,1,0:T(8,128)S(1)}, f32[4,24,512]{2,1,0:T(8,128)S(1)}, u32[]{:S(2)}, u32[]{:S(2)}) %collective-permute-start.3) | collective-permute-done | bytes 196640 | tf_op jit(solution)/shard_map/ppermute | solution.py:25
  122.6 2.5 %collective-permute-done.1 = f32[4,24,512]{2,1,0:T(8,128)S(1)} collective-permute-done((f32[4,24,512]{2,1,0:T(8,128)S(1)}, f32[4,24,512]{2,1,0:T(8,128)S(1)}, u32[]{:S(2)}, u32[]{:S(2)}) %collective-permute-start.1) | collective-permute-done | bytes 196640 | tf_op jit(solution)/shard_map/ppermute | solution.py:25
  125.2 3.0 %collective-permute-start.6 = (f32[24,512]{1,0:T(8,128)S(1)}, f32[24,512]{1,0:T(8,128)S(1)}, u32[]{:S(2)}, u32[]{:S(2)}) collective-permute-start(f32[24,512]{1,0:T(8,128)S(1)} %get-tuple-element.20), channel_id=1, source_target_pairs={{0,8},{8,16},{16,24},{24,0},{1,9},{9,17},{17,25},{25,1},{2,10},{10... | collective-permute-start | bytes 147464 | tf_op jit(solution)/shard_map/ppermute | solution.py:25
  128.2 2.8 %collective-permute-start.5 = (f32[24,512]{1,0:T(8,128)S(1)}, f32[24,512]{1,0:T(8,128)S(1)}, u32[]{:S(2)}, u32[]{:S(2)}) collective-permute-start(f32[24,512]{1,0:T(8,128)S(1)} %get-tuple-element.21), channel_id=1, source_target_pairs={{0,16},{8,24},{16,0},{24,8},{1,17},{9,25},{17,1},{25,9},{2,18},{10... | collective-permute-start | bytes 147464 | tf_op jit(solution)/shard_map/ppermute | solution.py:25
  131.0 2.9 %collective-permute-start.4 = (f32[24,512]{1,0:T(8,128)S(1)}, f32[24,512]{1,0:T(8,128)S(1)}, u32[]{:S(2)}, u32[]{:S(2)}) collective-permute-start(f32[24,512]{1,0:T(8,128)S(1)} %get-tuple-element.19), channel_id=1, source_target_pairs={{0,24},{8,0},{16,8},{24,16},{1,25},{9,1},{17,9},{25,17},{2,26},{10... | collective-permute-start | bytes 147464 | tf_op jit(solution)/shard_map/ppermute | solution.py:25
  133.9 1.9 %collective-permute-done.5 = f32[24,512]{1,0:T(8,128)S(1)} collective-permute-done((f32[24,512]{1,0:T(8,128)S(1)}, f32[24,512]{1,0:T(8,128)S(1)}, u32[]{:S(2)}, u32[]{:S(2)}) %collective-permute-start.5) | collective-permute-done | bytes 49184 | tf_op jit(solution)/shard_map/ppermute | solution.py:25
  135.8 2.4 %collective-permute-done.4 = f32[24,512]{1,0:T(8,128)S(1)} collective-permute-done((f32[24,512]{1,0:T(8,128)S(1)}, f32[24,512]{1,0:T(8,128)S(1)}, u32[]{:S(2)}, u32[]{:S(2)}) %collective-permute-start.4) | collective-permute-done | bytes 49184 | tf_op jit(solution)/shard_map/ppermute | solution.py:25
  (20 shorter events, 3.1 us)
Async XLA Ops:
  2.8 10.4 %copy-start.1 = (s32[24]{0:T(128)S(1)}, s32[24]{0:T(128)}, u32[]{:S(2)}) copy-start(s32[24]{0:T(128)} %param.7) | copy-start | bytes 292
  2.8 10.5 %copy-start = (f32[24,512]{1,0:T(8,128)S(1)}, f32[24,512]{1,0:T(8,128)}, u32[]{:S(2)}) copy-start(f32[24,512]{1,0:T(8,128)} %param.4) | copy-start | bytes 147460
  2.8 48.5 %all-to-all-start = ((f32[32,24,512]{2,1,0:T(8,128)}), f32[32,24,512]{2,1,0:T(8,128)S(1)}, u32[]{:S(2)}, u32[]{:S(2)}) async-start(f32[32,24,512]{2,1,0:T(8,128)} %broadcast_in_dim.2), calls=%async_computation | async-start | bytes 3145728 | tf_op jit(solution)/shard_map/all_to_all | solution.py:21
  54.9 9.7 %all-to-all-start.1 = ((f32[8,8,128]{2,1,0:T(8,128)}), f32[8,8,128]{2,1,0:T(8,128)}, u32[]{:S(2)}, u32[]{:S(2)}) async-start(f32[8,8,128]{2,1,0:T(8,128)} %get-tuple-element.10), calls=%async_computation.1 | async-start | bytes 65536 | tf_op jit(solution)/shard_map/all_to_all | solution.py:165
  64.6 20.2 %all-to-all-start.2 = ((f32[16,8,128]{2,1,0:T(8,128)}), f32[16,8,128]{2,1,0:T(8,128)}, u32[]{:S(2)}, u32[]{:S(2)}) async-start(f32[16,8,128]{2,1,0:T(8,128)} %get-tuple-element.13), calls=%async_computation.2 | async-start | bytes 131072 | tf_op jit(solution)/shard_map/all_to_all | solution.py:169
  87.9 50.9 %all-to-all-start.3 = ((f32[16,24,512]{2,1,0:T(8,128)}), f32[16,24,512]{2,1,0:T(8,128)S(1)}, u32[]{:S(2)}, u32[]{:S(2)}) async-start(f32[16,24,512]{2,1,0:T(8,128)} %get-tuple-element.14), calls=%async_computation.3 | async-start | bytes 1572864 | tf_op jit(solution)/shard_map/all_to_all | solution.py:191
  102.7 4.3 %collective-permute-start = (f32[4,4,24,512]{3,2,1,0:T(8,128)S(1)}, f32[4,4,24,512]{3,2,1,0:T(8,128)}, u32[]{:S(2)}, u32[]{:S(2)}) collective-permute-start(f32[4,4,24,512]{3,2,1,0:T(8,128)S(1)} %dynamic-slice_bitcast_fusion), channel_id=1, source_target_pairs={{0,1},{1,0},{2,3},{3,2},{4,5},{5,4},{6,7},{7,6},{8,9},{9,8},{10,11... | collective-permute-start | bytes 2359304 | tf_op jit(solution)/shard_map/ppermute | solution.py:25
  108.4 14.3 %collective-permute-start.3 = (f32[4,24,512]{2,1,0:T(8,128)S(1)}, f32[4,24,512]{2,1,0:T(8,128)S(1)}, u32[]{:S(2)}, u32[]{:S(2)}) collective-permute-start(f32[4,24,512]{2,1,0:T(8,128)S(1)} %get-tuple-element.17), channel_id=1, source_target_pairs={{0,2},{2,4},{4,6},{6,0},{1,3},{3,5},{5,7},{7,1},{8,10},{10,12},{12... | collective-permute-start | bytes 589832 | tf_op jit(solution)/shard_map/ppermute | solution.py:25
  110.8 11.8 %collective-permute-start.2 = (f32[4,24,512]{2,1,0:T(8,128)S(1)}, f32[4,24,512]{2,1,0:T(8,128)S(1)}, u32[]{:S(2)}, u32[]{:S(2)}) collective-permute-start(f32[4,24,512]{2,1,0:T(8,128)S(1)} %get-tuple-element.18), channel_id=1, source_target_pairs={{0,4},{2,6},{4,0},{6,2},{1,5},{3,7},{5,1},{7,3},{8,12},{10,14},{12... | collective-permute-start | bytes 589832 | tf_op jit(solution)/shard_map/ppermute | solution.py:25
  114.8 10.3 %collective-permute-start.1 = (f32[4,24,512]{2,1,0:T(8,128)S(1)}, f32[4,24,512]{2,1,0:T(8,128)S(1)}, u32[]{:S(2)}, u32[]{:S(2)}) collective-permute-start(f32[4,24,512]{2,1,0:T(8,128)S(1)} %get-tuple-element.16), channel_id=1, source_target_pairs={{0,6},{2,0},{4,2},{6,4},{1,7},{3,1},{5,3},{7,5},{8,14},{10,8},{12,... | collective-permute-start | bytes 589832 | tf_op jit(solution)/shard_map/ppermute | solution.py:25
  125.2 8.6 %collective-permute-start.6 = (f32[24,512]{1,0:T(8,128)S(1)}, f32[24,512]{1,0:T(8,128)S(1)}, u32[]{:S(2)}, u32[]{:S(2)}) collective-permute-start(f32[24,512]{1,0:T(8,128)S(1)} %get-tuple-element.20), channel_id=1, source_target_pairs={{0,8},{8,16},{16,24},{24,0},{1,9},{9,17},{17,25},{25,1},{2,10},{10... | collective-permute-start | bytes 147464 | tf_op jit(solution)/shard_map/ppermute | solution.py:25
  128.2 7.6 %collective-permute-start.5 = (f32[24,512]{1,0:T(8,128)S(1)}, f32[24,512]{1,0:T(8,128)S(1)}, u32[]{:S(2)}, u32[]{:S(2)}) collective-permute-start(f32[24,512]{1,0:T(8,128)S(1)} %get-tuple-element.21), channel_id=1, source_target_pairs={{0,16},{8,24},{16,0},{24,8},{1,17},{9,25},{17,1},{25,9},{2,18},{10... | collective-permute-start | bytes 147464 | tf_op jit(solution)/shard_map/ppermute | solution.py:25
  131.0 7.2 %collective-permute-start.4 = (f32[24,512]{1,0:T(8,128)S(1)}, f32[24,512]{1,0:T(8,128)S(1)}, u32[]{:S(2)}, u32[]{:S(2)}) collective-permute-start(f32[24,512]{1,0:T(8,128)S(1)} %get-tuple-element.19), channel_id=1, source_target_pairs={{0,24},{8,0},{16,8},{24,16},{1,25},{9,1},{17,9},{25,17},{2,26},{10... | collective-permute-start | bytes 147464 | tf_op jit(solution)/shard_map/ppermute | solution.py:25

commit v9 on v8

--- a/solution.py
+++ b/solution.py
@@ -147,14 +147,14 @@
         score_kernel,
         out_shape=(
             jax.ShapeDtypeStruct((row_count, col_count), jnp.float32),
-            pltpu.HBM((SIDE * CORE, 8, LANES), jnp.float32),
+            pltpu.HBM((PLANE, 8, LANES), jnp.float32),
             pltpu.HBM((Z, 8, LANES), jnp.float32),
         ),
         in_specs=[SMEM, VMEM, VMEM, VMEM],
         out_specs=(ANY, HBM, HBM),
         scratch_shapes=[
             pltpu.VMEM((row_count, col_count), jnp.float32),
-            pltpu.VMEM((SIDE * CORE, 8, LANES), jnp.float32),
+            pltpu.VMEM((PLANE, 8, LANES), jnp.float32),
             pltpu.VMEM((Z, 8, LANES), jnp.float32),
             pltpu.SemaphoreType.DMA((3,)),
         ],
@@ -162,10 +162,8 @@
         name="scores",
     )(scale, rows, cols, numbers)
 
-    heard_col = lax.all_to_all(col_message, ("y", "core"), 0, 0, tiled=True)
+    heard_col = lax.all_to_all(col_message, ("x", "y", "core"), 0, 0, tiled=True)
     heard_col, row_message = lax.optimization_barrier((heard_col, row_message))
-    top = jnp.max(heard_col, axis=0)
-    heard_col = lax.all_gather(top + jnp.log(jnp.sum(jnp.exp(heard_col - top[None]), axis=0)), "x", axis=0)
     heard_row = lax.all_to_all(row_message, "z", 0, 0, tiled=True)
 
     weights, grad_rows = pl.pallas_call(
@@ -178,7 +176,7 @@
         out_specs=(HBM, HBM),
         scratch_shapes=[
             pltpu.VMEM((row_count, col_count), jnp.float32),
-            pltpu.VMEM((SIDE, 8, LANES), jnp.float32),
+            pltpu.VMEM((PLANE, 8, LANES), jnp.float32),
             pltpu.VMEM((Z, 8, LANES), jnp.float32),
             pltpu.VMEM((row_count, col_count), jnp.float32),
             pltpu.VMEM((Z, own, width), jnp.float32),

time: 142 us -> 138 us (0.972)
  starting transfers between devices: 52.5 us -> 40.7 us
  waiting for transfers between devices: 19.4 us -> 27.2 us
  other arithmetic: 4.2 us -> 2.65 us
    all_to_all x0 -> x1, blocking collectives: none -> 13.4 us  [local(): lax.all_to_all(col_message, ('x', 'y', 'core'), 0, 0, tiled=True)]
    all_to_all x1, waiting for transfers between devices: 0.01 us -> 13.1 us  [local(): heard_row = lax.all_to_all(row_message, 'z', 0, 0, tiled=True)]
    all_gather x1 -> x0, blocking collectives: 11.9 us -> none  [local(): lax.all_gather(top + jnp.log(jnp.sum(jnp.exp(heard_col - top[None]), axis...]
    all_to_all x1, starting transfers between devices: 12 us -> 3.62 us  [local(): row_parts = lax.all_to_all(grad_rows, 'z', 0, 0, tiled=True)]
    all_to_all x1 -> x0, waiting for transfers between devices: 5.55 us -> none  [local(): heard_col = lax.all_to_all(col_message, ('y', 'core'), 0, 0, tiled=True)]
    all_to_all x1 -> x0, starting transfers between devices: 4.13 us -> none  [local(): heard_col = lax.all_to_all(col_message, ('y', 'core'), 0, 0, tiled=True)]
  transfers between devices with their start and end apart: 11 -> 10, of which waited for: 6 -> 6; matrix products, arithmetic and copies ran while one was open for 5% -> 4% of each run, Pallas kernels for 0% -> 0%
where the time goes in v9:
time: 138 us; the launch traced here: 136 us
  blocking collectives  51.4 us (37%)
  starting transfers between devices  40.7 us (29%)
  waiting for transfers between devices  27.2 us (20%)
  Pallas kernels  6.82 us (5%)
  local copies, waits for them, and re-layouts  3.22 us (2%)
  matrix products  2.71 us (2%)
  other arithmetic  2.65 us (2%)
  between operations  1.62 us (1%)
    all_gather x1, blocking collectives, local(): rows = lax.all_gather(row_embed, 'z', axis=0, tiled=True)  38.1 us
    ppermute x7, starting transfers between devices, shift(): lax.ppermute(block, axis, [(i, (i + by) % count) for i in range(count)])  20.5 us
    ppermute x7, waiting for transfers between devices, shift(): lax.ppermute(block, axis, [(i, (i + by) % count) for i in range(count)])  14.1 us
    all_to_all x1, blocking collectives, local(): lax.all_to_all(col_message, ('x', 'y', 'core'), 0, 0, tiled=True)  13.4 us
    all_to_all x1, waiting for transfers between devices, local(): heard_row = lax.all_to_all(row_message, 'z', 0, 0, tiled=True)  13.1 us
    all_to_all x1, starting transfers between devices, to_all(): return lax.all_to_all(sent, axes, 0, 0, tiled=True)  9.76 us
    all_to_all x1, starting transfers between devices, local(): heard_row = lax.all_to_all(row_message, 'z', 0, 0, tiled=True)  6.81 us
    pallas_call x1, Pallas kernels, local(): pl.pallas_call(score_kernel, out_shape=(jax.ShapeDtypeStruct((row_count,...  3.64 us
  transfers between devices with their start and end apart: 10, of which 6 were waited for; matrix products, arithmetic and copies ran while one was open for 4% of the time, Pallas kernels for 0%

profile of v9, /device:TPU:6, one launch (start us, length us, event | category | flops | bytes accessed | tf_op | source)
XLA Modules:
  0.0 136.4 jit_solution(8363404764545302221)
XLA Ops:
  0.6 2.2 %broadcast_in_dim.2 = f32[32,24,512]{2,1,0:T(8,128)} broadcast(f32[24,512]{1,0:T(8,128)} %param.5), dimensions={1,2} | broadcast | bytes 1622016 | tf_op jit(solution)/shard_map/broadcast_in_dim | solution.py:20
  2.8 9.8 %all-to-all-start = ((f32[32,24,512]{2,1,0:T(8,128)}), f32[32,24,512]{2,1,0:T(8,128)S(1)}, u32[]{:S(2)}, u32[]{:S(2)}) async-start(f32[32,24,512]{2,1,0:T(8,128)} %broadcast_in_dim.2), calls=%async_computation | async-start | bytes 3145728 | tf_op jit(solution)/shard_map/all_to_all | solution.py:21
  13.3 38.1 %all_gather.3.row_ref = f32[384,512]{1,0:T(8,128)S(1)} all-gather(f32[24,512]{1,0:T(8,128)S(1)} %copy-done.1), channel_id=1, replica_groups=mesh['z'=16,'x'=4,'y'=4,'core'=2] {'z'}, dimensions={0}, use_global_device_ids=true | all-gather | bytes 835584 | tf_op jit(solution)/shard_map/all_gather | solution.py:142
  51.3 3.6 %scores.1 = (f32[384,768]{1,0:T(8,128)S(1)}, f32[32,8,128]{2,1,0:T(8,128)}, f32[16,8,128]{2,1,0:T(8,128)}) custom-call(f32[1]{0:T(128)} %bitcast.38.scale_ref, f32[384,512]{1,0:T(8,128)S(1)} %all_gather.3.row_ref, f32[768,512]{1,0:T(8,128)S(1)} %bitcast.40, f32[1,128]{1,0:T(1,128)S(1)} %pad_bitcast_fusion.target_ref), custom_call_target="tpu_custom_call" | custom-call | tf_op jit(solution)/shard_map/scores/pallas_call | solution.py:146
  55.0 13.4 %all_to_all.20.heard_col_in = f32[32,8,128]{2,1,0:T(8,128)} all-to-all(f32[32,8,128]{2,1,0:T(8,128)} %get-tuple-element.10), channel_id=1, replica_groups=mesh['z'=16,'x'=4,'y'=4,'core'=2] {'x','y','core'}, dimensions={0} | all-to-all | bytes 262144 | tf_op jit(solution)/shard_map/all_to_all | solution.py:165
  68.4 6.8 %all-to-all-start.2 = ((f32[16,8,128]{2,1,0:T(8,128)}), f32[16,8,128]{2,1,0:T(8,128)}, u32[]{:S(2)}, u32[]{:S(2)}) async-start(f32[16,8,128]{2,1,0:T(8,128)} %get-tuple-element.13), calls=%async_computation.2 | async-start | bytes 131072 | tf_op jit(solution)/shard_map/all_to_all | solution.py:167
  75.2 13.1 %all-to-all-done.2.heard_row_in = f32[16,8,128]{2,1,0:T(8,128)} async-done(((f32[16,8,128]{2,1,0:T(8,128)}), f32[16,8,128]{2,1,0:T(8,128)}, u32[]{:S(2)}, u32[]{:S(2)}) %all-to-all-start.2) | async-done | bytes 65568 | tf_op jit(solution)/shard_map/all_to_all | solution.py:167
  88.3 0.9 copy-done
  89.2 3.2 %weights.1 = (f32[384,768]{1,0:T(8,128)}, f32[16,24,512]{2,1,0:T(8,128)}) custom-call(f32[1]{0:T(128)} %bitcast.39.scale_ref, f32[1]{0:T(128)} %bitcast.1.base_ref, f32[768,512]{1,0:T(8,128)S(1)} %bitcast.41, f32[384,768]{1,0:T(8,128)S(1)} %get-tuple-element.9.score_in, f32[32,8,128]{2,1,0:T(8,128)S(1)} %copy-done, f32[16,8,128]{2,1,0:T(8,128)} %all-to-all-done.2.heard_row_in), custom_call_target="tpu_custom_call" | custom-call | tf_op jit(solution)/shard_map/weights/pallas_call | solution.py:169
  92.4 3.6 %all-to-all-start.3 = ((f32[16,24,512]{2,1,0:T(8,128)}), f32[16,24,512]{2,1,0:T(8,128)S(1)}, u32[]{:S(2)}, u32[]{:S(2)}) async-start(f32[16,24,512]{2,1,0:T(8,128)} %get-tuple-element.14), calls=%async_computation.3 | async-start | bytes 1572864 | tf_op jit(solution)/shard_map/all_to_all | solution.py:189
  96.0 2.7 %fusion.5 = f32[768,512]{1,0:T(8,128)S(1)} fusion(f32[384,768]{1,0:T(8,128)} %get-tuple-element.15, f32[384,512]{1,0:T(8,128)S(1)} %all_gather.3.row_ref), kind=kOutput, calls=%fused_computation.16 | convolution fusion | flops 905969664 | bytes 3538944 | tf_op jit(solution)/shard_map/dot_general | solution.py:190
  98.8 1.9 %collective-permute-start = (f32[4,4,24,512]{3,2,1,0:T(8,128)S(1)}, f32[4,4,24,512]{3,2,1,0:T(8,128)}, u32[]{:S(2)}, u32[]{:S(2)}) collective-permute-start(f32[4,4,24,512]{3,2,1,0:T(8,128)S(1)} %dynamic-slice_bitcast_fusion), channel_id=1, source_target_pairs={{0,1},{1,0},{2,3},{3,2},{4,5},{5,4},{6,7},{7,6},{8,9},{9,8},{10,11... | collective-permute-start | bytes 2359304 | tf_op jit(solution)/shard_map/ppermute | solution.py:25
  100.8 2.3 %collective-permute-done = f32[4,4,24,512]{3,2,1,0:T(8,128)} collective-permute-done((f32[4,4,24,512]{3,2,1,0:T(8,128)S(1)}, f32[4,4,24,512]{3,2,1,0:T(8,128)}, u32[]{:S(2)}, u32[]{:S(2)}) %collective-permute-start) | collective-permute-done | bytes 786464 | tf_op jit(solution)/shard_map/ppermute | solution.py:25
  103.1 1.3 bitcast_add_fusion
  104.4 2.5 %collective-permute-start.3 = (f32[4,24,512]{2,1,0:T(8,128)S(1)}, f32[4,24,512]{2,1,0:T(8,128)S(1)}, u32[]{:S(2)}, u32[]{:S(2)}) collective-permute-start(f32[4,24,512]{2,1,0:T(8,128)S(1)} %get-tuple-element.17), channel_id=1, source_target_pairs={{0,2},{2,4},{4,6},{6,0},{1,3},{3,5},{5,7},{7,1},{8,10},{10,12},{12... | collective-permute-start | bytes 589832 | tf_op jit(solution)/shard_map/ppermute | solution.py:25
  106.9 4.1 %collective-permute-start.2 = (f32[4,24,512]{2,1,0:T(8,128)S(1)}, f32[4,24,512]{2,1,0:T(8,128)S(1)}, u32[]{:S(2)}, u32[]{:S(2)}) collective-permute-start(f32[4,24,512]{2,1,0:T(8,128)S(1)} %get-tuple-element.18), channel_id=1, source_target_pairs={{0,4},{2,6},{4,0},{6,2},{1,5},{3,7},{5,1},{7,3},{8,12},{10,14},{12... | collective-permute-start | bytes 589832 | tf_op jit(solution)/shard_map/ppermute | solution.py:25
  111.0 2.8 %collective-permute-start.1 = (f32[4,24,512]{2,1,0:T(8,128)S(1)}, f32[4,24,512]{2,1,0:T(8,128)S(1)}, u32[]{:S(2)}, u32[]{:S(2)}) collective-permute-start(f32[4,24,512]{2,1,0:T(8,128)S(1)} %get-tuple-element.16), channel_id=1, source_target_pairs={{0,6},{2,0},{4,2},{6,4},{1,7},{3,1},{5,3},{7,5},{8,14},{10,8},{12,... | collective-permute-start | bytes 589832 | tf_op jit(solution)/shard_map/ppermute | solution.py:25
  113.9 4.8 %collective-permute-done.3 = f32[4,24,512]{2,1,0:T(8,128)S(1)} collective-permute-done((f32[4,24,512]{2,1,0:T(8,128)S(1)}, f32[4,24,512]{2,1,0:T(8,128)S(1)}, u32[]{:S(2)}, u32[]{:S(2)}) %collective-permute-start.3) | collective-permute-done | bytes 196640 | tf_op jit(solution)/shard_map/ppermute | solution.py:25
  118.7 2.5 %collective-permute-done.1 = f32[4,24,512]{2,1,0:T(8,128)S(1)} collective-permute-done((f32[4,24,512]{2,1,0:T(8,128)S(1)}, f32[4,24,512]{2,1,0:T(8,128)S(1)}, u32[]{:S(2)}, u32[]{:S(2)}) %collective-permute-start.1) | collective-permute-done | bytes 196640 | tf_op jit(solution)/shard_map/ppermute | solution.py:25
  121.3 4.0 %collective-permute-start.6 = (f32[24,512]{1,0:T(8,128)S(1)}, f32[24,512]{1,0:T(8,128)S(1)}, u32[]{:S(2)}, u32[]{:S(2)}) collective-permute-start(f32[24,512]{1,0:T(8,128)S(1)} %get-tuple-element.20), channel_id=1, source_target_pairs={{0,8},{8,16},{16,24},{24,0},{1,9},{9,17},{17,25},{25,1},{2,10},{10... | collective-permute-start | bytes 147464 | tf_op jit(solution)/shard_map/ppermute | solution.py:25
  125.3 2.6 %collective-permute-start.5 = (f32[24,512]{1,0:T(8,128)S(1)}, f32[24,512]{1,0:T(8,128)S(1)}, u32[]{:S(2)}, u32[]{:S(2)}) collective-permute-start(f32[24,512]{1,0:T(8,128)S(1)} %get-tuple-element.21), channel_id=1, source_target_pairs={{0,16},{8,24},{16,0},{24,8},{1,17},{9,25},{17,1},{25,9},{2,18},{10... | collective-permute-start | bytes 147464 | tf_op jit(solution)/shard_map/ppermute | solution.py:25
  127.9 2.7 %collective-permute-start.4 = (f32[24,512]{1,0:T(8,128)S(1)}, f32[24,512]{1,0:T(8,128)S(1)}, u32[]{:S(2)}, u32[]{:S(2)}) collective-permute-start(f32[24,512]{1,0:T(8,128)S(1)} %get-tuple-element.19), channel_id=1, source_target_pairs={{0,24},{8,0},{16,8},{24,16},{1,25},{9,1},{17,9},{25,17},{2,26},{10... | collective-permute-start | bytes 147464 | tf_op jit(solution)/shard_map/ppermute | solution.py:25
  130.6 2.6 %collective-permute-done.5 = f32[24,512]{1,0:T(8,128)S(1)} collective-permute-done((f32[24,512]{1,0:T(8,128)S(1)}, f32[24,512]{1,0:T(8,128)S(1)}, u32[]{:S(2)}, u32[]{:S(2)}) %collective-permute-start.5) | collective-permute-done | bytes 49184 | tf_op jit(solution)/shard_map/ppermute | solution.py:25
  133.2 1.9 %collective-permute-done.4 = f32[24,512]{1,0:T(8,128)S(1)} collective-permute-done((f32[24,512]{1,0:T(8,128)S(1)}, f32[24,512]{1,0:T(8,128)S(1)}, u32[]{:S(2)}, u32[]{:S(2)}) %collective-permute-start.4) | collective-permute-done | bytes 49184 | tf_op jit(solution)/shard_map/ppermute | solution.py:25
  (17 shorter events, 1.5 us)
Async XLA Ops:
  2.8 10.4 %copy-start.2 = (s32[24]{0:T(128)S(1)}, s32[24]{0:T(128)}, u32[]{:S(2)}) copy-start(s32[24]{0:T(128)} %param.7) | copy-start | bytes 292
  2.8 10.5 %copy-start.1 = (f32[24,512]{1,0:T(8,128)S(1)}, f32[24,512]{1,0:T(8,128)}, u32[]{:S(2)}) copy-start(f32[24,512]{1,0:T(8,128)} %param.4) | copy-start | bytes 147460
  2.8 48.5 %all-to-all-start = ((f32[32,24,512]{2,1,0:T(8,128)}), f32[32,24,512]{2,1,0:T(8,128)S(1)}, u32[]{:S(2)}, u32[]{:S(2)}) async-start(f32[32,24,512]{2,1,0:T(8,128)} %broadcast_in_dim.2), calls=%async_computation | async-start | bytes 3145728 | tf_op jit(solution)/shard_map/all_to_all | solution.py:21
  68.4 19.9 %all-to-all-start.2 = ((f32[16,8,128]{2,1,0:T(8,128)}), f32[16,8,128]{2,1,0:T(8,128)}, u32[]{:S(2)}, u32[]{:S(2)}) async-start(f32[16,8,128]{2,1,0:T(8,128)} %get-tuple-element.13), calls=%async_computation.2 | async-start | bytes 131072 | tf_op jit(solution)/shard_map/all_to_all | solution.py:167
  88.3 0.9 copy-start
  92.4 43.4 %all-to-all-start.3 = ((f32[16,24,512]{2,1,0:T(8,128)}), f32[16,24,512]{2,1,0:T(8,128)S(1)}, u32[]{:S(2)}, u32[]{:S(2)}) async-start(f32[16,24,512]{2,1,0:T(8,128)} %get-tuple-element.14), calls=%async_computation.3 | async-start | bytes 1572864 | tf_op jit(solution)/shard_map/all_to_all | solution.py:189
  98.8 4.3 %collective-permute-start = (f32[4,4,24,512]{3,2,1,0:T(8,128)S(1)}, f32[4,4,24,512]{3,2,1,0:T(8,128)}, u32[]{:S(2)}, u32[]{:S(2)}) collective-permute-start(f32[4,4,24,512]{3,2,1,0:T(8,128)S(1)} %dynamic-slice_bitcast_fusion), channel_id=1, source_target_pairs={{0,1},{1,0},{2,3},{3,2},{4,5},{5,4},{6,7},{7,6},{8,9},{9,8},{10,11... | collective-permute-start | bytes 2359304 | tf_op jit(solution)/shard_map/ppermute | solution.py:25
  104.4 14.3 %collective-permute-start.3 = (f32[4,24,512]{2,1,0:T(8,128)S(1)}, f32[4,24,512]{2,1,0:T(8,128)S(1)}, u32[]{:S(2)}, u32[]{:S(2)}) collective-permute-start(f32[4,24,512]{2,1,0:T(8,128)S(1)} %get-tuple-element.17), channel_id=1, source_target_pairs={{0,2},{2,4},{4,6},{6,0},{1,3},{3,5},{5,7},{7,1},{8,10},{10,12},{12... | collective-permute-start | bytes 589832 | tf_op jit(solution)/shard_map/ppermute | solution.py:25
  106.9 11.8 %collective-permute-start.2 = (f32[4,24,512]{2,1,0:T(8,128)S(1)}, f32[4,24,512]{2,1,0:T(8,128)S(1)}, u32[]{:S(2)}, u32[]{:S(2)}) collective-permute-start(f32[4,24,512]{2,1,0:T(8,128)S(1)} %get-tuple-element.18), channel_id=1, source_target_pairs={{0,4},{2,6},{4,0},{6,2},{1,5},{3,7},{5,1},{7,3},{8,12},{10,14},{12... | collective-permute-start | bytes 589832 | tf_op jit(solution)/shard_map/ppermute | solution.py:25
  111.0 10.2 %collective-permute-start.1 = (f32[4,24,512]{2,1,0:T(8,128)S(1)}, f32[4,24,512]{2,1,0:T(8,128)S(1)}, u32[]{:S(2)}, u32[]{:S(2)}) collective-permute-start(f32[4,24,512]{2,1,0:T(8,128)S(1)} %get-tuple-element.16), channel_id=1, source_target_pairs={{0,6},{2,0},{4,2},{6,4},{1,7},{3,1},{5,3},{7,5},{8,14},{10,8},{12,... | collective-permute-start | bytes 589832 | tf_op jit(solution)/shard_map/ppermute | solution.py:25
  121.3 9.3 %collective-permute-start.6 = (f32[24,512]{1,0:T(8,128)S(1)}, f32[24,512]{1,0:T(8,128)S(1)}, u32[]{:S(2)}, u32[]{:S(2)}) collective-permute-start(f32[24,512]{1,0:T(8,128)S(1)} %get-tuple-element.20), channel_id=1, source_target_pairs={{0,8},{8,16},{16,24},{24,0},{1,9},{9,17},{17,25},{25,1},{2,10},{10... | collective-permute-start | bytes 147464 | tf_op jit(solution)/shard_map/ppermute | solution.py:25
  125.3 7.9 %collective-permute-start.5 = (f32[24,512]{1,0:T(8,128)S(1)}, f32[24,512]{1,0:T(8,128)S(1)}, u32[]{:S(2)}, u32[]{:S(2)}) collective-permute-start(f32[24,512]{1,0:T(8,128)S(1)} %get-tuple-element.21), channel_id=1, source_target_pairs={{0,16},{8,24},{16,0},{24,8},{1,17},{9,25},{17,1},{25,9},{2,18},{10... | collective-permute-start | bytes 147464 | tf_op jit(solution)/shard_map/ppermute | solution.py:25
  127.9 7.2 %collective-permute-start.4 = (f32[24,512]{1,0:T(8,128)S(1)}, f32[24,512]{1,0:T(8,128)S(1)}, u32[]{:S(2)}, u32[]{:S(2)}) collective-permute-start(f32[24,512]{1,0:T(8,128)S(1)} %get-tuple-element.19), channel_id=1, source_target_pairs={{0,24},{8,0},{16,8},{24,16},{1,25},{9,1},{17,9},{25,17},{2,26},{10... | collective-permute-start | bytes 147464 | tf_op jit(solution)/shard_map/ppermute | solution.py:25

commit v10 on v9

--- a/solution.py
+++ b/solution.py
@@ -16,8 +16,23 @@
 PARAMS = pltpu.CompilerParams(vmem_limit_bytes=48 * 1024 * 1024)
 
 
+def repeat_kernel(block_ref, out, sems):
+    copies = [pltpu.make_async_copy(block_ref, out.at[k], sems.at[k]) for k in range(out.shape[0])]
+    for copy in copies:
+        copy.start()
+    for copy in copies:
+        copy.wait()
+
+
 def to_all(block, axes, count):
-    sent = jnp.broadcast_to(block[None], (count,) + block.shape)
+    sent = pl.pallas_call(
+        repeat_kernel,
+        out_shape=pltpu.HBM((count,) + block.shape, block.dtype),
+        in_specs=[VMEM],
+        out_specs=HBM,
+        scratch_shapes=[pltpu.SemaphoreType.DMA((count,))],
+        name="repeat",
+    )(block)
     return lax.all_to_all(sent, axes, 0, 0, tiled=True)
 
 
@@ -94,7 +109,14 @@
     row_count, col_count = score_ref.shape
     own = grad_ref.shape[1]
     col_high, col_low = split(col_ref[...])
-    ids = lax.broadcasted_iota(jnp.int32, (own, col_count), 1).astype(jnp.float32)
+    place = lax.broadcasted_iota(jnp.int32, (own, col_count), 1)
+    half = col_count // CORE
+    place_core = (place >= half).astype(jnp.int32)
+    place = place - place_core * half
+    chip = jnp.zeros_like(place)
+    for k in range(1, PLANE // CORE):
+        chip = chip + (place >= k * own).astype(jnp.int32)
+    ids = (place + (chip + place_core) * own).astype(jnp.float32)
     base = base_ref[0]
     for fetch in fetches:
         fetch.wait()
@@ -138,7 +160,7 @@
     own, width = row_embed.shape
     plane, across, along, core = (lax.axis_index(a) for a in ALL)
     scale = logit_scale.reshape(1)
-    cols = to_all(col_embed, ("x", "y", "core"), PLANE).reshape(PLANE * own, width)
+    cols = to_all(col_embed, ("core", "x", "y"), PLANE).reshape(PLANE * own, width)
     rows = lax.all_gather(row_embed, "z", axis=0, tiled=True)
     row_count, col_count = rows.shape[0], cols.shape[0]
 
@@ -162,9 +184,10 @@
         name="scores",
     )(scale, rows, cols, numbers)
 
-    heard_col = lax.all_to_all(col_message, ("x", "y", "core"), 0, 0, tiled=True)
+    heard_col = lax.all_to_all(col_message, ("core", "x", "y"), 0, 0, tiled=True)
     heard_col, row_message = lax.optimization_barrier((heard_col, row_message))
     heard_row = lax.all_to_all(row_message, "z", 0, 0, tiled=True)
+    heard_col = pltpu.with_memory_space_constraint(heard_col, pltpu.HBM)
 
     weights, grad_rows = pl.pallas_call(
         weight_kernel,
@@ -187,12 +210,16 @@
         name="weights",
     )(scale, (plane * col_count).astype(jnp.float32).reshape(1), cols, scores, heard_col, heard_row)
     row_parts = lax.all_to_all(grad_rows, "z", 0, 0, tiled=True)
-    grad_cols = lax.dot_general(
-        weights, rows, (((0,), (0,)), ((), ())),
-        precision=lax.Precision.HIGH, preferred_element_type=jnp.float32,
-    ).reshape(SIDE, SIDE, CORE, own, width)
-    col_sum = home(grad_cols, "core", CORE, 2, core)
-    col_sum = home(col_sum, "y", SIDE, 1, along)
+
+    def grad_cols(of_core):
+        half = col_count // CORE
+        return lax.dot_general(
+            lax.dynamic_slice(weights, (0, of_core * half), (row_count, half)), rows, (((0,), (0,)), ((), ())),
+            precision=lax.Precision.HIGH, preferred_element_type=jnp.float32,
+        ).reshape(SIDE, SIDE, own, width)
+
+    given = shift(grad_cols(1 - core), "core", CORE, 1)
+    col_sum = home(grad_cols(core) + given, "y", SIDE, 1, along)
     col_sum = home(col_sum, "x", SIDE, 0, across)
     return jnp.sum(row_parts, axis=0), logit_scale * col_sum
 

time: 138 us -> 136 us (0.986)
  local copies, waits for them, and re-layouts: 3.22 us -> 0.09 us
  Pallas kernels: 6.82 us -> 9.19 us
    pallas_call x0 -> x1, Pallas kernels: none -> 2.26 us  [to_all(): pl.pallas_call(repeat_kernel, out_shape=pltpu.HBM((count,) + block.shape,...]
    broadcast_in_dim x1 -> x0, local copies, waits for them, and re-layouts: 2.16 us -> none  [to_all(): sent = jnp.broadcast_to(block[None], (count,) + block.shape)]
  transfers between devices with their start and end apart: 10 -> 10, of which waited for: 6 -> 7; matrix products, arithmetic and copies ran while one was open for 4% -> 3% of each run, Pallas kernels for 0% -> 0%
where the time goes in v10:
time: 136 us; the launch traced here: 134 us
  blocking collectives  51.4 us (38%)
  starting transfers between devices  41.1 us (30%)
  waiting for transfers between devices  26.3 us (19%)
  Pallas kernels  9.19 us (7%)
  other arithmetic  2.64 us (2%)
  matrix products  1.68 us (1%)
  between operations  1.63 us (1%)
    all_gather x1, blocking collectives, local(): rows = lax.all_gather(row_embed, 'z', axis=0, tiled=True)  38.1 us
    ppermute x7, starting transfers between devices, shift(): lax.ppermute(block, axis, [(i, (i + by) % count) for i in range(count)])  20.9 us
    all_to_all x1, blocking collectives, local(): lax.all_to_all(col_message, ('core', 'x', 'y'), 0, 0, tiled=True)  13.3 us
    all_to_all x1, waiting for transfers between devices, local(): heard_row = lax.all_to_all(row_message, 'z', 0, 0, tiled=True)  13.1 us
    ppermute x7, waiting for transfers between devices, shift(): lax.ppermute(block, axis, [(i, (i + by) % count) for i in range(count)])  12.9 us
    all_to_all x1, starting transfers between devices, to_all(): return lax.all_to_all(sent, axes, 0, 0, tiled=True)  9.69 us
    all_to_all x1, starting transfers between devices, local(): heard_row = lax.all_to_all(row_message, 'z', 0, 0, tiled=True)  6.83 us
    all_to_all x1, starting transfers between devices, local(): row_parts = lax.all_to_all(grad_rows, 'z', 0, 0, tiled=True)  3.76 us
  transfers between devices with their start and end apart: 10, of which 7 were waited for; matrix products, arithmetic and copies ran while one was open for 3% of the time, Pallas kernels for 0%

profile of v10, /device:TPU:6, one launch (start us, length us, event | category | flops | bytes accessed | tf_op | source)
XLA Modules:
  0.0 134.1 jit_solution(2597021914542448406)
XLA Ops:
  0.6 2.3 %repeat.1 = f32[32,24,512]{2,1,0:T(8,128)} custom-call(f32[24,512]{1,0:T(8,128)} %block_ref.1), custom_call_target="tpu_custom_call" | custom-call | tf_op jit(solution)/shard_map/repeat/pallas_call | solution.py:28
  2.9 9.7 %all-to-all-start = ((f32[32,24,512]{2,1,0:T(8,128)}), f32[32,24,512]{2,1,0:T(8,128)S(1)}, u32[]{:S(2)}, u32[]{:S(2)}) async-start(f32[32,24,512]{2,1,0:T(8,128)} %repeat.1), calls=%async_computation | async-start | bytes 3145728 | tf_op jit(solution)/shard_map/all_to_all | solution.py:36
  13.3 38.1 %all_gather.3.row_ref = f32[384,512]{1,0:T(8,128)S(1)} all-gather(f32[24,512]{1,0:T(8,128)S(1)} %copy-done.1), channel_id=1, replica_groups=mesh['z'=16,'x'=4,'y'=4,'core'=2] {'z'}, dimensions={0}, use_global_device_ids=true | all-gather | bytes 835584 | tf_op jit(solution)/shard_map/all_gather | solution.py:164
  51.4 3.7 %scores.1 = (f32[384,768]{1,0:T(8,128)S(1)}, f32[32,8,128]{2,1,0:T(8,128)}, f32[16,8,128]{2,1,0:T(8,128)}) custom-call(f32[1]{0:T(128)} %bitcast.35.scale_ref, f32[384,512]{1,0:T(8,128)S(1)} %all_gather.3.row_ref, f32[768,512]{1,0:T(8,128)S(1)} %bitcast.37, f32[1,128]{1,0:T(1,128)S(1)} %pad_bitcast_fusion.target_ref), custom_call_target="tpu_custom_call" | custom-call | tf_op jit(solution)/shard_map/scores/pallas_call | solution.py:168
  55.1 13.3 %all_to_all.20.heard_col_in = f32[32,8,128]{2,1,0:T(8,128)} all-to-all(f32[32,8,128]{2,1,0:T(8,128)} %get-tuple-element.10), channel_id=1, replica_groups=mesh['z'=16,'x'=4,'y'=4,'core'=2] {'core','x','y'}, dimensions={0} | all-to-all | bytes 262144 | tf_op jit(solution)/shard_map/all_to_all | solution.py:187
  68.4 6.8 %all-to-all-start.2 = ((f32[16,8,128]{2,1,0:T(8,128)}), f32[16,8,128]{2,1,0:T(8,128)}, u32[]{:S(2)}, u32[]{:S(2)}) async-start(f32[16,8,128]{2,1,0:T(8,128)} %get-tuple-element.13), calls=%async_computation.2 | async-start | bytes 131072 | tf_op jit(solution)/shard_map/all_to_all | solution.py:189
  75.2 13.1 %all-to-all-done.2.heard_row_in = f32[16,8,128]{2,1,0:T(8,128)} async-done(((f32[16,8,128]{2,1,0:T(8,128)}), f32[16,8,128]{2,1,0:T(8,128)}, u32[]{:S(2)}, u32[]{:S(2)}) %all-to-all-start.2) | async-done | bytes 65568 | tf_op jit(solution)/shard_map/all_to_all | solution.py:189
  88.3 3.3 %weights.1 = (f32[384,768]{1,0:T(8,128)}, f32[16,24,512]{2,1,0:T(8,128)}) custom-call(f32[1]{0:T(128)} %bitcast.36.scale_ref, f32[1]{0:T(128)} %bitcast.1.base_ref, f32[768,512]{1,0:T(8,128)S(1)} %bitcast.38, f32[384,768]{1,0:T(8,128)S(1)} %get-tuple-element.9.score_in, f32[32,8,128]{2,1,0:T(8,128)} %all_to_all.20.heard_col_in, ...), custom_call_target="tpu_custom_call" | custom-call | tf_op jit(solution)/shard_map/weights/pallas_call | solution.py:192
  91.6 3.8 %all-to-all-start.3 = ((f32[16,24,512]{2,1,0:T(8,128)}), f32[16,24,512]{2,1,0:T(8,128)S(1)}, u32[]{:S(2)}, u32[]{:S(2)}) async-start(f32[16,24,512]{2,1,0:T(8,128)} %get-tuple-element.14), calls=%async_computation.3 | async-start | bytes 1572864 | tf_op jit(solution)/shard_map/all_to_all | solution.py:212
  95.4 0.8 fusion
  96.2 1.9 %collective-permute-start = (f32[4,4,24,512]{3,2,1,0:T(8,128)S(1)}, f32[4,4,24,512]{3,2,1,0:T(8,128)}, u32[]{:S(2)}, u32[]{:S(2)}) collective-permute-start(f32[4,4,24,512]{3,2,1,0:T(8,128)S(1)} %bitcast.40), channel_id=1, source_target_pairs={{0,1},{1,0},{2,3},{3,2},{4,5},{5,4},{6,7},{7,6},{8,9},{9,8},{10,11... | collective-permute-start | bytes 2359304 | tf_op jit(solution)/shard_map/ppermute | solution.py:40
  98.2 0.8 fusion.2
  99.0 1.5 %collective-permute-done = f32[4,4,24,512]{3,2,1,0:T(8,128)} collective-permute-done((f32[4,4,24,512]{3,2,1,0:T(8,128)S(1)}, f32[4,4,24,512]{3,2,1,0:T(8,128)}, u32[]{:S(2)}, u32[]{:S(2)}) %collective-permute-start) | collective-permute-done | bytes 786464 | tf_op jit(solution)/shard_map/ppermute | solution.py:40
  100.5 1.3 add.124
  101.9 2.2 %collective-permute-start.3 = (f32[4,24,512]{2,1,0:T(8,128)S(1)}, f32[4,24,512]{2,1,0:T(8,128)S(1)}, u32[]{:S(2)}, u32[]{:S(2)}) collective-permute-start(f32[4,24,512]{2,1,0:T(8,128)S(1)} %get-tuple-element.17), channel_id=1, source_target_pairs={{0,2},{2,4},{4,6},{6,0},{1,3},{3,5},{5,7},{7,1},{8,10},{10,12},{12... | collective-permute-start | bytes 589832 | tf_op jit(solution)/shard_map/ppermute | solution.py:40
  104.1 4.4 %collective-permute-start.2 = (f32[4,24,512]{2,1,0:T(8,128)S(1)}, f32[4,24,512]{2,1,0:T(8,128)S(1)}, u32[]{:S(2)}, u32[]{:S(2)}) collective-permute-start(f32[4,24,512]{2,1,0:T(8,128)S(1)} %get-tuple-element.18), channel_id=1, source_target_pairs={{0,4},{2,6},{4,0},{6,2},{1,5},{3,7},{5,1},{7,3},{8,12},{10,14},{12... | collective-permute-start | bytes 589832 | tf_op jit(solution)/shard_map/ppermute | solution.py:40
  108.6 3.0 %collective-permute-start.1 = (f32[4,24,512]{2,1,0:T(8,128)S(1)}, f32[4,24,512]{2,1,0:T(8,128)S(1)}, u32[]{:S(2)}, u32[]{:S(2)}) collective-permute-start(f32[4,24,512]{2,1,0:T(8,128)S(1)} %get-tuple-element.16), channel_id=1, source_target_pairs={{0,6},{2,0},{4,2},{6,4},{1,7},{3,1},{5,3},{7,5},{8,14},{10,8},{12,... | collective-permute-start | bytes 589832 | tf_op jit(solution)/shard_map/ppermute | solution.py:40
  111.6 4.6 %collective-permute-done.3 = f32[4,24,512]{2,1,0:T(8,128)S(1)} collective-permute-done((f32[4,24,512]{2,1,0:T(8,128)S(1)}, f32[4,24,512]{2,1,0:T(8,128)S(1)}, u32[]{:S(2)}, u32[]{:S(2)}) %collective-permute-start.3) | collective-permute-done | bytes 196640 | tf_op jit(solution)/shard_map/ppermute | solution.py:40
  116.1 2.5 %collective-permute-done.1 = f32[4,24,512]{2,1,0:T(8,128)S(1)} collective-permute-done((f32[4,24,512]{2,1,0:T(8,128)S(1)}, f32[4,24,512]{2,1,0:T(8,128)S(1)}, u32[]{:S(2)}, u32[]{:S(2)}) %collective-permute-start.1) | collective-permute-done | bytes 196640 | tf_op jit(solution)/shard_map/ppermute | solution.py:40
  118.7 3.8 %collective-permute-start.6 = (f32[24,512]{1,0:T(8,128)S(1)}, f32[24,512]{1,0:T(8,128)S(1)}, u32[]{:S(2)}, u32[]{:S(2)}) collective-permute-start(f32[24,512]{1,0:T(8,128)S(1)} %get-tuple-element.20), channel_id=1, source_target_pairs={{0,8},{8,16},{16,24},{24,0},{1,9},{9,17},{17,25},{25,1},{2,10},{10... | collective-permute-start | bytes 147464 | tf_op jit(solution)/shard_map/ppermute | solution.py:40
  122.6 2.7 %collective-permute-start.5 = (f32[24,512]{1,0:T(8,128)S(1)}, f32[24,512]{1,0:T(8,128)S(1)}, u32[]{:S(2)}, u32[]{:S(2)}) collective-permute-start(f32[24,512]{1,0:T(8,128)S(1)} %get-tuple-element.21), channel_id=1, source_target_pairs={{0,16},{8,24},{16,0},{24,8},{1,17},{9,25},{17,1},{25,9},{2,18},{10... | collective-permute-start | bytes 147464 | tf_op jit(solution)/shard_map/ppermute | solution.py:40
  125.3 2.8 %collective-permute-start.4 = (f32[24,512]{1,0:T(8,128)S(1)}, f32[24,512]{1,0:T(8,128)S(1)}, u32[]{:S(2)}, u32[]{:S(2)}) collective-permute-start(f32[24,512]{1,0:T(8,128)S(1)} %get-tuple-element.19), channel_id=1, source_target_pairs={{0,24},{8,0},{16,8},{24,16},{1,25},{9,1},{17,9},{25,17},{2,26},{10... | collective-permute-start | bytes 147464 | tf_op jit(solution)/shard_map/ppermute | solution.py:40
  128.1 2.4 %collective-permute-done.5 = f32[24,512]{1,0:T(8,128)S(1)} collective-permute-done((f32[24,512]{1,0:T(8,128)S(1)}, f32[24,512]{1,0:T(8,128)S(1)}, u32[]{:S(2)}, u32[]{:S(2)}) %collective-permute-start.5) | collective-permute-done | bytes 49184 | tf_op jit(solution)/shard_map/ppermute | solution.py:40
  130.5 2.0 %collective-permute-done.4 = f32[24,512]{1,0:T(8,128)S(1)} collective-permute-done((f32[24,512]{1,0:T(8,128)S(1)}, f32[24,512]{1,0:T(8,128)S(1)}, u32[]{:S(2)}, u32[]{:S(2)}) %collective-permute-start.4) | collective-permute-done | bytes 49184 | tf_op jit(solution)/shard_map/ppermute | solution.py:40
  (17 shorter events, 1.8 us)
Async XLA Ops:
  2.9 10.4 %copy-start.2 = (s32[24]{0:T(128)S(1)}, s32[24]{0:T(128)}, u32[]{:S(2)}) copy-start(s32[24]{0:T(128)} %param.7) | copy-start | bytes 292
  2.9 10.4 %copy-start.1 = (f32[24,512]{1,0:T(8,128)S(1)}, f32[24,512]{1,0:T(8,128)}, u32[]{:S(2)}) copy-start(f32[24,512]{1,0:T(8,128)} %param.4) | copy-start | bytes 147460
  2.9 48.5 %all-to-all-start = ((f32[32,24,512]{2,1,0:T(8,128)}), f32[32,24,512]{2,1,0:T(8,128)S(1)}, u32[]{:S(2)}, u32[]{:S(2)}) async-start(f32[32,24,512]{2,1,0:T(8,128)} %repeat.1), calls=%async_computation | async-start | bytes 3145728 | tf_op jit(solution)/shard_map/all_to_all | solution.py:36
  68.4 19.9 %all-to-all-start.2 = ((f32[16,8,128]{2,1,0:T(8,128)}), f32[16,8,128]{2,1,0:T(8,128)}, u32[]{:S(2)}, u32[]{:S(2)}) async-start(f32[16,8,128]{2,1,0:T(8,128)} %get-tuple-element.13), calls=%async_computation.2 | async-start | bytes 131072 | tf_op jit(solution)/shard_map/all_to_all | solution.py:189
  91.6 3.8 %copy-start = (f32[384,768]{1,0:T(8,128)S(1)}, f32[384,768]{1,0:T(8,128)}, u32[]{:S(2)}) copy-start(f32[384,768]{1,0:T(8,128)} %get-tuple-element.15) | copy-start | bytes 3538948
  91.6 41.8 %all-to-all-start.3 = ((f32[16,24,512]{2,1,0:T(8,128)}), f32[16,24,512]{2,1,0:T(8,128)S(1)}, u32[]{:S(2)}, u32[]{:S(2)}) async-start(f32[16,24,512]{2,1,0:T(8,128)} %get-tuple-element.14), calls=%async_computation.3 | async-start | bytes 1572864 | tf_op jit(solution)/shard_map/all_to_all | solution.py:212
  96.2 4.3 %collective-permute-start = (f32[4,4,24,512]{3,2,1,0:T(8,128)S(1)}, f32[4,4,24,512]{3,2,1,0:T(8,128)}, u32[]{:S(2)}, u32[]{:S(2)}) collective-permute-start(f32[4,4,24,512]{3,2,1,0:T(8,128)S(1)} %bitcast.40), channel_id=1, source_target_pairs={{0,1},{1,0},{2,3},{3,2},{4,5},{5,4},{6,7},{7,6},{8,9},{9,8},{10,11... | collective-permute-start | bytes 2359304 | tf_op jit(solution)/shard_map/ppermute | solution.py:40
  101.9 14.3 %collective-permute-start.3 = (f32[4,24,512]{2,1,0:T(8,128)S(1)}, f32[4,24,512]{2,1,0:T(8,128)S(1)}, u32[]{:S(2)}, u32[]{:S(2)}) collective-permute-start(f32[4,24,512]{2,1,0:T(8,128)S(1)} %get-tuple-element.17), channel_id=1, source_target_pairs={{0,2},{2,4},{4,6},{6,0},{1,3},{3,5},{5,7},{7,1},{8,10},{10,12},{12... | collective-permute-start | bytes 589832 | tf_op jit(solution)/shard_map/ppermute | solution.py:40
  104.1 12.0 %collective-permute-start.2 = (f32[4,24,512]{2,1,0:T(8,128)S(1)}, f32[4,24,512]{2,1,0:T(8,128)S(1)}, u32[]{:S(2)}, u32[]{:S(2)}) collective-permute-start(f32[4,24,512]{2,1,0:T(8,128)S(1)} %get-tuple-element.18), channel_id=1, source_target_pairs={{0,4},{2,6},{4,0},{6,2},{1,5},{3,7},{5,1},{7,3},{8,12},{10,14},{12... | collective-permute-start | bytes 589832 | tf_op jit(solution)/shard_map/ppermute | solution.py:40
  108.6 10.1 %collective-permute-start.1 = (f32[4,24,512]{2,1,0:T(8,128)S(1)}, f32[4,24,512]{2,1,0:T(8,128)S(1)}, u32[]{:S(2)}, u32[]{:S(2)}) collective-permute-start(f32[4,24,512]{2,1,0:T(8,128)S(1)} %get-tuple-element.16), channel_id=1, source_target_pairs={{0,6},{2,0},{4,2},{6,4},{1,7},{3,1},{5,3},{7,5},{8,14},{10,8},{12,... | collective-permute-start | bytes 589832 | tf_op jit(solution)/shard_map/ppermute | solution.py:40
  118.7 9.4 %collective-permute-start.6 = (f32[24,512]{1,0:T(8,128)S(1)}, f32[24,512]{1,0:T(8,128)S(1)}, u32[]{:S(2)}, u32[]{:S(2)}) collective-permute-start(f32[24,512]{1,0:T(8,128)S(1)} %get-tuple-element.20), channel_id=1, source_target_pairs={{0,8},{8,16},{16,24},{24,0},{1,9},{9,17},{17,25},{25,1},{2,10},{10... | collective-permute-start | bytes 147464 | tf_op jit(solution)/shard_map/ppermute | solution.py:40
  122.6 7.9 %collective-permute-start.5 = (f32[24,512]{1,0:T(8,128)S(1)}, f32[24,512]{1,0:T(8,128)S(1)}, u32[]{:S(2)}, u32[]{:S(2)}) collective-permute-start(f32[24,512]{1,0:T(8,128)S(1)} %get-tuple-element.21), channel_id=1, source_target_pairs={{0,16},{8,24},{16,0},{24,8},{1,17},{9,25},{17,1},{25,9},{2,18},{10... | collective-permute-start | bytes 147464 | tf_op jit(solution)/shard_map/ppermute | solution.py:40
  125.3 7.2 %collective-permute-start.4 = (f32[24,512]{1,0:T(8,128)S(1)}, f32[24,512]{1,0:T(8,128)S(1)}, u32[]{:S(2)}, u32[]{:S(2)}) collective-permute-start(f32[24,512]{1,0:T(8,128)S(1)} %get-tuple-element.19), channel_id=1, source_target_pairs={{0,24},{8,0},{16,8},{24,16},{1,25},{9,1},{17,9},{25,17},{2,26},{10... | collective-permute-start | bytes 147464 | tf_op jit(solution)/shard_map/ppermute | solution.py:40

commit v11 on v10

--- a/solution.py
+++ b/solution.py
@@ -71,7 +71,6 @@
         lse = jnp.transpose(jnp.broadcast_to(lse, (LANES, LANES)))[:1]
         row_part[:, k, :] = jnp.broadcast_to(lse, (row_part.shape[0], LANES))
     row_part[:, used, :] = jnp.broadcast_to(target_ref[...], (row_part.shape[0], LANES))
-    row_part[:, used + 1:, :] = jnp.zeros_like(row_part[:, used + 1:, :])
     stores[1].start()
     top = jnp.max(scores, axis=0, keepdims=True)
     lse = top + jnp.log(jnp.sum(jnp.exp(scores - top), axis=0, keepdims=True))
@@ -95,13 +94,13 @@
 
 
 def weight_kernel(
-    scale_ref, base_ref, col_ref, score_in, heard_col_in, heard_row_in,
-    weight_out, grad_out, score_ref, heard_col_ref, heard_row_ref, weight_ref, grad_ref, sems, out_sems,
+    scale_ref, base_ref, col_ref, score_ref, heard_col_in, heard_row_in,
+    weight_out, grad_out, heard_col_ref, heard_row_ref, weight_ref, grad_ref, sems, out_sems,
 ):
     fetches = [
         pltpu.make_async_copy(source, target, sems.at[k])
         for k, (source, target) in enumerate(
-            ((heard_row_in, heard_row_ref), (heard_col_in, heard_col_ref), (score_in, score_ref))
+            ((heard_row_in, heard_row_ref), (heard_col_in, heard_col_ref))
         )
     ]
     for fetch in fetches:
@@ -170,14 +169,14 @@
         out_shape=(
             jax.ShapeDtypeStruct((row_count, col_count), jnp.float32),
             pltpu.HBM((PLANE, 8, LANES), jnp.float32),
-            pltpu.HBM((Z, 8, LANES), jnp.float32),
+            pltpu.HBM((Z, 4, LANES), jnp.float32),
         ),
         in_specs=[SMEM, VMEM, VMEM, VMEM],
         out_specs=(ANY, HBM, HBM),
         scratch_shapes=[
             pltpu.VMEM((row_count, col_count), jnp.float32),
             pltpu.VMEM((PLANE, 8, LANES), jnp.float32),
-            pltpu.VMEM((Z, 8, LANES), jnp.float32),
+            pltpu.VMEM((Z, 4, LANES), jnp.float32),
             pltpu.SemaphoreType.DMA((3,)),
         ],
         compiler_params=PARAMS,
@@ -195,15 +194,14 @@
             pltpu.HBM((row_count, col_count), jnp.float32),
             pltpu.HBM((Z, own, width), jnp.float32),
         ),
-        in_specs=[SMEM, SMEM, VMEM, ANY, ANY, ANY],
+        in_specs=[SMEM, SMEM, VMEM, VMEM, ANY, ANY],
         out_specs=(HBM, HBM),
         scratch_shapes=[
-            pltpu.VMEM((row_count, col_count), jnp.float32),
             pltpu.VMEM((PLANE, 8, LANES), jnp.float32),
-            pltpu.VMEM((Z, 8, LANES), jnp.float32),
+            pltpu.VMEM((Z, 4, LANES), jnp.float32),
             pltpu.VMEM((row_count, col_count), jnp.float32),
             pltpu.VMEM((Z, own, width), jnp.float32),
-            pltpu.SemaphoreType.DMA((3,)),
+            pltpu.SemaphoreType.DMA((2,)),
             pltpu.SemaphoreType.DMA((2, 2)),
         ],
         compiler_params=PARAMS,

time: 136 us -> 136 us (level)
  transfers between devices with their start and end apart: 10 -> 10, of which waited for: 7 -> 6; matrix products, arithmetic and copies ran while one was open for 3% -> 3% of each run, Pallas kernels for 0% -> 0%
where the time goes in v11:
time: 136 us; the launch traced here: 134 us
  blocking collectives  51.4 us (38%)
  starting transfers between devices  41.2 us (30%)
  waiting for transfers between devices  25.8 us (19%)
  Pallas kernels  9.16 us (7%)
  other arithmetic  2.64 us (2%)
  matrix products  1.69 us (1%)
  between operations  1.63 us (1%)
    all_gather x1, blocking collectives, local(): rows = lax.all_gather(row_embed, 'z', axis=0, tiled=True)  38.1 us
    ppermute x7, starting transfers between devices, shift(): lax.ppermute(block, axis, [(i, (i + by) % count) for i in range(count)])  20.9 us
    all_to_all x1, blocking collectives, local(): lax.all_to_all(col_message, ('core', 'x', 'y'), 0, 0, tiled=True)  13.3 us
    ppermute x7, waiting for transfers between devices, shift(): lax.ppermute(block, axis, [(i, (i + by) % count) for i in range(count)])  13.2 us
    all_to_all x1, waiting for transfers between devices, local(): heard_row = lax.all_to_all(row_message, 'z', 0, 0, tiled=True)  12.6 us
    all_to_all x1, starting transfers between devices, to_all(): return lax.all_to_all(sent, axes, 0, 0, tiled=True)  9.69 us
    all_to_all x1, starting transfers between devices, local(): heard_row = lax.all_to_all(row_message, 'z', 0, 0, tiled=True)  6.83 us
    all_to_all x1, starting transfers between devices, local(): row_parts = lax.all_to_all(grad_rows, 'z', 0, 0, tiled=True)  3.76 us
  transfers between devices with their start and end apart: 10, of which 6 were waited for; matrix products, arithmetic and copies ran while one was open for 3% of the time, Pallas kernels for 0%

profile of v11, /device:TPU:6, one launch (start us, length us, event | category | flops | bytes accessed | tf_op | source)
XLA Modules:
  0.0 133.6 jit_solution(6390054723659598660)
XLA Ops:
  0.6 2.3 %repeat.1 = f32[32,24,512]{2,1,0:T(8,128)} custom-call(f32[24,512]{1,0:T(8,128)} %block_ref.1), custom_call_target="tpu_custom_call" | custom-call | tf_op jit(solution)/shard_map/repeat/pallas_call | solution.py:28
  2.9 9.7 %all-to-all-start = ((f32[32,24,512]{2,1,0:T(8,128)}), f32[32,24,512]{2,1,0:T(8,128)S(1)}, u32[]{:S(2)}, u32[]{:S(2)}) async-start(f32[32,24,512]{2,1,0:T(8,128)} %repeat.1), calls=%async_computation | async-start | bytes 3145728 | tf_op jit(solution)/shard_map/all_to_all | solution.py:36
  13.3 38.1 %all_gather.3.row_ref = f32[384,512]{1,0:T(8,128)S(1)} all-gather(f32[24,512]{1,0:T(8,128)S(1)} %copy-done.1), channel_id=1, replica_groups=mesh['z'=16,'x'=4,'y'=4,'core'=2] {'z'}, dimensions={0}, use_global_device_ids=true | all-gather | bytes 835584 | tf_op jit(solution)/shard_map/all_gather | solution.py:163
  51.4 3.6 %scores.1 = (f32[384,768]{1,0:T(8,128)S(1)}, f32[32,8,128]{2,1,0:T(8,128)}, f32[16,4,128]{2,1,0:T(4,128)}) custom-call(f32[1]{0:T(128)} %bitcast.35.scale_ref, f32[384,512]{1,0:T(8,128)S(1)} %all_gather.3.row_ref, f32[768,512]{1,0:T(8,128)S(1)} %bitcast.37, f32[1,128]{1,0:T(1,128)S(1)} %pad_bitcast_fusion.target_ref), custom_call_target="tpu_custom_call" | custom-call | tf_op jit(solution)/shard_map/scores/pallas_call | solution.py:167
  55.1 13.3 %all_to_all.20.heard_col_in = f32[32,8,128]{2,1,0:T(8,128)} all-to-all(f32[32,8,128]{2,1,0:T(8,128)} %get-tuple-element.10), channel_id=1, replica_groups=mesh['z'=16,'x'=4,'y'=4,'core'=2] {'core','x','y'}, dimensions={0} | all-to-all | bytes 262144 | tf_op jit(solution)/shard_map/all_to_all | solution.py:186
  68.4 6.8 %all-to-all-start.2 = ((f32[16,4,128]{2,1,0:T(4,128)}), f32[16,4,128]{2,1,0:T(4,128)}, u32[]{:S(2)}, u32[]{:S(2)}) async-start(f32[16,4,128]{2,1,0:T(4,128)} %get-tuple-element.13), calls=%async_computation.2 | async-start | bytes 65536 | tf_op jit(solution)/shard_map/all_to_all | solution.py:188
  75.2 12.6 %all-to-all-done.2.heard_row_in = f32[16,4,128]{2,1,0:T(4,128)} async-done(((f32[16,4,128]{2,1,0:T(4,128)}), f32[16,4,128]{2,1,0:T(4,128)}, u32[]{:S(2)}, u32[]{:S(2)}) %all-to-all-start.2) | async-done | bytes 32800 | tf_op jit(solution)/shard_map/all_to_all | solution.py:188
  87.8 3.3 %weights.1 = (f32[384,768]{1,0:T(8,128)}, f32[16,24,512]{2,1,0:T(8,128)}) custom-call(f32[1]{0:T(128)} %bitcast.36.scale_ref, f32[1]{0:T(128)} %bitcast.1.base_ref, f32[768,512]{1,0:T(8,128)S(1)} %bitcast.38, f32[384,768]{1,0:T(8,128)S(1)} %get-tuple-element.9.score_ref, f32[32,8,128]{2,1,0:T(8,128)} %all_to_all.20.heard_col_in, ...), custom_call_target="tpu_custom_call" | custom-call | tf_op jit(solution)/shard_map/weights/pallas_call | solution.py:191
  91.1 3.8 %all-to-all-start.3 = ((f32[16,24,512]{2,1,0:T(8,128)}), f32[16,24,512]{2,1,0:T(8,128)S(1)}, u32[]{:S(2)}, u32[]{:S(2)}) async-start(f32[16,24,512]{2,1,0:T(8,128)} %get-tuple-element.14), calls=%async_computation.3 | async-start | bytes 1572864 | tf_op jit(solution)/shard_map/all_to_all | solution.py:210
  94.9 0.9 fusion
  95.7 1.9 %collective-permute-start = (f32[4,4,24,512]{3,2,1,0:T(8,128)S(1)}, f32[4,4,24,512]{3,2,1,0:T(8,128)}, u32[]{:S(2)}, u32[]{:S(2)}) collective-permute-start(f32[4,4,24,512]{3,2,1,0:T(8,128)S(1)} %bitcast.40), channel_id=1, source_target_pairs={{0,1},{1,0},{2,3},{3,2},{4,5},{5,4},{6,7},{7,6},{8,9},{9,8},{10,11... | collective-permute-start | bytes 2359304 | tf_op jit(solution)/shard_map/ppermute | solution.py:40
  97.7 0.8 fusion.2
  98.5 1.5 %collective-permute-done = f32[4,4,24,512]{3,2,1,0:T(8,128)} collective-permute-done((f32[4,4,24,512]{3,2,1,0:T(8,128)S(1)}, f32[4,4,24,512]{3,2,1,0:T(8,128)}, u32[]{:S(2)}, u32[]{:S(2)}) %collective-permute-start) | collective-permute-done | bytes 786464 | tf_op jit(solution)/shard_map/ppermute | solution.py:40
  100.0 1.3 add.124
  101.4 2.2 %collective-permute-start.3 = (f32[4,24,512]{2,1,0:T(8,128)S(1)}, f32[4,24,512]{2,1,0:T(8,128)S(1)}, u32[]{:S(2)}, u32[]{:S(2)}) collective-permute-start(f32[4,24,512]{2,1,0:T(8,128)S(1)} %get-tuple-element.17), channel_id=1, source_target_pairs={{0,2},{2,4},{4,6},{6,0},{1,3},{3,5},{5,7},{7,1},{8,10},{10,12},{12... | collective-permute-start | bytes 589832 | tf_op jit(solution)/shard_map/ppermute | solution.py:40
  103.6 4.4 %collective-permute-start.2 = (f32[4,24,512]{2,1,0:T(8,128)S(1)}, f32[4,24,512]{2,1,0:T(8,128)S(1)}, u32[]{:S(2)}, u32[]{:S(2)}) collective-permute-start(f32[4,24,512]{2,1,0:T(8,128)S(1)} %get-tuple-element.18), channel_id=1, source_target_pairs={{0,4},{2,6},{4,0},{6,2},{1,5},{3,7},{5,1},{7,3},{8,12},{10,14},{12... | collective-permute-start | bytes 589832 | tf_op jit(solution)/shard_map/ppermute | solution.py:40
  108.1 3.0 %collective-permute-start.1 = (f32[4,24,512]{2,1,0:T(8,128)S(1)}, f32[4,24,512]{2,1,0:T(8,128)S(1)}, u32[]{:S(2)}, u32[]{:S(2)}) collective-permute-start(f32[4,24,512]{2,1,0:T(8,128)S(1)} %get-tuple-element.16), channel_id=1, source_target_pairs={{0,6},{2,0},{4,2},{6,4},{1,7},{3,1},{5,3},{7,5},{8,14},{10,8},{12,... | collective-permute-start | bytes 589832 | tf_op jit(solution)/shard_map/ppermute | solution.py:40
  111.1 4.5 %collective-permute-done.3 = f32[4,24,512]{2,1,0:T(8,128)S(1)} collective-permute-done((f32[4,24,512]{2,1,0:T(8,128)S(1)}, f32[4,24,512]{2,1,0:T(8,128)S(1)}, u32[]{:S(2)}, u32[]{:S(2)}) %collective-permute-start.3) | collective-permute-done | bytes 196640 | tf_op jit(solution)/shard_map/ppermute | solution.py:40
  115.6 2.5 %collective-permute-done.1 = f32[4,24,512]{2,1,0:T(8,128)S(1)} collective-permute-done((f32[4,24,512]{2,1,0:T(8,128)S(1)}, f32[4,24,512]{2,1,0:T(8,128)S(1)}, u32[]{:S(2)}, u32[]{:S(2)}) %collective-permute-start.1) | collective-permute-done | bytes 196640 | tf_op jit(solution)/shard_map/ppermute | solution.py:40
  118.2 4.1 %collective-permute-start.6 = (f32[24,512]{1,0:T(8,128)S(1)}, f32[24,512]{1,0:T(8,128)S(1)}, u32[]{:S(2)}, u32[]{:S(2)}) collective-permute-start(f32[24,512]{1,0:T(8,128)S(1)} %get-tuple-element.20), channel_id=1, source_target_pairs={{0,8},{8,16},{16,24},{24,0},{1,9},{9,17},{17,25},{25,1},{2,10},{10... | collective-permute-start | bytes 147464 | tf_op jit(solution)/shard_map/ppermute | solution.py:40
  122.3 2.8 %collective-permute-start.5 = (f32[24,512]{1,0:T(8,128)S(1)}, f32[24,512]{1,0:T(8,128)S(1)}, u32[]{:S(2)}, u32[]{:S(2)}) collective-permute-start(f32[24,512]{1,0:T(8,128)S(1)} %get-tuple-element.21), channel_id=1, source_target_pairs={{0,16},{8,24},{16,0},{24,8},{1,17},{9,25},{17,1},{25,9},{2,18},{10... | collective-permute-start | bytes 147464 | tf_op jit(solution)/shard_map/ppermute | solution.py:40
  125.1 2.5 %collective-permute-start.4 = (f32[24,512]{1,0:T(8,128)S(1)}, f32[24,512]{1,0:T(8,128)S(1)}, u32[]{:S(2)}, u32[]{:S(2)}) collective-permute-start(f32[24,512]{1,0:T(8,128)S(1)} %get-tuple-element.19), channel_id=1, source_target_pairs={{0,24},{8,0},{16,8},{24,16},{1,25},{9,1},{17,9},{25,17},{2,26},{10... | collective-permute-start | bytes 147464 | tf_op jit(solution)/shard_map/ppermute | solution.py:40
  127.6 2.6 %collective-permute-done.5 = f32[24,512]{1,0:T(8,128)S(1)} collective-permute-done((f32[24,512]{1,0:T(8,128)S(1)}, f32[24,512]{1,0:T(8,128)S(1)}, u32[]{:S(2)}, u32[]{:S(2)}) %collective-permute-start.5) | collective-permute-done | bytes 49184 | tf_op jit(solution)/shard_map/ppermute | solution.py:40
  130.3 2.1 %collective-permute-done.4 = f32[24,512]{1,0:T(8,128)S(1)} collective-permute-done((f32[24,512]{1,0:T(8,128)S(1)}, f32[24,512]{1,0:T(8,128)S(1)}, u32[]{:S(2)}, u32[]{:S(2)}) %collective-permute-start.4) | collective-permute-done | bytes 49184 | tf_op jit(solution)/shard_map/ppermute | solution.py:40
  (17 shorter events, 1.5 us)
Async XLA Ops:
  2.9 10.4 %copy-start.2 = (s32[24]{0:T(128)S(1)}, s32[24]{0:T(128)}, u32[]{:S(2)}) copy-start(s32[24]{0:T(128)} %param.7) | copy-start | bytes 292
  2.9 10.4 %copy-start.1 = (f32[24,512]{1,0:T(8,128)S(1)}, f32[24,512]{1,0:T(8,128)}, u32[]{:S(2)}) copy-start(f32[24,512]{1,0:T(8,128)} %param.4) | copy-start | bytes 147460
  2.9 48.5 %all-to-all-start = ((f32[32,24,512]{2,1,0:T(8,128)}), f32[32,24,512]{2,1,0:T(8,128)S(1)}, u32[]{:S(2)}, u32[]{:S(2)}) async-start(f32[32,24,512]{2,1,0:T(8,128)} %repeat.1), calls=%async_computation | async-start | bytes 3145728 | tf_op jit(solution)/shard_map/all_to_all | solution.py:36
  68.4 19.5 %all-to-all-start.2 = ((f32[16,4,128]{2,1,0:T(4,128)}), f32[16,4,128]{2,1,0:T(4,128)}, u32[]{:S(2)}, u32[]{:S(2)}) async-start(f32[16,4,128]{2,1,0:T(4,128)} %get-tuple-element.13), calls=%async_computation.2 | async-start | bytes 65536 | tf_op jit(solution)/shard_map/all_to_all | solution.py:188
  91.1 3.8 %copy-start = (f32[384,768]{1,0:T(8,128)S(1)}, f32[384,768]{1,0:T(8,128)}, u32[]{:S(2)}) copy-start(f32[384,768]{1,0:T(8,128)} %get-tuple-element.15) | copy-start | bytes 3538948
  91.1 41.9 %all-to-all-start.3 = ((f32[16,24,512]{2,1,0:T(8,128)}), f32[16,24,512]{2,1,0:T(8,128)S(1)}, u32[]{:S(2)}, u32[]{:S(2)}) async-start(f32[16,24,512]{2,1,0:T(8,128)} %get-tuple-element.14), calls=%async_computation.3 | async-start | bytes 1572864 | tf_op jit(solution)/shard_map/all_to_all | solution.py:210
  95.7 4.3 %collective-permute-start = (f32[4,4,24,512]{3,2,1,0:T(8,128)S(1)}, f32[4,4,24,512]{3,2,1,0:T(8,128)}, u32[]{:S(2)}, u32[]{:S(2)}) collective-permute-start(f32[4,4,24,512]{3,2,1,0:T(8,128)S(1)} %bitcast.40), channel_id=1, source_target_pairs={{0,1},{1,0},{2,3},{3,2},{4,5},{5,4},{6,7},{7,6},{8,9},{9,8},{10,11... | collective-permute-start | bytes 2359304 | tf_op jit(solution)/shard_map/ppermute | solution.py:40
  101.4 14.3 %collective-permute-start.3 = (f32[4,24,512]{2,1,0:T(8,128)S(1)}, f32[4,24,512]{2,1,0:T(8,128)S(1)}, u32[]{:S(2)}, u32[]{:S(2)}) collective-permute-start(f32[4,24,512]{2,1,0:T(8,128)S(1)} %get-tuple-element.17), channel_id=1, source_target_pairs={{0,2},{2,4},{4,6},{6,0},{1,3},{3,5},{5,7},{7,1},{8,10},{10,12},{12... | collective-permute-start | bytes 589832 | tf_op jit(solution)/shard_map/ppermute | solution.py:40
  103.6 12.0 %collective-permute-start.2 = (f32[4,24,512]{2,1,0:T(8,128)S(1)}, f32[4,24,512]{2,1,0:T(8,128)S(1)}, u32[]{:S(2)}, u32[]{:S(2)}) collective-permute-start(f32[4,24,512]{2,1,0:T(8,128)S(1)} %get-tuple-element.18), channel_id=1, source_target_pairs={{0,4},{2,6},{4,0},{6,2},{1,5},{3,7},{5,1},{7,3},{8,12},{10,14},{12... | collective-permute-start | bytes 589832 | tf_op jit(solution)/shard_map/ppermute | solution.py:40
  108.1 10.1 %collective-permute-start.1 = (f32[4,24,512]{2,1,0:T(8,128)S(1)}, f32[4,24,512]{2,1,0:T(8,128)S(1)}, u32[]{:S(2)}, u32[]{:S(2)}) collective-permute-start(f32[4,24,512]{2,1,0:T(8,128)S(1)} %get-tuple-element.16), channel_id=1, source_target_pairs={{0,6},{2,0},{4,2},{6,4},{1,7},{3,1},{5,3},{7,5},{8,14},{10,8},{12,... | collective-permute-start | bytes 589832 | tf_op jit(solution)/shard_map/ppermute | solution.py:40
  118.2 9.4 %collective-permute-start.6 = (f32[24,512]{1,0:T(8,128)S(1)}, f32[24,512]{1,0:T(8,128)S(1)}, u32[]{:S(2)}, u32[]{:S(2)}) collective-permute-start(f32[24,512]{1,0:T(8,128)S(1)} %get-tuple-element.20), channel_id=1, source_target_pairs={{0,8},{8,16},{16,24},{24,0},{1,9},{9,17},{17,25},{25,1},{2,10},{10... | collective-permute-start | bytes 147464 | tf_op jit(solution)/shard_map/ppermute | solution.py:40
  122.3 8.0 %collective-permute-start.5 = (f32[24,512]{1,0:T(8,128)S(1)}, f32[24,512]{1,0:T(8,128)S(1)}, u32[]{:S(2)}, u32[]{:S(2)}) collective-permute-start(f32[24,512]{1,0:T(8,128)S(1)} %get-tuple-element.21), channel_id=1, source_target_pairs={{0,16},{8,24},{16,0},{24,8},{1,17},{9,25},{17,1},{25,9},{2,18},{10... | collective-permute-start | bytes 147464 | tf_op jit(solution)/shard_map/ppermute | solution.py:40
  125.1 7.2 %collective-permute-start.4 = (f32[24,512]{1,0:T(8,128)S(1)}, f32[24,512]{1,0:T(8,128)S(1)}, u32[]{:S(2)}, u32[]{:S(2)}) collective-permute-start(f32[24,512]{1,0:T(8,128)S(1)} %get-tuple-element.19), channel_id=1, source_target_pairs={{0,24},{8,0},{16,8},{24,16},{1,25},{9,1},{17,9},{25,17},{2,26},{10... | collective-permute-start | bytes 147464 | tf_op jit(solution)/shard_map/ppermute | solution.py:40

commit v12 on v11

--- a/solution.py
+++ b/solution.py
@@ -93,34 +93,15 @@
     return top + jnp.log(jnp.sum(jnp.exp(heard - top[None]), axis=0))
 
 
-def weight_kernel(
-    scale_ref, base_ref, col_ref, score_ref, heard_col_in, heard_row_in,
-    weight_out, grad_out, heard_col_ref, heard_row_ref, weight_ref, grad_ref, sems, out_sems,
-):
-    fetches = [
-        pltpu.make_async_copy(source, target, sems.at[k])
-        for k, (source, target) in enumerate(
-            ((heard_row_in, heard_row_ref), (heard_col_in, heard_col_ref))
-        )
-    ]
-    for fetch in fetches:
-        fetch.start()
-    row_count, col_count = score_ref.shape
-    own = grad_ref.shape[1]
-    col_high, col_low = split(col_ref[...])
-    place = lax.broadcasted_iota(jnp.int32, (own, col_count), 1)
-    half = col_count // CORE
-    place_core = (place >= half).astype(jnp.int32)
-    place = place - place_core * half
-    chip = jnp.zeros_like(place)
-    for k in range(1, PLANE // CORE):
-        chip = chip + (place >= k * own).astype(jnp.int32)
-    ids = (place + (chip + place_core) * own).astype(jnp.float32)
-    base = base_ref[0]
-    for fetch in fetches:
-        fetch.wait()
-    col_lse = combined(heard_col_ref[...])
-    col_lse = jnp.concatenate([col_lse[k:k + 1] for k in range(col_count // LANES)], axis=1)
+def fetched(pairs, sems):
+    copies = [pltpu.make_async_copy(source, target, sems.at[k]) for k, (source, target) in enumerate(pairs)]
+    for copy in copies:
+        copy.start()
+    for copy in copies:
+        copy.wait()
+
+
+def row_facts(heard_row_ref, row_count):
     row_lse = combined(heard_row_ref[...])
     row_lse = jnp.concatenate(
         [jnp.transpose(jnp.broadcast_to(row_lse[k:k + 1], (LANES, LANES))) for k in range(row_count // LANES)], axis=0
@@ -128,20 +109,44 @@
     targets = jnp.transpose(
         jnp.concatenate([heard_row_ref[:, row_count // LANES, :], jnp.zeros((LANES - Z, LANES), jnp.float32)], axis=0)
     )
+    return row_lse, targets
+
+
+def column_ids(own, of_core):
+    place = lax.broadcasted_iota(jnp.int32, (own, PLANE // CORE * own), 1)
+    chip = jnp.zeros_like(place)
+    for k in range(1, PLANE // CORE):
+        chip = chip + (place >= k * own).astype(jnp.int32)
+    return (place + (chip + of_core) * own).astype(jnp.float32)
+
+
+def weigh(scores, row_lse, col_lse, targets, ids):
+    return (
+        0.5 * jnp.exp(scores - row_lse)
+        + 0.5 * jnp.exp(scores - col_lse)
+        - jnp.where(targets == ids, 1.0, 0.0)
+    )
+
+
+def row_kernel(
+    scale_ref, base_ref, col_ref, score_ref, heard_col_in, heard_row_in,
+    grad_out, heard_col_ref, heard_row_ref, weight_ref, grad_ref, sems, out_sems,
+):
+    row_count, col_count = score_ref.shape
+    own = grad_ref.shape[1]
+    fetched(((heard_row_in, heard_row_ref), (heard_col_in, heard_col_ref)), sems)
+    col_high, col_low = split(col_ref[...])
+    ids = jnp.concatenate([column_ids(own, c) for c in range(CORE)], axis=1)
+    col_lse = combined(heard_col_ref[...])
+    col_lse = jnp.concatenate([col_lse[k:k + 1] for k in range(col_count // LANES)], axis=1)
+    row_lse, targets = row_facts(heard_row_ref, row_count)
+    base = base_ref[0]
     stores = []
     for part in range(2):
         first, count = part * Z // 2, Z // 2
         for z in range(first, first + count):
             here = slice(z * own, (z + 1) * own)
-            scores = score_ref[here, :]
-            weight_ref[here, :] = (
-                0.5 * jnp.exp(scores - row_lse[here])
-                + 0.5 * jnp.exp(scores - col_lse)
-                - jnp.where(targets[:own, z:z + 1] - base == ids, 1.0, 0.0)
-            )
-        here = pl.ds(first * own, count * own)
-        stores.append(pltpu.make_async_copy(weight_ref.at[here], weight_out.at[here], out_sems.at[0, part]))
-        stores[-1].start()
+            weight_ref[here, :] = weigh(score_ref[here, :], row_lse[here], col_lse, targets[:own, z:z + 1] - base, ids)
         high, low = split(weight_ref[first * own:(first + count) * own, :])
         total = None
         for left, right in ((high, col_high), (high, col_low), (low, col_high)):
@@ -149,10 +154,40 @@
             total = term if total is None else total + term
         here = pl.ds(first, count)
         grad_ref[here] = (scale_ref[0] * total).reshape(count, own, total.shape[1])
-        stores.append(pltpu.make_async_copy(grad_ref.at[here], grad_out.at[here], out_sems.at[1, part]))
+        stores.append(pltpu.make_async_copy(grad_ref.at[here], grad_out.at[here], out_sems.at[part]))
         stores[-1].start()
     for store in stores:
         store.wait()
+
+
+def col_kernel(
+    scale_ref, base_ref, core_ref, row_ref, score_ref, heard_col_in, heard_row_in,
+    grad_out, heard_col_ref, heard_row_ref, lse_ref, weight_ref, grad_ref, sems,
+):
+    row_count, half = weight_ref.shape
+    own = grad_ref.shape[1]
+    fetched(((heard_row_in, heard_row_ref), (heard_col_in, heard_col_ref)), sems)
+    of_core = core_ref[0]
+    row_high, row_low = split(row_ref[...])
+    ids = column_ids(own, of_core)
+    lse_ref[...] = combined(heard_col_ref[...])
+    used = half // LANES
+    col_lse = jnp.concatenate([lse_ref[pl.ds(of_core * used + k, 1), :] for k in range(used)], axis=1)
+    row_lse, targets = row_facts(heard_row_ref, row_count)
+    base = base_ref[0]
+    there = pl.ds(pl.multiple_of(of_core * half, LANES), half)
+    for z in range(Z):
+        here = slice(z * own, (z + 1) * own)
+        weight_ref[here, :] = weigh(score_ref[here, there], row_lse[here], col_lse, targets[:own, z:z + 1] - base, ids)
+    high, low = split(weight_ref[...])
+    total = None
+    for left, right in ((high, row_high), (high, row_low), (low, row_high)):
+        term = lax.dot_general(left, right, (((0,), (0,)), ((), ())), preferred_element_type=jnp.float32)
+        total = term if total is None else total + term
+    grad_ref[...] = (scale_ref[0] * total).reshape(grad_ref.shape)
+    store = pltpu.make_async_copy(grad_ref, grad_out, sems.at[2])
+    store.start()
+    store.wait()
 
 
 def local(row_embed, col_embed, logit_scale, targets):
@@ -188,38 +223,45 @@
     heard_row = lax.all_to_all(row_message, "z", 0, 0, tiled=True)
     heard_col = pltpu.with_memory_space_constraint(heard_col, pltpu.HBM)
 
-    weights, grad_rows = pl.pallas_call(
-        weight_kernel,
-        out_shape=(
-            pltpu.HBM((row_count, col_count), jnp.float32),
-            pltpu.HBM((Z, own, width), jnp.float32),
-        ),
+    base = (plane * col_count).astype(jnp.float32).reshape(1)
+    heard_scratch = [pltpu.VMEM((PLANE, 8, LANES), jnp.float32), pltpu.VMEM((Z, 4, LANES), jnp.float32)]
+    grad_rows = pl.pallas_call(
+        row_kernel,
+        out_shape=pltpu.HBM((Z, own, width), jnp.float32),
         in_specs=[SMEM, SMEM, VMEM, VMEM, ANY, ANY],
-        out_specs=(HBM, HBM),
-        scratch_shapes=[
-            pltpu.VMEM((PLANE, 8, LANES), jnp.float32),
-            pltpu.VMEM((Z, 4, LANES), jnp.float32),
+        out_specs=HBM,
+        scratch_shapes=heard_scratch + [
             pltpu.VMEM((row_count, col_count), jnp.float32),
             pltpu.VMEM((Z, own, width), jnp.float32),
             pltpu.SemaphoreType.DMA((2,)),
-            pltpu.SemaphoreType.DMA((2, 2)),
+            pltpu.SemaphoreType.DMA((2,)),
         ],
         compiler_params=PARAMS,
-        name="weights",
-    )(scale, (plane * col_count).astype(jnp.float32).reshape(1), cols, scores, heard_col, heard_row)
+        name="row_grads",
+    )(scale, base, cols, scores, heard_col, heard_row)
     row_parts = lax.all_to_all(grad_rows, "z", 0, 0, tiled=True)
 
     def grad_cols(of_core):
         half = col_count // CORE
-        return lax.dot_general(
-            lax.dynamic_slice(weights, (0, of_core * half), (row_count, half)), rows, (((0,), (0,)), ((), ())),
-            precision=lax.Precision.HIGH, preferred_element_type=jnp.float32,
-        ).reshape(SIDE, SIDE, own, width)
+        return pl.pallas_call(
+            col_kernel,
+            out_shape=jax.ShapeDtypeStruct((SIDE * SIDE, own, width), jnp.float32),
+            in_specs=[SMEM, SMEM, SMEM, VMEM, VMEM, ANY, ANY],
+            out_specs=ANY,
+            scratch_shapes=heard_scratch + [
+                pltpu.VMEM((8, LANES), jnp.float32),
+                pltpu.VMEM((row_count, half), jnp.float32),
+                pltpu.VMEM((SIDE * SIDE, own, width), jnp.float32),
+                pltpu.SemaphoreType.DMA((3,)),
+            ],
+            compiler_params=PARAMS,
+            name="col_grads",
+        )(scale, base, of_core.reshape(1), rows, scores, heard_col, heard_row).reshape(SIDE, SIDE, own, width)
 
     given = shift(grad_cols(1 - core), "core", CORE, 1)
     col_sum = home(grad_cols(core) + given, "y", SIDE, 1, along)
     col_sum = home(col_sum, "x", SIDE, 0, across)
-    return jnp.sum(row_parts, axis=0), logit_scale * col_sum
+    return jnp.sum(row_parts, axis=0), col_sum
 
 
 def solution(mesh):

time: 136 us -> 136 us (level); the launches traced: 134 us -> 135 us
  Pallas kernels: 9.16 us -> 13.9 us
  matrix products: 1.69 us -> 0 us
    pallas_call x1 -> x3, Pallas kernels: 3.25 us -> 8 us  [the longest x2 4.71 us: grad_cols(): pl.pallas_call(col_kernel, out_shape=jax.ShapeDtypeStruct((SIDE * SIDE, o...]
    dot_general x2 -> x0, matrix products: 1.69 us -> none  [grad_cols(): lax.dot_general(lax.dynamic_slice(weights, (0, of_core * half), (row_coun...]
  transfers between devices with their start and end apart: 10 -> 10, of which waited for: 6 -> 5; matrix products, arithmetic and copies ran while one was open for 3% -> 2% of each run, Pallas kernels for 0% -> 3%
where the time goes in v12:
time: 136 us; the launch traced here: 135 us
  blocking collectives  51.4 us (38%)
  starting transfers between devices  41.1 us (30%)
  waiting for transfers between devices  24.8 us (18%)
  Pallas kernels  13.9 us (10%)
  other arithmetic  2.64 us (2%)
  between operations  1.62 us (1%)
    all_gather x1, blocking collectives, local(): rows = lax.all_gather(row_embed, 'z', axis=0, tiled=True)  38.1 us
    ppermute x7, starting transfers between devices, shift(): lax.ppermute(block, axis, [(i, (i + by) % count) for i in range(count)])  20.9 us
    all_to_all x1, blocking collectives, local(): lax.all_to_all(col_message, ('core', 'x', 'y'), 0, 0, tiled=True)  13.3 us
    all_to_all x1, waiting for transfers between devices, local(): heard_row = lax.all_to_all(row_message, 'z', 0, 0, tiled=True)  12.6 us
    ppermute x7, waiting for transfers between devices, shift(): lax.ppermute(block, axis, [(i, (i + by) % count) for i in range(count)])  12.2 us
    all_to_all x1, starting transfers between devices, to_all(): return lax.all_to_all(sent, axes, 0, 0, tiled=True)  9.69 us
    all_to_all x1, starting transfers between devices, local(): heard_row = lax.all_to_all(row_message, 'z', 0, 0, tiled=True)  6.83 us
    pallas_call x2, Pallas kernels, grad_cols(): pl.pallas_call(col_kernel, out_shape=jax.ShapeDtypeStruct((SIDE * SIDE, o...  4.71 us
  transfers between devices with their start and end apart: 10, of which 5 were waited for; matrix products, arithmetic and copies ran while one was open for 2% of the time, Pallas kernels for 3%

profile of v12, /device:TPU:6, one launch (start us, length us, event | category | flops | bytes accessed | tf_op | source)
XLA Modules:
  0.0 135.5 jit_solution(13095763149885422511)
XLA Ops:
  0.6 2.2 %repeat.1 = f32[32,24,512]{2,1,0:T(8,128)} custom-call(f32[24,512]{1,0:T(8,128)} %block_ref.1), custom_call_target="tpu_custom_call" | custom-call | tf_op jit(solution)/shard_map/repeat/pallas_call | solution.py:28
  2.9 9.7 %all-to-all-start = ((f32[32,24,512]{2,1,0:T(8,128)}), f32[32,24,512]{2,1,0:T(8,128)S(1)}, u32[]{:S(2)}, u32[]{:S(2)}) async-start(f32[32,24,512]{2,1,0:T(8,128)} %repeat.1), calls=%async_computation | async-start | bytes 3145728 | tf_op jit(solution)/shard_map/all_to_all | solution.py:36
  13.3 38.1 %all_gather.3.row_ref = f32[384,512]{1,0:T(8,128)S(1)} all-gather(f32[24,512]{1,0:T(8,128)S(1)} %copy-done), channel_id=1, replica_groups=mesh['z'=16,'x'=4,'y'=4,'core'=2] {'z'}, dimensions={0}, use_global_device_ids=true | all-gather | bytes 835584 | tf_op jit(solution)/shard_map/all_gather | solution.py:198
  51.4 3.7 %scores.1 = (f32[384,768]{1,0:T(8,128)S(1)}, f32[32,8,128]{2,1,0:T(8,128)}, f32[16,4,128]{2,1,0:T(4,128)}) custom-call(f32[1]{0:T(128)} %bitcast.33.scale_ref, f32[384,512]{1,0:T(8,128)S(1)} %all_gather.3.row_ref, f32[768,512]{1,0:T(8,128)S(1)} %bitcast.37, f32[1,128]{1,0:T(1,128)S(1)} %pad_bitcast_fusion.target_ref), custom_call_target="tpu_custom_call" | custom-call | tf_op jit(solution)/shard_map/scores/pallas_call | solution.py:202
  55.1 13.3 %all_to_all.20.heard_col_in = f32[32,8,128]{2,1,0:T(8,128)} all-to-all(f32[32,8,128]{2,1,0:T(8,128)} %get-tuple-element.8), channel_id=1, replica_groups=mesh['z'=16,'x'=4,'y'=4,'core'=2] {'core','x','y'}, dimensions={0} | all-to-all | bytes 262144 | tf_op jit(solution)/shard_map/all_to_all | solution.py:221
  68.4 6.8 %all-to-all-start.2 = ((f32[16,4,128]{2,1,0:T(4,128)}), f32[16,4,128]{2,1,0:T(4,128)}, u32[]{:S(2)}, u32[]{:S(2)}) async-start(f32[16,4,128]{2,1,0:T(4,128)} %get-tuple-element.11), calls=%async_computation.2 | async-start | bytes 65536 | tf_op jit(solution)/shard_map/all_to_all | solution.py:223
  75.2 12.6 %all-to-all-done.2.heard_row_in = f32[16,4,128]{2,1,0:T(4,128)} async-done(((f32[16,4,128]{2,1,0:T(4,128)}), f32[16,4,128]{2,1,0:T(4,128)}, u32[]{:S(2)}, u32[]{:S(2)}) %all-to-all-start.2) | async-done | bytes 32800 | tf_op jit(solution)/shard_map/all_to_all | solution.py:223
  87.8 3.3 %row_grads.1 = f32[16,24,512]{2,1,0:T(8,128)} custom-call(f32[1]{0:T(128)} %bitcast.34.scale_ref, f32[1]{0:T(128)} %bitcast.1.base_ref, f32[768,512]{1,0:T(8,128)S(1)} %bitcast.38, f32[384,768]{1,0:T(8,128)S(1)} %get-tuple-element.7.score_ref, f32[32,8,128]{2,1,0:T(8,128)} %all_to_all.20.heard_col_in, f32[16,4,128]{2,1,0:T(4,128)} %all-to-all-done.2.heard_row_in), custom_call_target="tpu_custom_call" | custom-call | tf_op jit(solution)/shard_map/row_grads/pallas_call | solution.py:228
  91.1 3.6 %all-to-all-start.3 = ((f32[16,24,512]{2,1,0:T(8,128)}), f32[16,24,512]{2,1,0:T(8,128)S(1)}, u32[]{:S(2)}, u32[]{:S(2)}) async-start(f32[16,24,512]{2,1,0:T(8,128)} %row_grads.1), calls=%async_computation.3 | async-start | bytes 1572864 | tf_op jit(solution)/shard_map/all_to_all | solution.py:242
  94.7 2.4 %col_grads.3 = f32[16,24,512]{2,1,0:T(8,128)S(1)} custom-call(f32[1]{0:T(128)} %bitcast.36.scale_ref, f32[1]{0:T(128)} %bitcast.1.base_ref, s32[1]{0:T(128)} %bitcast.6.core_ref, f32[384,512]{1,0:T(8,128)S(1)} %all_gather.3.row_ref, f32[384,768]{1,0:T(8,128)S(1)} %get-tuple-element.7.score_ref, f32[32,8,128]{2,1,0:T(8,128)} %all_to_all.20.heard_col_in, ...), custom_call_target="tpu_custom_call" | custom-call | tf_op jit(solution)/shard_map/col_grads/pallas_call | solution.py:246
  97.1 1.9 %collective-permute-start = (f32[4,4,24,512]{3,2,1,0:T(8,128)S(1)}, f32[4,4,24,512]{3,2,1,0:T(8,128)}, u32[]{:S(2)}, u32[]{:S(2)}) collective-permute-start(f32[4,4,24,512]{3,2,1,0:T(8,128)S(1)} %bitcast.40), channel_id=1, source_target_pairs={{0,1},{1,0},{2,3},{3,2},{4,5},{5,4},{6,7},{7,6},{8,9},{9,8},{10,11... | collective-permute-start | bytes 2359304 | tf_op jit(solution)/shard_map/ppermute | solution.py:40
  99.1 2.3 %col_grads.2 = f32[16,24,512]{2,1,0:T(8,128)S(1)} custom-call(f32[1]{0:T(128)} %bitcast.35.scale_ref, f32[1]{0:T(128)} %bitcast.1.base_ref, s32[1]{0:T(128)} %bitcast.4.core_ref, f32[384,512]{1,0:T(8,128)S(1)} %all_gather.3.row_ref, f32[384,768]{1,0:T(8,128)S(1)} %get-tuple-element.7.score_ref, f32[32,8,128]{2,1,0:T(8,128)} %all_to_all.20.heard_col_in, ...), custom_call_target="tpu_custom_call" | custom-call | tf_op jit(solution)/shard_map/col_grads/pallas_call | solution.py:246
  101.5 1.3 add.116
  102.8 2.2 %collective-permute-start.3 = (f32[4,24,512]{2,1,0:T(8,128)S(1)}, f32[4,24,512]{2,1,0:T(8,128)S(1)}, u32[]{:S(2)}, u32[]{:S(2)}) collective-permute-start(f32[4,24,512]{2,1,0:T(8,128)S(1)} %get-tuple-element.13), channel_id=1, source_target_pairs={{0,2},{2,4},{4,6},{6,0},{1,3},{3,5},{5,7},{7,1},{8,10},{10,12},{12... | collective-permute-start | bytes 589832 | tf_op jit(solution)/shard_map/ppermute | solution.py:40
  105.0 4.4 %collective-permute-start.2 = (f32[4,24,512]{2,1,0:T(8,128)S(1)}, f32[4,24,512]{2,1,0:T(8,128)S(1)}, u32[]{:S(2)}, u32[]{:S(2)}) collective-permute-start(f32[4,24,512]{2,1,0:T(8,128)S(1)} %get-tuple-element.14), channel_id=1, source_target_pairs={{0,4},{2,6},{4,0},{6,2},{1,5},{3,7},{5,1},{7,3},{8,12},{10,14},{12... | collective-permute-start | bytes 589832 | tf_op jit(solution)/shard_map/ppermute | solution.py:40
  109.5 3.0 %collective-permute-start.1 = (f32[4,24,512]{2,1,0:T(8,128)S(1)}, f32[4,24,512]{2,1,0:T(8,128)S(1)}, u32[]{:S(2)}, u32[]{:S(2)}) collective-permute-start(f32[4,24,512]{2,1,0:T(8,128)S(1)} %get-tuple-element.12), channel_id=1, source_target_pairs={{0,6},{2,0},{4,2},{6,4},{1,7},{3,1},{5,3},{7,5},{8,14},{10,8},{12,... | collective-permute-start | bytes 589832 | tf_op jit(solution)/shard_map/ppermute | solution.py:40
  112.5 4.9 %collective-permute-done.3 = f32[4,24,512]{2,1,0:T(8,128)S(1)} collective-permute-done((f32[4,24,512]{2,1,0:T(8,128)S(1)}, f32[4,24,512]{2,1,0:T(8,128)S(1)}, u32[]{:S(2)}, u32[]{:S(2)}) %collective-permute-start.3) | collective-permute-done | bytes 196640 | tf_op jit(solution)/shard_map/ppermute | solution.py:40
  117.4 2.5 %collective-permute-done.1 = f32[4,24,512]{2,1,0:T(8,128)S(1)} collective-permute-done((f32[4,24,512]{2,1,0:T(8,128)S(1)}, f32[4,24,512]{2,1,0:T(8,128)S(1)}, u32[]{:S(2)}, u32[]{:S(2)}) %collective-permute-start.1) | collective-permute-done | bytes 196640 | tf_op jit(solution)/shard_map/ppermute | solution.py:40
  120.0 4.1 %collective-permute-start.6 = (f32[24,512]{1,0:T(8,128)S(1)}, f32[24,512]{1,0:T(8,128)S(1)}, u32[]{:S(2)}, u32[]{:S(2)}) collective-permute-start(f32[24,512]{1,0:T(8,128)S(1)} %get-tuple-element.16), channel_id=1, source_target_pairs={{0,8},{8,16},{16,24},{24,0},{1,9},{9,17},{17,25},{25,1},{2,10},{10... | collective-permute-start | bytes 147464 | tf_op jit(solution)/shard_map/ppermute | solution.py:40
  124.1 2.9 %collective-permute-start.5 = (f32[24,512]{1,0:T(8,128)S(1)}, f32[24,512]{1,0:T(8,128)S(1)}, u32[]{:S(2)}, u32[]{:S(2)}) collective-permute-start(f32[24,512]{1,0:T(8,128)S(1)} %get-tuple-element.17), channel_id=1, source_target_pairs={{0,16},{8,24},{16,0},{24,8},{1,17},{9,25},{17,1},{25,9},{2,18},{10... | collective-permute-start | bytes 147464 | tf_op jit(solution)/shard_map/ppermute | solution.py:40
  127.0 2.4 %collective-permute-start.4 = (f32[24,512]{1,0:T(8,128)S(1)}, f32[24,512]{1,0:T(8,128)S(1)}, u32[]{:S(2)}, u32[]{:S(2)}) collective-permute-start(f32[24,512]{1,0:T(8,128)S(1)} %get-tuple-element.15), channel_id=1, source_target_pairs={{0,24},{8,0},{16,8},{24,16},{1,25},{9,1},{17,9},{25,17},{2,26},{10... | collective-permute-start | bytes 147464 | tf_op jit(solution)/shard_map/ppermute | solution.py:40
  129.4 2.4 %collective-permute-done.5 = f32[24,512]{1,0:T(8,128)S(1)} collective-permute-done((f32[24,512]{1,0:T(8,128)S(1)}, f32[24,512]{1,0:T(8,128)S(1)}, u32[]{:S(2)}, u32[]{:S(2)}) %collective-permute-start.5) | collective-permute-done | bytes 49184 | tf_op jit(solution)/shard_map/ppermute | solution.py:40
  131.8 2.3 %collective-permute-done.4 = f32[24,512]{1,0:T(8,128)S(1)} collective-permute-done((f32[24,512]{1,0:T(8,128)S(1)}, f32[24,512]{1,0:T(8,128)S(1)}, u32[]{:S(2)}, u32[]{:S(2)}) %collective-permute-start.4) | collective-permute-done | bytes 49184 | tf_op jit(solution)/shard_map/ppermute | solution.py:40
  134.8 0.7 reduce_sum.9
  (15 shorter events, 0.8 us)
Async XLA Ops:
  2.9 10.4 %copy-start.1 = (s32[24]{0:T(128)S(1)}, s32[24]{0:T(128)}, u32[]{:S(2)}) copy-start(s32[24]{0:T(128)} %param.7) | copy-start | bytes 292
  2.9 10.4 %copy-start = (f32[24,512]{1,0:T(8,128)S(1)}, f32[24,512]{1,0:T(8,128)}, u32[]{:S(2)}) copy-start(f32[24,512]{1,0:T(8,128)} %param.4) | copy-start | bytes 147460
  2.9 48.5 %all-to-all-start = ((f32[32,24,512]{2,1,0:T(8,128)}), f32[32,24,512]{2,1,0:T(8,128)S(1)}, u32[]{:S(2)}, u32[]{:S(2)}) async-start(f32[32,24,512]{2,1,0:T(8,128)} %repeat.1), calls=%async_computation | async-start | bytes 3145728 | tf_op jit(solution)/shard_map/all_to_all | solution.py:36
  68.4 19.5 %all-to-all-start.2 = ((f32[16,4,128]{2,1,0:T(4,128)}), f32[16,4,128]{2,1,0:T(4,128)}, u32[]{:S(2)}, u32[]{:S(2)}) async-start(f32[16,4,128]{2,1,0:T(4,128)} %get-tuple-element.11), calls=%async_computation.2 | async-start | bytes 65536 | tf_op jit(solution)/shard_map/all_to_all | solution.py:223
  91.1 43.7 %all-to-all-start.3 = ((f32[16,24,512]{2,1,0:T(8,128)}), f32[16,24,512]{2,1,0:T(8,128)S(1)}, u32[]{:S(2)}, u32[]{:S(2)}) async-start(f32[16,24,512]{2,1,0:T(8,128)} %row_grads.1), calls=%async_computation.3 | async-start | bytes 1572864 | tf_op jit(solution)/shard_map/all_to_all | solution.py:242
  97.1 4.3 %collective-permute-start = (f32[4,4,24,512]{3,2,1,0:T(8,128)S(1)}, f32[4,4,24,512]{3,2,1,0:T(8,128)}, u32[]{:S(2)}, u32[]{:S(2)}) collective-permute-start(f32[4,4,24,512]{3,2,1,0:T(8,128)S(1)} %bitcast.40), channel_id=1, source_target_pairs={{0,1},{1,0},{2,3},{3,2},{4,5},{5,4},{6,7},{7,6},{8,9},{9,8},{10,11... | collective-permute-start | bytes 2359304 | tf_op jit(solution)/shard_map/ppermute | solution.py:40
  102.8 14.6 %collective-permute-start.3 = (f32[4,24,512]{2,1,0:T(8,128)S(1)}, f32[4,24,512]{2,1,0:T(8,128)S(1)}, u32[]{:S(2)}, u32[]{:S(2)}) collective-permute-start(f32[4,24,512]{2,1,0:T(8,128)S(1)} %get-tuple-element.13), channel_id=1, source_target_pairs={{0,2},{2,4},{4,6},{6,0},{1,3},{3,5},{5,7},{7,1},{8,10},{10,12},{12... | collective-permute-start | bytes 589832 | tf_op jit(solution)/shard_map/ppermute | solution.py:40
  105.0 12.4 %collective-permute-start.2 = (f32[4,24,512]{2,1,0:T(8,128)S(1)}, f32[4,24,512]{2,1,0:T(8,128)S(1)}, u32[]{:S(2)}, u32[]{:S(2)}) collective-permute-start(f32[4,24,512]{2,1,0:T(8,128)S(1)} %get-tuple-element.14), channel_id=1, source_target_pairs={{0,4},{2,6},{4,0},{6,2},{1,5},{3,7},{5,1},{7,3},{8,12},{10,14},{12... | collective-permute-start | bytes 589832 | tf_op jit(solution)/shard_map/ppermute | solution.py:40
  109.5 10.4 %collective-permute-start.1 = (f32[4,24,512]{2,1,0:T(8,128)S(1)}, f32[4,24,512]{2,1,0:T(8,128)S(1)}, u32[]{:S(2)}, u32[]{:S(2)}) collective-permute-start(f32[4,24,512]{2,1,0:T(8,128)S(1)} %get-tuple-element.12), channel_id=1, source_target_pairs={{0,6},{2,0},{4,2},{6,4},{1,7},{3,1},{5,3},{7,5},{8,14},{10,8},{12,... | collective-permute-start | bytes 589832 | tf_op jit(solution)/shard_map/ppermute | solution.py:40
  120.0 9.4 %collective-permute-start.6 = (f32[24,512]{1,0:T(8,128)S(1)}, f32[24,512]{1,0:T(8,128)S(1)}, u32[]{:S(2)}, u32[]{:S(2)}) collective-permute-start(f32[24,512]{1,0:T(8,128)S(1)} %get-tuple-element.16), channel_id=1, source_target_pairs={{0,8},{8,16},{16,24},{24,0},{1,9},{9,17},{17,25},{25,1},{2,10},{10... | collective-permute-start | bytes 147464 | tf_op jit(solution)/shard_map/ppermute | solution.py:40
  124.1 7.7 %collective-permute-start.5 = (f32[24,512]{1,0:T(8,128)S(1)}, f32[24,512]{1,0:T(8,128)S(1)}, u32[]{:S(2)}, u32[]{:S(2)}) collective-permute-start(f32[24,512]{1,0:T(8,128)S(1)} %get-tuple-element.17), channel_id=1, source_target_pairs={{0,16},{8,24},{16,0},{24,8},{1,17},{9,25},{17,1},{25,9},{2,18},{10... | collective-permute-start | bytes 147464 | tf_op jit(solution)/shard_map/ppermute | solution.py:40
  127.0 7.2 %collective-permute-start.4 = (f32[24,512]{1,0:T(8,128)S(1)}, f32[24,512]{1,0:T(8,128)S(1)}, u32[]{:S(2)}, u32[]{:S(2)}) collective-permute-start(f32[24,512]{1,0:T(8,128)S(1)} %get-tuple-element.15), channel_id=1, source_target_pairs={{0,24},{8,0},{16,8},{24,16},{1,25},{9,1},{17,9},{25,17},{2,26},{10... | collective-permute-start | bytes 147464 | tf_op jit(solution)/shard_map/ppermute | solution.py:40

commit v13 on v11

--- a/solution.py
+++ b/solution.py
@@ -50,12 +50,10 @@
     return total
 
 
-def score_kernel(
-    scale_ref, row_ref, col_ref, target_ref, score_out, col_out, row_out, score_ref, col_part, row_part, sems
-):
+def score_kernel(scale_ref, row_ref, col_ref, score_out, col_out, score_ref, col_part, sems):
     stores = [
         pltpu.make_async_copy(source, target, sems.at[k])
-        for k, (source, target) in enumerate(((score_ref, score_out), (row_part, row_out), (col_part, col_out)))
+        for k, (source, target) in enumerate(((score_ref, score_out), (col_part, col_out)))
     ]
     scores = scale_ref[0] * lax.dot_general(
         row_ref[...], col_ref[...], (((1,), (1,)), ((), ())),
@@ -63,24 +61,29 @@
     )
     score_ref[...] = scores
     stores[0].start()
-    used = scores.shape[0] // LANES
-    for k in range(used):
-        part = scores[k * LANES:(k + 1) * LANES]
-        top = jnp.max(part, axis=1, keepdims=True)
-        lse = top + jnp.log(jnp.sum(jnp.exp(part - top), axis=1, keepdims=True))
-        lse = jnp.transpose(jnp.broadcast_to(lse, (LANES, LANES)))[:1]
-        row_part[:, k, :] = jnp.broadcast_to(lse, (row_part.shape[0], LANES))
-    row_part[:, used, :] = jnp.broadcast_to(target_ref[...], (row_part.shape[0], LANES))
-    stores[1].start()
     top = jnp.max(scores, axis=0, keepdims=True)
     lse = top + jnp.log(jnp.sum(jnp.exp(scores - top), axis=0, keepdims=True))
     used = lse.shape[1] // LANES
     for k in range(used):
         col_part[:, k, :] = jnp.broadcast_to(lse[:, k * LANES:(k + 1) * LANES], (col_part.shape[0], LANES))
     col_part[:, used:, :] = jnp.zeros_like(col_part[:, used:, :])
-    stores[2].start()
+    stores[1].start()
     for store in stores:
         store.wait()
+
+
+def row_message_kernel(score_ref, target_ref, row_out, row_part, sem):
+    used = score_ref.shape[0] // LANES
+    for k in range(used):
+        part = score_ref[k * LANES:(k + 1) * LANES, :]
+        top = jnp.max(part, axis=1, keepdims=True)
+        lse = top + jnp.log(jnp.sum(jnp.exp(part - top), axis=1, keepdims=True))
+        lse = jnp.transpose(jnp.broadcast_to(lse, (LANES, LANES)))[:1]
+        row_part[:, k, :] = jnp.broadcast_to(lse, (row_part.shape[0], LANES))
+    row_part[:, used, :] = jnp.broadcast_to(target_ref[...], (row_part.shape[0], LANES))
+    store = pltpu.make_async_copy(row_part, row_out, sem)
+    store.start()
+    store.wait()
 
 
 def split(values):
@@ -164,26 +167,33 @@
     row_count, col_count = rows.shape[0], cols.shape[0]
 
     numbers = jnp.pad(targets.astype(jnp.float32), (0, LANES - own)).reshape(1, LANES)
-    scores, col_message, row_message = pl.pallas_call(
+    scores, col_message = pl.pallas_call(
         score_kernel,
         out_shape=(
             jax.ShapeDtypeStruct((row_count, col_count), jnp.float32),
             pltpu.HBM((PLANE, 8, LANES), jnp.float32),
-            pltpu.HBM((Z, 4, LANES), jnp.float32),
         ),
-        in_specs=[SMEM, VMEM, VMEM, VMEM],
-        out_specs=(ANY, HBM, HBM),
+        in_specs=[SMEM, VMEM, VMEM],
+        out_specs=(ANY, HBM),
         scratch_shapes=[
             pltpu.VMEM((row_count, col_count), jnp.float32),
             pltpu.VMEM((PLANE, 8, LANES), jnp.float32),
-            pltpu.VMEM((Z, 4, LANES), jnp.float32),
-            pltpu.SemaphoreType.DMA((3,)),
+            pltpu.SemaphoreType.DMA((2,)),
         ],
         compiler_params=PARAMS,
         name="scores",
-    )(scale, rows, cols, numbers)
-
+    )(scale, rows, cols)
     heard_col = lax.all_to_all(col_message, ("core", "x", "y"), 0, 0, tiled=True)
+    row_message = pl.pallas_call(
+        row_message_kernel,
+        out_shape=pltpu.HBM((Z, 4, LANES), jnp.float32),
+        in_specs=[VMEM, VMEM],
+        out_specs=HBM,
+        scratch_shapes=[pltpu.VMEM((Z, 4, LANES), jnp.float32), pltpu.SemaphoreType.DMA],
+        compiler_params=PARAMS,
+        cost_estimate=pl.CostEstimate(flops=4 * row_count * col_count, bytes_accessed=4 * row_count * col_count, transcendentals=row_count * col_count),
+        name="row_message",
+    )(scores, numbers)
     heard_col, row_message = lax.optimization_barrier((heard_col, row_message))
     heard_row = lax.all_to_all(row_message, "z", 0, 0, tiled=True)
     heard_col = pltpu.with_memory_space_constraint(heard_col, pltpu.HBM)

time: 136 us -> 135 us (level)
  blocking collectives: 51.4 us -> 38.1 us
  starting transfers between devices: 41.2 us -> 48.4 us
  waiting for transfers between devices: 25.8 us -> 30.8 us
    all_to_all x1 -> x0, blocking collectives: 13.3 us -> none  [local(): lax.all_to_all(col_message, ('core', 'x', 'y'), 0, 0, tiled=True)]
    all_to_all x0 -> x1, starting transfers between devices: none -> 7.24 us  [local(): lax.all_to_all(col_message, ('core', 'x', 'y'), 0, 0, tiled=True)]
    all_to_all x0 -> x1, waiting for transfers between devices: none -> 4.96 us  [local(): lax.all_to_all(col_message, ('core', 'x', 'y'), 0, 0, tiled=True)]
  transfers between devices with their start and end apart: 10 -> 11, of which waited for: 6 -> 7; matrix products, arithmetic and copies ran while one was open for 3% -> 3% of each run, Pallas kernels for 0% -> 1%
where the time goes in v13:
time: 135 us; the launch traced here: 133 us
  starting transfers between devices  48.4 us (36%)
  blocking collectives  38.1 us (28%)
  waiting for transfers between devices  30.8 us (23%)
  Pallas kernels  9.88 us (7%)
  other arithmetic  2.64 us (2%)
  matrix products  1.69 us (1%)
  between operations  1.64 us (1%)
    all_gather x1, blocking collectives, local(): rows = lax.all_gather(row_embed, 'z', axis=0, tiled=True)  38.1 us
    ppermute x7, starting transfers between devices, shift(): lax.ppermute(block, axis, [(i, (i + by) % count) for i in range(count)])  20.9 us
    ppermute x7, waiting for transfers between devices, shift(): lax.ppermute(block, axis, [(i, (i + by) % count) for i in range(count)])  13.3 us
    all_to_all x1, waiting for transfers between devices, local(): heard_row = lax.all_to_all(row_message, 'z', 0, 0, tiled=True)  12.6 us
    all_to_all x1, starting transfers between devices, to_all(): return lax.all_to_all(sent, axes, 0, 0, tiled=True)  9.7 us
    all_to_all x1, starting transfers between devices, local(): lax.all_to_all(col_message, ('core', 'x', 'y'), 0, 0, tiled=True)  7.24 us
    all_to_all x1, starting transfers between devices, local(): heard_row = lax.all_to_all(row_message, 'z', 0, 0, tiled=True)  6.83 us
    all_to_all x1, waiting for transfers between devices, local(): lax.all_to_all(col_message, ('core', 'x', 'y'), 0, 0, tiled=True)  4.96 us
  transfers between devices with their start and end apart: 11, of which 7 were waited for; matrix products, arithmetic and copies ran while one was open for 3% of the time, Pallas kernels for 1%

profile of v13, /device:TPU:6, one launch (start us, length us, event | category | flops | bytes accessed | tf_op | source)
XLA Modules:
  0.0 133.3 jit_solution(9479027700706044403)
XLA Ops:
  0.6 2.3 %repeat.1 = f32[32,24,512]{2,1,0:T(8,128)} custom-call(f32[24,512]{1,0:T(8,128)} %block_ref.1), custom_call_target="tpu_custom_call" | custom-call | tf_op jit(solution)/shard_map/repeat/pallas_call | solution.py:28
  2.9 9.7 %all-to-all-start = ((f32[32,24,512]{2,1,0:T(8,128)}), f32[32,24,512]{2,1,0:T(8,128)S(1)}, u32[]{:S(2)}, u32[]{:S(2)}) async-start(f32[32,24,512]{2,1,0:T(8,128)} %repeat.1), calls=%async_computation | async-start | bytes 3145728 | tf_op jit(solution)/shard_map/all_to_all | solution.py:36
  13.3 38.1 %all_gather.3.row_ref = f32[384,512]{1,0:T(8,128)S(1)} all-gather(f32[24,512]{1,0:T(8,128)S(1)} %copy-done.1), channel_id=1, replica_groups=mesh['z'=16,'x'=4,'y'=4,'core'=2] {'z'}, dimensions={0}, use_global_device_ids=true | all-gather | bytes 835584 | tf_op jit(solution)/shard_map/all_gather | solution.py:166
  51.4 3.3 %scores.1 = (f32[384,768]{1,0:T(8,128)S(1)}, f32[32,8,128]{2,1,0:T(8,128)}) custom-call(f32[1]{0:T(128)} %bitcast.35.scale_ref, f32[384,512]{1,0:T(8,128)S(1)} %all_gather.3.row_ref, f32[768,512]{1,0:T(8,128)S(1)} %bitcast.37), custom_call_target="tpu_custom_call" | custom-call | tf_op jit(solution)/shard_map/scores/pallas_call | solution.py:170
  54.7 7.2 %all-to-all-start.1 = ((f32[32,8,128]{2,1,0:T(8,128)}), f32[32,8,128]{2,1,0:T(8,128)}, u32[]{:S(2)}, u32[]{:S(2)}) async-start(f32[32,8,128]{2,1,0:T(8,128)} %get-tuple-element.9), calls=%async_computation.1 | async-start | bytes 262144 | tf_op jit(solution)/shard_map/all_to_all | solution.py:186
  62.0 1.0 row_message.1
  63.1 5.0 %all-to-all-done.1.heard_col_in = f32[32,8,128]{2,1,0:T(8,128)} async-done(((f32[32,8,128]{2,1,0:T(8,128)}), f32[32,8,128]{2,1,0:T(8,128)}, u32[]{:S(2)}, u32[]{:S(2)}) %all-to-all-start.1) | async-done | bytes 131104 | tf_op jit(solution)/shard_map/all_to_all | solution.py:186
  68.0 6.8 %all-to-all-start.2 = ((f32[16,4,128]{2,1,0:T(4,128)}), f32[16,4,128]{2,1,0:T(4,128)}, u32[]{:S(2)}, u32[]{:S(2)}) async-start(f32[16,4,128]{2,1,0:T(4,128)} %row_message.1), calls=%async_computation.2 | async-start | bytes 65536 | tf_op jit(solution)/shard_map/all_to_all | solution.py:198
  74.9 12.6 %all-to-all-done.2.heard_row_in = f32[16,4,128]{2,1,0:T(4,128)} async-done(((f32[16,4,128]{2,1,0:T(4,128)}), f32[16,4,128]{2,1,0:T(4,128)}, u32[]{:S(2)}, u32[]{:S(2)}) %all-to-all-start.2) | async-done | bytes 32800 | tf_op jit(solution)/shard_map/all_to_all | solution.py:198
  87.5 3.3 %weights.1 = (f32[384,768]{1,0:T(8,128)}, f32[16,24,512]{2,1,0:T(8,128)}) custom-call(f32[1]{0:T(128)} %bitcast.36.scale_ref, f32[1]{0:T(128)} %bitcast.1.base_ref, f32[768,512]{1,0:T(8,128)S(1)} %bitcast.38, f32[384,768]{1,0:T(8,128)S(1)} %get-tuple-element.8.score_ref, f32[32,8,128]{2,1,0:T(8,128)} %all-to-all-done.1.heard_col_in, ...), custom_call_target="tpu_custom_call" | custom-call | tf_op jit(solution)/shard_map/weights/pallas_call | solution.py:201
  90.8 3.8 %all-to-all-start.3 = ((f32[16,24,512]{2,1,0:T(8,128)}), f32[16,24,512]{2,1,0:T(8,128)S(1)}, u32[]{:S(2)}, u32[]{:S(2)}) async-start(f32[16,24,512]{2,1,0:T(8,128)} %get-tuple-element.12), calls=%async_computation.3 | async-start | bytes 1572864 | tf_op jit(solution)/shard_map/all_to_all | solution.py:220
  95.4 1.9 %collective-permute-start = (f32[4,4,24,512]{3,2,1,0:T(8,128)S(1)}, f32[4,4,24,512]{3,2,1,0:T(8,128)}, u32[]{:S(2)}, u32[]{:S(2)}) collective-permute-start(f32[4,4,24,512]{3,2,1,0:T(8,128)S(1)} %bitcast.40), channel_id=1, source_target_pairs={{0,1},{1,0},{2,3},{3,2},{4,5},{5,4},{6,7},{7,6},{8,9},{9,8},{10,11... | collective-permute-start | bytes 2359304 | tf_op jit(solution)/shard_map/ppermute | solution.py:40
  98.2 1.5 %collective-permute-done = f32[4,4,24,512]{3,2,1,0:T(8,128)} collective-permute-done((f32[4,4,24,512]{3,2,1,0:T(8,128)S(1)}, f32[4,4,24,512]{3,2,1,0:T(8,128)}, u32[]{:S(2)}, u32[]{:S(2)}) %collective-permute-start) | collective-permute-done | bytes 786464 | tf_op jit(solution)/shard_map/ppermute | solution.py:40
  99.7 1.3 add.124
  101.0 2.2 %collective-permute-start.3 = (f32[4,24,512]{2,1,0:T(8,128)S(1)}, f32[4,24,512]{2,1,0:T(8,128)S(1)}, u32[]{:S(2)}, u32[]{:S(2)}) collective-permute-start(f32[4,24,512]{2,1,0:T(8,128)S(1)} %get-tuple-element.15), channel_id=1, source_target_pairs={{0,2},{2,4},{4,6},{6,0},{1,3},{3,5},{5,7},{7,1},{8,10},{10,12},{12... | collective-permute-start | bytes 589832 | tf_op jit(solution)/shard_map/ppermute | solution.py:40
  103.3 4.4 %collective-permute-start.2 = (f32[4,24,512]{2,1,0:T(8,128)S(1)}, f32[4,24,512]{2,1,0:T(8,128)S(1)}, u32[]{:S(2)}, u32[]{:S(2)}) collective-permute-start(f32[4,24,512]{2,1,0:T(8,128)S(1)} %get-tuple-element.16), channel_id=1, source_target_pairs={{0,4},{2,6},{4,0},{6,2},{1,5},{3,7},{5,1},{7,3},{8,12},{10,14},{12... | collective-permute-start | bytes 589832 | tf_op jit(solution)/shard_map/ppermute | solution.py:40
  107.7 3.0 %collective-permute-start.1 = (f32[4,24,512]{2,1,0:T(8,128)S(1)}, f32[4,24,512]{2,1,0:T(8,128)S(1)}, u32[]{:S(2)}, u32[]{:S(2)}) collective-permute-start(f32[4,24,512]{2,1,0:T(8,128)S(1)} %get-tuple-element.14), channel_id=1, source_target_pairs={{0,6},{2,0},{4,2},{6,4},{1,7},{3,1},{5,3},{7,5},{8,14},{10,8},{12,... | collective-permute-start | bytes 589832 | tf_op jit(solution)/shard_map/ppermute | solution.py:40
  110.7 4.6 %collective-permute-done.3 = f32[4,24,512]{2,1,0:T(8,128)S(1)} collective-permute-done((f32[4,24,512]{2,1,0:T(8,128)S(1)}, f32[4,24,512]{2,1,0:T(8,128)S(1)}, u32[]{:S(2)}, u32[]{:S(2)}) %collective-permute-start.3) | collective-permute-done | bytes 196640 | tf_op jit(solution)/shard_map/ppermute | solution.py:40
  115.3 2.5 %collective-permute-done.1 = f32[4,24,512]{2,1,0:T(8,128)S(1)} collective-permute-done((f32[4,24,512]{2,1,0:T(8,128)S(1)}, f32[4,24,512]{2,1,0:T(8,128)S(1)}, u32[]{:S(2)}, u32[]{:S(2)}) %collective-permute-start.1) | collective-permute-done | bytes 196640 | tf_op jit(solution)/shard_map/ppermute | solution.py:40
  117.9 4.1 %collective-permute-start.6 = (f32[24,512]{1,0:T(8,128)S(1)}, f32[24,512]{1,0:T(8,128)S(1)}, u32[]{:S(2)}, u32[]{:S(2)}) collective-permute-start(f32[24,512]{1,0:T(8,128)S(1)} %get-tuple-element.18), channel_id=1, source_target_pairs={{0,8},{8,16},{16,24},{24,0},{1,9},{9,17},{17,25},{25,1},{2,10},{10... | collective-permute-start | bytes 147464 | tf_op jit(solution)/shard_map/ppermute | solution.py:40
  122.0 2.8 %collective-permute-start.5 = (f32[24,512]{1,0:T(8,128)S(1)}, f32[24,512]{1,0:T(8,128)S(1)}, u32[]{:S(2)}, u32[]{:S(2)}) collective-permute-start(f32[24,512]{1,0:T(8,128)S(1)} %get-tuple-element.19), channel_id=1, source_target_pairs={{0,16},{8,24},{16,0},{24,8},{1,17},{9,25},{17,1},{25,9},{2,18},{10... | collective-permute-start | bytes 147464 | tf_op jit(solution)/shard_map/ppermute | solution.py:40
  124.8 2.5 %collective-permute-start.4 = (f32[24,512]{1,0:T(8,128)S(1)}, f32[24,512]{1,0:T(8,128)S(1)}, u32[]{:S(2)}, u32[]{:S(2)}) collective-permute-start(f32[24,512]{1,0:T(8,128)S(1)} %get-tuple-element.17), channel_id=1, source_target_pairs={{0,24},{8,0},{16,8},{24,16},{1,25},{9,1},{17,9},{25,17},{2,26},{10... | collective-permute-start | bytes 147464 | tf_op jit(solution)/shard_map/ppermute | solution.py:40
  127.3 2.6 %collective-permute-done.5 = f32[24,512]{1,0:T(8,128)S(1)} collective-permute-done((f32[24,512]{1,0:T(8,128)S(1)}, f32[24,512]{1,0:T(8,128)S(1)}, u32[]{:S(2)}, u32[]{:S(2)}) %collective-permute-start.5) | collective-permute-done | bytes 49184 | tf_op jit(solution)/shard_map/ppermute | solution.py:40
  129.9 2.1 %collective-permute-done.4 = f32[24,512]{1,0:T(8,128)S(1)} collective-permute-done((f32[24,512]{1,0:T(8,128)S(1)}, f32[24,512]{1,0:T(8,128)S(1)}, u32[]{:S(2)}, u32[]{:S(2)}) %collective-permute-start.4) | collective-permute-done | bytes 49184 | tf_op jit(solution)/shard_map/ppermute | solution.py:40
  (19 shorter events, 3.2 us)
Async XLA Ops:
  2.9 10.4 %copy-start.1 = (f32[24,512]{1,0:T(8,128)S(1)}, f32[24,512]{1,0:T(8,128)}, u32[]{:S(2)}) copy-start(f32[24,512]{1,0:T(8,128)} %param.4) | copy-start | bytes 147460
  2.9 48.5 %all-to-all-start = ((f32[32,24,512]{2,1,0:T(8,128)}), f32[32,24,512]{2,1,0:T(8,128)S(1)}, u32[]{:S(2)}, u32[]{:S(2)}) async-start(f32[32,24,512]{2,1,0:T(8,128)} %repeat.1), calls=%async_computation | async-start | bytes 3145728 | tf_op jit(solution)/shard_map/all_to_all | solution.py:36
  51.4 10.6 %copy-start.2 = (s32[24]{0:T(128)S(1)}, s32[24]{0:T(128)}, u32[]{:S(2)}) copy-start(s32[24]{0:T(128)} %param.7) | copy-start | bytes 292
  54.7 13.3 %all-to-all-start.1 = ((f32[32,8,128]{2,1,0:T(8,128)}), f32[32,8,128]{2,1,0:T(8,128)}, u32[]{:S(2)}, u32[]{:S(2)}) async-start(f32[32,8,128]{2,1,0:T(8,128)} %get-tuple-element.9), calls=%async_computation.1 | async-start | bytes 262144 | tf_op jit(solution)/shard_map/all_to_all | solution.py:186
  68.0 19.5 %all-to-all-start.2 = ((f32[16,4,128]{2,1,0:T(4,128)}), f32[16,4,128]{2,1,0:T(4,128)}, u32[]{:S(2)}, u32[]{:S(2)}) async-start(f32[16,4,128]{2,1,0:T(4,128)} %row_message.1), calls=%async_computation.2 | async-start | bytes 65536 | tf_op jit(solution)/shard_map/all_to_all | solution.py:198
  90.7 3.8 %copy-start = (f32[384,768]{1,0:T(8,128)S(1)}, f32[384,768]{1,0:T(8,128)}, u32[]{:S(2)}) copy-start(f32[384,768]{1,0:T(8,128)} %get-tuple-element.13) | copy-start | bytes 3538948
  90.8 41.9 %all-to-all-start.3 = ((f32[16,24,512]{2,1,0:T(8,128)}), f32[16,24,512]{2,1,0:T(8,128)S(1)}, u32[]{:S(2)}, u32[]{:S(2)}) async-start(f32[16,24,512]{2,1,0:T(8,128)} %get-tuple-element.12), calls=%async_computation.3 | async-start | bytes 1572864 | tf_op jit(solution)/shard_map/all_to_all | solution.py:220
  95.4 4.3 %collective-permute-start = (f32[4,4,24,512]{3,2,1,0:T(8,128)S(1)}, f32[4,4,24,512]{3,2,1,0:T(8,128)}, u32[]{:S(2)}, u32[]{:S(2)}) collective-permute-start(f32[4,4,24,512]{3,2,1,0:T(8,128)S(1)} %bitcast.40), channel_id=1, source_target_pairs={{0,1},{1,0},{2,3},{3,2},{4,5},{5,4},{6,7},{7,6},{8,9},{9,8},{10,11... | collective-permute-start | bytes 2359304 | tf_op jit(solution)/shard_map/ppermute | solution.py:40
  101.0 14.3 %collective-permute-start.3 = (f32[4,24,512]{2,1,0:T(8,128)S(1)}, f32[4,24,512]{2,1,0:T(8,128)S(1)}, u32[]{:S(2)}, u32[]{:S(2)}) collective-permute-start(f32[4,24,512]{2,1,0:T(8,128)S(1)} %get-tuple-element.15), channel_id=1, source_target_pairs={{0,2},{2,4},{4,6},{6,0},{1,3},{3,5},{5,7},{7,1},{8,10},{10,12},{12... | collective-permute-start | bytes 589832 | tf_op jit(solution)/shard_map/ppermute | solution.py:40
  103.3 12.0 %collective-permute-start.2 = (f32[4,24,512]{2,1,0:T(8,128)S(1)}, f32[4,24,512]{2,1,0:T(8,128)S(1)}, u32[]{:S(2)}, u32[]{:S(2)}) collective-permute-start(f32[4,24,512]{2,1,0:T(8,128)S(1)} %get-tuple-element.16), channel_id=1, source_target_pairs={{0,4},{2,6},{4,0},{6,2},{1,5},{3,7},{5,1},{7,3},{8,12},{10,14},{12... | collective-permute-start | bytes 589832 | tf_op jit(solution)/shard_map/ppermute | solution.py:40
  107.7 10.1 %collective-permute-start.1 = (f32[4,24,512]{2,1,0:T(8,128)S(1)}, f32[4,24,512]{2,1,0:T(8,128)S(1)}, u32[]{:S(2)}, u32[]{:S(2)}) collective-permute-start(f32[4,24,512]{2,1,0:T(8,128)S(1)} %get-tuple-element.14), channel_id=1, source_target_pairs={{0,6},{2,0},{4,2},{6,4},{1,7},{3,1},{5,3},{7,5},{8,14},{10,8},{12,... | collective-permute-start | bytes 589832 | tf_op jit(solution)/shard_map/ppermute | solution.py:40
  117.9 9.4 %collective-permute-start.6 = (f32[24,512]{1,0:T(8,128)S(1)}, f32[24,512]{1,0:T(8,128)S(1)}, u32[]{:S(2)}, u32[]{:S(2)}) collective-permute-start(f32[24,512]{1,0:T(8,128)S(1)} %get-tuple-element.18), channel_id=1, source_target_pairs={{0,8},{8,16},{16,24},{24,0},{1,9},{9,17},{17,25},{25,1},{2,10},{10... | collective-permute-start | bytes 147464 | tf_op jit(solution)/shard_map/ppermute | solution.py:40
  122.0 8.0 %collective-permute-start.5 = (f32[24,512]{1,0:T(8,128)S(1)}, f32[24,512]{1,0:T(8,128)S(1)}, u32[]{:S(2)}, u32[]{:S(2)}) collective-permute-start(f32[24,512]{1,0:T(8,128)S(1)} %get-tuple-element.19), channel_id=1, source_target_pairs={{0,16},{8,24},{16,0},{24,8},{1,17},{9,25},{17,1},{25,9},{2,18},{10... | collective-permute-start | bytes 147464 | tf_op jit(solution)/shard_map/ppermute | solution.py:40
  124.8 7.2 %collective-permute-start.4 = (f32[24,512]{1,0:T(8,128)S(1)}, f32[24,512]{1,0:T(8,128)S(1)}, u32[]{:S(2)}, u32[]{:S(2)}) collective-permute-start(f32[24,512]{1,0:T(8,128)S(1)} %get-tuple-element.17), channel_id=1, source_target_pairs={{0,24},{8,0},{16,8},{24,16},{1,25},{9,1},{17,9},{25,17},{2,26},{10... | collective-permute-start | bytes 147464 | tf_op jit(solution)/shard_map/ppermute | solution.py:40

commit v14 on v13

--- a/solution.py
+++ b/solution.py
@@ -131,29 +131,29 @@
     targets = jnp.transpose(
         jnp.concatenate([heard_row_ref[:, row_count // LANES, :], jnp.zeros((LANES - Z, LANES), jnp.float32)], axis=0)
     )
+    for z in range(Z):
+        here = slice(z * own, (z + 1) * own)
+        weight_ref[here, :] = (
+            0.5 * jnp.exp(score_ref[here, :] - row_lse[here])
+            + 0.5 * jnp.exp(score_ref[here, :] - col_lse)
+            - jnp.where(targets[:own, z:z + 1] - base == ids, 1.0, 0.0)
+        )
     stores = []
+    high, low = split(weight_ref[...])
+    half = grad_ref.shape[2] // 2
     for part in range(2):
-        first, count = part * Z // 2, Z // 2
-        for z in range(first, first + count):
-            here = slice(z * own, (z + 1) * own)
-            scores = score_ref[here, :]
-            weight_ref[here, :] = (
-                0.5 * jnp.exp(scores - row_lse[here])
-                + 0.5 * jnp.exp(scores - col_lse)
-                - jnp.where(targets[:own, z:z + 1] - base == ids, 1.0, 0.0)
-            )
-        here = pl.ds(first * own, count * own)
-        stores.append(pltpu.make_async_copy(weight_ref.at[here], weight_out.at[here], out_sems.at[0, part]))
-        stores[-1].start()
-        high, low = split(weight_ref[first * own:(first + count) * own, :])
+        here = slice(part * half, (part + 1) * half)
         total = None
         for left, right in ((high, col_high), (high, col_low), (low, col_high)):
-            term = jnp.dot(left, right, preferred_element_type=jnp.float32)
+            term = jnp.dot(left, right[:, here], preferred_element_type=jnp.float32)
             total = term if total is None else total + term
-        here = pl.ds(first, count)
-        grad_ref[here] = (scale_ref[0] * total).reshape(count, own, total.shape[1])
-        stores.append(pltpu.make_async_copy(grad_ref.at[here], grad_out.at[here], out_sems.at[1, part]))
+        grad_ref[:, :, here] = (scale_ref[0] * total).reshape(grad_ref.shape[0], own, half)
+        there = pl.ds(part * half, half)
+        stores.append(pltpu.make_async_copy(grad_ref.at[:, :, there], grad_out.at[:, :, there], out_sems.at[part]))
         stores[-1].start()
+        if part == 0:
+            stores.append(pltpu.make_async_copy(weight_ref, weight_out, out_sems.at[2]))
+            stores[-1].start()
     for store in stores:
         store.wait()
 
@@ -212,7 +212,7 @@
             pltpu.VMEM((row_count, col_count), jnp.float32),
             pltpu.VMEM((Z, own, width), jnp.float32),
             pltpu.SemaphoreType.DMA((2,)),
-            pltpu.SemaphoreType.DMA((2, 2)),
+            pltpu.SemaphoreType.DMA((3,)),
         ],
         compiler_params=PARAMS,
         name="weights",

time: 135 us -> 136 us (level)
  no operation moved by 1% of the time
where the time goes in v14:
time: 136 us; the launch traced here: 134 us
  starting transfers between devices  48.5 us (36%)
  blocking collectives  38.1 us (28%)
  waiting for transfers between devices  30.8 us (23%)
  Pallas kernels  10.5 us (8%)
  other arithmetic  2.64 us (2%)
  matrix products  1.69 us (1%)
  between operations  1.64 us (1%)
    all_gather x1, blocking collectives, local(): rows = lax.all_gather(row_embed, 'z', axis=0, tiled=True)  38.1 us
    ppermute x7, starting transfers between devices, shift(): lax.ppermute(block, axis, [(i, (i + by) % count) for i in range(count)])  20.9 us
    ppermute x7, waiting for transfers between devices, shift(): lax.ppermute(block, axis, [(i, (i + by) % count) for i in range(count)])  13.2 us
    all_to_all x1, waiting for transfers between devices, local(): heard_row = lax.all_to_all(row_message, 'z', 0, 0, tiled=True)  12.6 us
    all_to_all x1, starting transfers between devices, to_all(): return lax.all_to_all(sent, axes, 0, 0, tiled=True)  9.7 us
    all_to_all x1, starting transfers between devices, local(): lax.all_to_all(col_message, ('core', 'x', 'y'), 0, 0, tiled=True)  7.24 us
    all_to_all x1, starting transfers between devices, local(): heard_row = lax.all_to_all(row_message, 'z', 0, 0, tiled=True)  6.83 us
    all_to_all x1, waiting for transfers between devices, local(): lax.all_to_all(col_message, ('core', 'x', 'y'), 0, 0, tiled=True)  4.96 us
  transfers between devices with their start and end apart: 11, of which 7 were waited for; matrix products, arithmetic and copies ran while one was open for 3% of the time, Pallas kernels for 1%

profile of v14, /device:TPU:6, one launch (start us, length us, event | category | flops | bytes accessed | tf_op | source)
XLA Modules:
  0.0 133.9 jit_solution(16560596914084698942)
XLA Ops:
  0.6 2.3 %repeat.1 = f32[32,24,512]{2,1,0:T(8,128)} custom-call(f32[24,512]{1,0:T(8,128)} %block_ref.1), custom_call_target="tpu_custom_call" | custom-call | tf_op jit(solution)/shard_map/repeat/pallas_call | solution.py:28
  2.9 9.7 %all-to-all-start = ((f32[32,24,512]{2,1,0:T(8,128)}), f32[32,24,512]{2,1,0:T(8,128)S(1)}, u32[]{:S(2)}, u32[]{:S(2)}) async-start(f32[32,24,512]{2,1,0:T(8,128)} %repeat.1), calls=%async_computation | async-start | bytes 3145728 | tf_op jit(solution)/shard_map/all_to_all | solution.py:36
  13.3 38.1 %all_gather.3.row_ref = f32[384,512]{1,0:T(8,128)S(1)} all-gather(f32[24,512]{1,0:T(8,128)S(1)} %copy-done.1), channel_id=1, replica_groups=mesh['z'=16,'x'=4,'y'=4,'core'=2] {'z'}, dimensions={0}, use_global_device_ids=true | all-gather | bytes 835584 | tf_op jit(solution)/shard_map/all_gather | solution.py:166
  51.4 3.3 %scores.1 = (f32[384,768]{1,0:T(8,128)S(1)}, f32[32,8,128]{2,1,0:T(8,128)}) custom-call(f32[1]{0:T(128)} %bitcast.35.scale_ref, f32[384,512]{1,0:T(8,128)S(1)} %all_gather.3.row_ref, f32[768,512]{1,0:T(8,128)S(1)} %bitcast.37), custom_call_target="tpu_custom_call" | custom-call | tf_op jit(solution)/shard_map/scores/pallas_call | solution.py:170
  54.7 7.2 %all-to-all-start.1 = ((f32[32,8,128]{2,1,0:T(8,128)}), f32[32,8,128]{2,1,0:T(8,128)}, u32[]{:S(2)}, u32[]{:S(2)}) async-start(f32[32,8,128]{2,1,0:T(8,128)} %get-tuple-element.9), calls=%async_computation.1 | async-start | bytes 262144 | tf_op jit(solution)/shard_map/all_to_all | solution.py:186
  62.0 1.0 row_message.1
  63.1 5.0 %all-to-all-done.1.heard_col_in = f32[32,8,128]{2,1,0:T(8,128)} async-done(((f32[32,8,128]{2,1,0:T(8,128)}), f32[32,8,128]{2,1,0:T(8,128)}, u32[]{:S(2)}, u32[]{:S(2)}) %all-to-all-start.1) | async-done | bytes 131104 | tf_op jit(solution)/shard_map/all_to_all | solution.py:186
  68.0 6.8 %all-to-all-start.2 = ((f32[16,4,128]{2,1,0:T(4,128)}), f32[16,4,128]{2,1,0:T(4,128)}, u32[]{:S(2)}, u32[]{:S(2)}) async-start(f32[16,4,128]{2,1,0:T(4,128)} %row_message.1), calls=%async_computation.2 | async-start | bytes 65536 | tf_op jit(solution)/shard_map/all_to_all | solution.py:198
  74.9 12.6 %all-to-all-done.2.heard_row_in = f32[16,4,128]{2,1,0:T(4,128)} async-done(((f32[16,4,128]{2,1,0:T(4,128)}), f32[16,4,128]{2,1,0:T(4,128)}, u32[]{:S(2)}, u32[]{:S(2)}) %all-to-all-start.2) | async-done | bytes 32800 | tf_op jit(solution)/shard_map/all_to_all | solution.py:198
  87.5 3.9 %weights.1 = (f32[384,768]{1,0:T(8,128)}, f32[16,24,512]{2,1,0:T(8,128)}) custom-call(f32[1]{0:T(128)} %bitcast.36.scale_ref, f32[1]{0:T(128)} %bitcast.1.base_ref, f32[768,512]{1,0:T(8,128)S(1)} %bitcast.38, f32[384,768]{1,0:T(8,128)S(1)} %get-tuple-element.8.score_ref, f32[32,8,128]{2,1,0:T(8,128)} %all-to-all-done.1.heard_col_in, ...), custom_call_target="tpu_custom_call" | custom-call | tf_op jit(solution)/shard_map/weights/pallas_call | solution.py:201
  91.4 3.8 %all-to-all-start.3 = ((f32[16,24,512]{2,1,0:T(8,128)}), f32[16,24,512]{2,1,0:T(8,128)S(1)}, u32[]{:S(2)}, u32[]{:S(2)}) async-start(f32[16,24,512]{2,1,0:T(8,128)} %get-tuple-element.12), calls=%async_computation.3 | async-start | bytes 1572864 | tf_op jit(solution)/shard_map/all_to_all | solution.py:220
  96.0 1.9 %collective-permute-start = (f32[4,4,24,512]{3,2,1,0:T(8,128)S(1)}, f32[4,4,24,512]{3,2,1,0:T(8,128)}, u32[]{:S(2)}, u32[]{:S(2)}) collective-permute-start(f32[4,4,24,512]{3,2,1,0:T(8,128)S(1)} %bitcast.40), channel_id=1, source_target_pairs={{0,1},{1,0},{2,3},{3,2},{4,5},{5,4},{6,7},{7,6},{8,9},{9,8},{10,11... | collective-permute-start | bytes 2359304 | tf_op jit(solution)/shard_map/ppermute | solution.py:40
  98.9 1.5 %collective-permute-done = f32[4,4,24,512]{3,2,1,0:T(8,128)} collective-permute-done((f32[4,4,24,512]{3,2,1,0:T(8,128)S(1)}, f32[4,4,24,512]{3,2,1,0:T(8,128)}, u32[]{:S(2)}, u32[]{:S(2)}) %collective-permute-start) | collective-permute-done | bytes 786464 | tf_op jit(solution)/shard_map/ppermute | solution.py:40
  100.3 1.3 add.124
  101.7 2.2 %collective-permute-start.3 = (f32[4,24,512]{2,1,0:T(8,128)S(1)}, f32[4,24,512]{2,1,0:T(8,128)S(1)}, u32[]{:S(2)}, u32[]{:S(2)}) collective-permute-start(f32[4,24,512]{2,1,0:T(8,128)S(1)} %get-tuple-element.15), channel_id=1, source_target_pairs={{0,2},{2,4},{4,6},{6,0},{1,3},{3,5},{5,7},{7,1},{8,10},{10,12},{12... | collective-permute-start | bytes 589832 | tf_op jit(solution)/shard_map/ppermute | solution.py:40
  103.9 4.4 %collective-permute-start.2 = (f32[4,24,512]{2,1,0:T(8,128)S(1)}, f32[4,24,512]{2,1,0:T(8,128)S(1)}, u32[]{:S(2)}, u32[]{:S(2)}) collective-permute-start(f32[4,24,512]{2,1,0:T(8,128)S(1)} %get-tuple-element.16), channel_id=1, source_target_pairs={{0,4},{2,6},{4,0},{6,2},{1,5},{3,7},{5,1},{7,3},{8,12},{10,14},{12... | collective-permute-start | bytes 589832 | tf_op jit(solution)/shard_map/ppermute | solution.py:40
  108.4 3.0 %collective-permute-start.1 = (f32[4,24,512]{2,1,0:T(8,128)S(1)}, f32[4,24,512]{2,1,0:T(8,128)S(1)}, u32[]{:S(2)}, u32[]{:S(2)}) collective-permute-start(f32[4,24,512]{2,1,0:T(8,128)S(1)} %get-tuple-element.14), channel_id=1, source_target_pairs={{0,6},{2,0},{4,2},{6,4},{1,7},{3,1},{5,3},{7,5},{8,14},{10,8},{12,... | collective-permute-start | bytes 589832 | tf_op jit(solution)/shard_map/ppermute | solution.py:40
  111.4 4.5 %collective-permute-done.3 = f32[4,24,512]{2,1,0:T(8,128)S(1)} collective-permute-done((f32[4,24,512]{2,1,0:T(8,128)S(1)}, f32[4,24,512]{2,1,0:T(8,128)S(1)}, u32[]{:S(2)}, u32[]{:S(2)}) %collective-permute-start.3) | collective-permute-done | bytes 196640 | tf_op jit(solution)/shard_map/ppermute | solution.py:40
  115.9 2.5 %collective-permute-done.1 = f32[4,24,512]{2,1,0:T(8,128)S(1)} collective-permute-done((f32[4,24,512]{2,1,0:T(8,128)S(1)}, f32[4,24,512]{2,1,0:T(8,128)S(1)}, u32[]{:S(2)}, u32[]{:S(2)}) %collective-permute-start.1) | collective-permute-done | bytes 196640 | tf_op jit(solution)/shard_map/ppermute | solution.py:40
  118.5 4.1 %collective-permute-start.6 = (f32[24,512]{1,0:T(8,128)S(1)}, f32[24,512]{1,0:T(8,128)S(1)}, u32[]{:S(2)}, u32[]{:S(2)}) collective-permute-start(f32[24,512]{1,0:T(8,128)S(1)} %get-tuple-element.18), channel_id=1, source_target_pairs={{0,8},{8,16},{16,24},{24,0},{1,9},{9,17},{17,25},{25,1},{2,10},{10... | collective-permute-start | bytes 147464 | tf_op jit(solution)/shard_map/ppermute | solution.py:40
  122.6 2.8 %collective-permute-start.5 = (f32[24,512]{1,0:T(8,128)S(1)}, f32[24,512]{1,0:T(8,128)S(1)}, u32[]{:S(2)}, u32[]{:S(2)}) collective-permute-start(f32[24,512]{1,0:T(8,128)S(1)} %get-tuple-element.19), channel_id=1, source_target_pairs={{0,16},{8,24},{16,0},{24,8},{1,17},{9,25},{17,1},{25,9},{2,18},{10... | collective-permute-start | bytes 147464 | tf_op jit(solution)/shard_map/ppermute | solution.py:40
  125.4 2.5 %collective-permute-start.4 = (f32[24,512]{1,0:T(8,128)S(1)}, f32[24,512]{1,0:T(8,128)S(1)}, u32[]{:S(2)}, u32[]{:S(2)}) collective-permute-start(f32[24,512]{1,0:T(8,128)S(1)} %get-tuple-element.17), channel_id=1, source_target_pairs={{0,24},{8,0},{16,8},{24,16},{1,25},{9,1},{17,9},{25,17},{2,26},{10... | collective-permute-start | bytes 147464 | tf_op jit(solution)/shard_map/ppermute | solution.py:40
  127.9 2.6 %collective-permute-done.5 = f32[24,512]{1,0:T(8,128)S(1)} collective-permute-done((f32[24,512]{1,0:T(8,128)S(1)}, f32[24,512]{1,0:T(8,128)S(1)}, u32[]{:S(2)}, u32[]{:S(2)}) %collective-permute-start.5) | collective-permute-done | bytes 49184 | tf_op jit(solution)/shard_map/ppermute | solution.py:40
  130.6 2.1 %collective-permute-done.4 = f32[24,512]{1,0:T(8,128)S(1)} collective-permute-done((f32[24,512]{1,0:T(8,128)S(1)}, f32[24,512]{1,0:T(8,128)S(1)}, u32[]{:S(2)}, u32[]{:S(2)}) %collective-permute-start.4) | collective-permute-done | bytes 49184 | tf_op jit(solution)/shard_map/ppermute | solution.py:40
  (19 shorter events, 3.2 us)
Async XLA Ops:
  2.9 10.4 %copy-start.1 = (f32[24,512]{1,0:T(8,128)S(1)}, f32[24,512]{1,0:T(8,128)}, u32[]{:S(2)}) copy-start(f32[24,512]{1,0:T(8,128)} %param.4) | copy-start | bytes 147460
  2.9 48.5 %all-to-all-start = ((f32[32,24,512]{2,1,0:T(8,128)}), f32[32,24,512]{2,1,0:T(8,128)S(1)}, u32[]{:S(2)}, u32[]{:S(2)}) async-start(f32[32,24,512]{2,1,0:T(8,128)} %repeat.1), calls=%async_computation | async-start | bytes 3145728 | tf_op jit(solution)/shard_map/all_to_all | solution.py:36
  51.4 10.6 %copy-start.2 = (s32[24]{0:T(128)S(1)}, s32[24]{0:T(128)}, u32[]{:S(2)}) copy-start(s32[24]{0:T(128)} %param.7) | copy-start | bytes 292
  54.7 13.3 %all-to-all-start.1 = ((f32[32,8,128]{2,1,0:T(8,128)}), f32[32,8,128]{2,1,0:T(8,128)}, u32[]{:S(2)}, u32[]{:S(2)}) async-start(f32[32,8,128]{2,1,0:T(8,128)} %get-tuple-element.9), calls=%async_computation.1 | async-start | bytes 262144 | tf_op jit(solution)/shard_map/all_to_all | solution.py:186
  68.0 19.5 %all-to-all-start.2 = ((f32[16,4,128]{2,1,0:T(4,128)}), f32[16,4,128]{2,1,0:T(4,128)}, u32[]{:S(2)}, u32[]{:S(2)}) async-start(f32[16,4,128]{2,1,0:T(4,128)} %row_message.1), calls=%async_computation.2 | async-start | bytes 65536 | tf_op jit(solution)/shard_map/all_to_all | solution.py:198
  91.4 3.8 %copy-start = (f32[384,768]{1,0:T(8,128)S(1)}, f32[384,768]{1,0:T(8,128)}, u32[]{:S(2)}) copy-start(f32[384,768]{1,0:T(8,128)} %get-tuple-element.13) | copy-start | bytes 3538948
  91.4 41.9 %all-to-all-start.3 = ((f32[16,24,512]{2,1,0:T(8,128)}), f32[16,24,512]{2,1,0:T(8,128)S(1)}, u32[]{:S(2)}, u32[]{:S(2)}) async-start(f32[16,24,512]{2,1,0:T(8,128)} %get-tuple-element.12), calls=%async_computation.3 | async-start | bytes 1572864 | tf_op jit(solution)/shard_map/all_to_all | solution.py:220
  96.0 4.3 %collective-permute-start = (f32[4,4,24,512]{3,2,1,0:T(8,128)S(1)}, f32[4,4,24,512]{3,2,1,0:T(8,128)}, u32[]{:S(2)}, u32[]{:S(2)}) collective-permute-start(f32[4,4,24,512]{3,2,1,0:T(8,128)S(1)} %bitcast.40), channel_id=1, source_target_pairs={{0,1},{1,0},{2,3},{3,2},{4,5},{5,4},{6,7},{7,6},{8,9},{9,8},{10,11... | collective-permute-start | bytes 2359304 | tf_op jit(solution)/shard_map/ppermute | solution.py:40
  101.7 14.3 %collective-permute-start.3 = (f32[4,24,512]{2,1,0:T(8,128)S(1)}, f32[4,24,512]{2,1,0:T(8,128)S(1)}, u32[]{:S(2)}, u32[]{:S(2)}) collective-permute-start(f32[4,24,512]{2,1,0:T(8,128)S(1)} %get-tuple-element.15), channel_id=1, source_target_pairs={{0,2},{2,4},{4,6},{6,0},{1,3},{3,5},{5,7},{7,1},{8,10},{10,12},{12... | collective-permute-start | bytes 589832 | tf_op jit(solution)/shard_map/ppermute | solution.py:40
  103.9 12.0 %collective-permute-start.2 = (f32[4,24,512]{2,1,0:T(8,128)S(1)}, f32[4,24,512]{2,1,0:T(8,128)S(1)}, u32[]{:S(2)}, u32[]{:S(2)}) collective-permute-start(f32[4,24,512]{2,1,0:T(8,128)S(1)} %get-tuple-element.16), channel_id=1, source_target_pairs={{0,4},{2,6},{4,0},{6,2},{1,5},{3,7},{5,1},{7,3},{8,12},{10,14},{12... | collective-permute-start | bytes 589832 | tf_op jit(solution)/shard_map/ppermute | solution.py:40
  108.4 10.1 %collective-permute-start.1 = (f32[4,24,512]{2,1,0:T(8,128)S(1)}, f32[4,24,512]{2,1,0:T(8,128)S(1)}, u32[]{:S(2)}, u32[]{:S(2)}) collective-permute-start(f32[4,24,512]{2,1,0:T(8,128)S(1)} %get-tuple-element.14), channel_id=1, source_target_pairs={{0,6},{2,0},{4,2},{6,4},{1,7},{3,1},{5,3},{7,5},{8,14},{10,8},{12,... | collective-permute-start | bytes 589832 | tf_op jit(solution)/shard_map/ppermute | solution.py:40
  118.5 9.4 %collective-permute-start.6 = (f32[24,512]{1,0:T(8,128)S(1)}, f32[24,512]{1,0:T(8,128)S(1)}, u32[]{:S(2)}, u32[]{:S(2)}) collective-permute-start(f32[24,512]{1,0:T(8,128)S(1)} %get-tuple-element.18), channel_id=1, source_target_pairs={{0,8},{8,16},{16,24},{24,0},{1,9},{9,17},{17,25},{25,1},{2,10},{10... | collective-permute-start | bytes 147464 | tf_op jit(solution)/shard_map/ppermute | solution.py:40
  122.6 8.0 %collective-permute-start.5 = (f32[24,512]{1,0:T(8,128)S(1)}, f32[24,512]{1,0:T(8,128)S(1)}, u32[]{:S(2)}, u32[]{:S(2)}) collective-permute-start(f32[24,512]{1,0:T(8,128)S(1)} %get-tuple-element.19), channel_id=1, source_target_pairs={{0,16},{8,24},{16,0},{24,8},{1,17},{9,25},{17,1},{25,9},{2,18},{10... | collective-permute-start | bytes 147464 | tf_op jit(solution)/shard_map/ppermute | solution.py:40
  125.4 7.2 %collective-permute-start.4 = (f32[24,512]{1,0:T(8,128)S(1)}, f32[24,512]{1,0:T(8,128)S(1)}, u32[]{:S(2)}, u32[]{:S(2)}) collective-permute-start(f32[24,512]{1,0:T(8,128)S(1)} %get-tuple-element.17), channel_id=1, source_target_pairs={{0,24},{8,0},{16,8},{24,16},{1,25},{9,1},{17,9},{25,17},{2,26},{10... | collective-permute-start | bytes 147464 | tf_op jit(solution)/shard_map/ppermute | solution.py:40
